TPU v7x, 128 devices: a whole 4x4x4 slice. The times are simulated.
128 devices in a mesh: reg: 16 (over y_lo, x, core), ch: 8 (over z, y_hi).
Axes of the slice: x: 4, y: 4 (y_hi: 2, y_lo: 2; y = y_hi * 2 + y_lo), z: 4, core: 2. Of those that a mesh axis runs over, the one named last changes fastest.
Arguments:
- inner_state: float32 [2, 122880], P(None, 'reg'), may hold values from -6 to 6
- energy: float32 [122880], P('reg'), may hold values from -20 to 20
- blocks: float32 [1024, 512, 512], P(('reg', 'ch')), may hold values from -1.25 to 1.25
- pattern: int32 [1024, 2], P(('reg', 'ch')), may hold values from 0 to 239, as said below
- surface: float32 [416, 122880], P('ch', 'reg'), may hold values from -3 to 3
- channel_symmetry: int32 [416], P('ch'), may hold values from 0 to 59
- outer_state: float32 [2, 416, 8192], P(None, 'ch', 'reg'), may hold values from -6 to 6
- channel_energy: float32 [416], P('ch'), may hold values from -10 to 10
- couple_source: int32 [416, 4], replicated, may hold values from 0 to 415
- couple_order: int32 [416, 4], replicated, may hold values from 0 to 2
- couple_weight: float32 [416, 4], replicated, may hold values from -24 to 24
Outputs:
- new_inner: float32 [2, 122880], P(None, 'reg')
- new_outer: float32 [2, 416, 8192], P(None, 'ch', 'reg')
Inputs may be any that keep to these rules, and one draw needn't show every extreme that they name: `pattern`: column 0 is a block row within the tile of the reg index that holds the row, below 15; column 1 is a global block column whose symmetry (block // 4) is one above or one below that of the block row.
All inputs are finite; a program needn't handle non-finite values.
Results may differ from a plain program's by a relative error of at most 0.0012.
Values may be sent and summed in bfloat16 or wider, within the bound.
No kernel may reach another device: no remote copies, remote signals or barrier semaphores. Data moves between devices by JAX's collectives and lax.ppermute only.
A program may use at most 64 MiB of HBM per device.

v0:
```python
import jax
import jax.numpy as jnp
from jax import lax
from jax.sharding import PartitionSpec as P

BLOCKS_PER_SYMM = 4
NLAM = 3


PRECISE = lax.Precision.HIGHEST
TIME_STEP = 0.05
GRID_STEP = 0.5
BOUNDARY_RADIUS = 20.0


def with_halo(cells, sides, width):
    for axis, dim in sides:
        count = lax.axis_size(axis)
        ends = count - 1
        head = lax.slice_in_dim(cells, 0, width, axis=dim)
        tail = lax.slice_in_dim(cells, cells.shape[dim] - width, cells.shape[dim], axis=dim)
        cells = jnp.concatenate(
            [
                lax.ppermute(tail, axis, [(i, (i + 1) % count) for i in range(ends)]),
                cells,
                lax.ppermute(head, axis, [((i + 1) % count, i) for i in range(ends)]),
            ],
            axis=dim,
        )
    return cells


def spread(value, axis, source):
    kept = jnp.where(lax.axis_index(axis) == source, value, 0).astype(value.dtype)
    return lax.psum(kept, axis)


def radial_grid(first, count):
    return (
        BOUNDARY_RADIUS
        + (first + jnp.arange(count, dtype=jnp.int32) + 1).astype(jnp.float32) * GRID_STEP
    )


def build_mats(source, order_list, weight, chan_total):
    onehot = source[:, :, None] == jnp.arange(chan_total, dtype=jnp.int32)[None, None, :]
    matrices = []
    for order in range(NLAM):
        picked = jnp.where(order_list == order, weight, jnp.float32(0.0))
        matrices.append(
            jnp.sum(jnp.where(onehot, picked[:, :, None], jnp.float32(0.0)), axis=1).astype(
                jnp.bfloat16
            )
        )
    return jnp.stack(matrices)


def radial_sum(totals, radius):
    combined = jnp.zeros(totals.shape[1:], jnp.float32)
    for order in range(totals.shape[0]):
        combined = combined + (BOUNDARY_RADIUS / radius) ** order * totals[order]
    return combined


def local(
    inner_state,
    energy,
    blocks,
    pattern,
    surface,
    channel_symmetry,
    outer_state,
    channel_energy,
    couple_source,
    couple_order,
    couple_weight,
):
    reg_index = lax.axis_index("reg")
    ch_index = lax.axis_index("ch")
    tile_len = inner_state.shape[1]
    block_len = blocks.shape[1]
    chan_local = outer_state.shape[1]
    rad_local = outer_state.shape[2]
    chan_total = couple_source.shape[0]
    sym_rows = BLOCKS_PER_SYMM * block_len
    rows = reg_index * tile_len + jnp.arange(tile_len, dtype=jnp.int32)
    masked = jnp.where(
        channel_symmetry[:, None] == (rows // sym_rows)[None, :], surface, jnp.float32(0.0)
    )
    radius = radial_grid(reg_index * rad_local, rad_local)
    angular = channel_symmetry.astype(jnp.float32)
    potential = (
        angular[:, None] * (angular[:, None] + 1.0) / (2.0 * radius[None, :] ** 2)
        + channel_energy[:, None]
    )
    row_select = (
        pattern[:, 0][:, None] == jnp.arange(tile_len // block_len, dtype=jnp.int32)[None, :]
    ).astype(jnp.float32)
    first_target = ch_index * chan_local
    coupling_mats = build_mats(
        lax.dynamic_slice_in_dim(couple_source, first_target, chan_local, 0),
        lax.dynamic_slice_in_dim(couple_order, first_target, chan_local, 0),
        lax.dynamic_slice_in_dim(couple_weight, first_target, chan_local, 0),
        chan_total,
    )
    inner_vec, outer_vec = (inner_state, outer_state)
    total_inner, total_outer = (inner_state, outer_state)
    for term in (1, 2):
        whole = with_halo(inner_vec, (("reg", 1),), 2 * sym_rows)
        offset = reg_index * tile_len - 2 * sym_rows
        starts = pattern[:, 1] * block_len - offset
        pieces = jax.vmap(lambda begin: lax.dynamic_slice_in_dim(whole, begin, block_len, 1))(
            starts
        )
        products = jnp.einsum("sij,spj->spi", blocks, pieces, precision=PRECISE)
        dipole = jnp.einsum("sb,spi->pbi", row_select, products, precision=PRECISE).reshape(
            2, tile_len
        )
        partial_value = jnp.dot(inner_vec, masked.T, precision=PRECISE)
        first_value = outer_vec[:, :, 0]
        boundary = lax.psum(partial_value, "reg")
        first_cell = spread(first_value, "reg", 0)
        slope = (first_cell - boundary) / GRID_STEP
        inner_part = dipole + 0.5 * jnp.dot(slope, masked, precision=PRECISE)
        inner_out = energy * inner_vec + lax.psum(inner_part, "ch")
        padded = with_halo(outer_vec, (("reg", 2),), 1)
        lower = jnp.where(reg_index == 0, boundary[:, :, None], padded[:, :, :1])
        left = jnp.concatenate([lower, padded[:, :, 1:rad_local]], axis=2)
        kinetic = -0.5 * (padded[:, :, 2:] - 2.0 * outer_vec + left) / (GRID_STEP * GRID_STEP)
        halves = outer_vec.astype(jnp.bfloat16)
        totals = jnp.einsum(
            "lts,psr->lptr",
            coupling_mats,
            lax.all_gather(halves, "ch", axis=1, tiled=True),
            preferred_element_type=jnp.float32,
        )
        rounded = radial_sum(totals, radius).astype(jnp.bfloat16)
        mixed = lax.optimization_barrier(rounded).astype(jnp.float32)
        outer_out = kinetic + potential * outer_vec + mixed
        factor = TIME_STEP / term
        inner_vec = factor * jnp.stack([inner_out[1], -inner_out[0]])
        outer_vec = factor * jnp.stack([outer_out[1], -outer_out[0]])
        total_inner = total_inner + inner_vec
        total_outer = total_outer + outer_vec
    return (total_inner, total_outer)


def solution(mesh):
    return jax.shard_map(
        local,
        mesh=mesh,
        in_specs=(
            P(None, "reg"),
            P("reg"),
            P(("reg", "ch"), None, None),
            P(("reg", "ch"), None),
            P("ch", "reg"),
            P("ch"),
            P(None, "ch", "reg"),
            P("ch"),
            P(),
            P(),
            P(),
        ),
        out_specs=(P(None, "reg"), P(None, "ch", "reg")),
        check_vma=False,
    )
```

profile of v0, /device:TPU:6, one launch (start us, length us, event | category | flops | bytes accessed | tf_op | source)
XLA Modules:
  0.0 296.8 jit_solution(8046791651399769452)
XLA Ops:
  0.7 1.1 copy.66
  1.9 1.9 collective-permute-start.5
  3.9 3.6 %collective-permute-start.4 = (f32[2,52,1]{2,1,0:T(8,128)S(1)}, f32[2,52,1]{2,1,0:T(8,128)}, u32[]{:S(2)}, u32[]{:S(2)}) collective-permute-start(f32[2,52,1]{2,1,0:T(8,128)S(1)} %get-tuple-element.60), channel_id=1, source_target_pairs={{8,0},{16,8},{24,16},{32,24},{40,32},{48,40},{56,48},{64,56},{72,6... | collective-permute-start | bytes 1256 | tf_op jit(solution)/shard_map/ppermute | solution.py:26
  7.5 1.5 fusion.78
  9.0 1.9 collective-permute-start
  10.9 3.6 %collective-permute-start.1 = (f32[2,4096]{1,0:T(2,128)}, f32[2,4096]{1,0:T(2,128)}, u32[]{:S(2)}, u32[]{:S(2)}) collective-permute-start(f32[2,4096]{1,0:T(2,128)} %get-tuple-element.68), channel_id=1, source_target_pairs={{8,0},{16,8},{24,16},{32,24},{40,32},{48,40},{56,48},{64,56},{72,6... | collective-permute-start | bytes 98312 | tf_op jit(solution)/shard_map/ppermute | solution.py:26
  14.5 1.0 convert_element_type.86
  15.6 0.8 compare_select_fusion.9
  16.9 38.9 %all_gather.6 = bf16[2,416,512]{2,0,1:T(2,128)(2,1)S(1)} all-gather(bf16[2,52,512]{2,0,1:T(2,128)(2,1)S(1)} %convert_element_type.86), channel_id=1, replica_groups=mesh['reg'=16,'ch'=8] {'ch'}, dimensions={1}, use_global_device_ids=true | all-gather | bytes 958464 | tf_op jit(solution)/shard_map/all_gather | solution.py:134
  55.9 1.5 fusion.4
  57.4 28.1 %all-reduce.2 = (f32[2,52]{1,0:T(2,128)S(1)}, f32[2,52]{1,0:T(2,128)S(1)}) all-reduce(f32[2,52]{1,0:T(2,128)S(1)} %get-tuple-element.59, f32[2,52]{1,0:T(2,128)S(1)} %fusion.4), channel_id=1, replica_groups=mesh['reg'=16,'ch'=8] {'reg'}, use_global_device_ids=true, to_apply=%region_0.1 | all-reduce | flops 208 | bytes 1664 | tf_op jit(solution)/shard_map/psum | solution.py:35
  85.5 0.9 select_reduce_fusion.2
  87.4 0.9 broadcast_select_fusion.1
  88.3 1.0 fusion.40
  89.5 37.3 %all_gather.7 = bf16[2,416,512]{2,0,1:T(2,128)(2,1)S(1)} all-gather(bf16[2,52,512]{2,0,1:T(2,128)(2,1)S(1)} %copy.81), channel_id=1, replica_groups=mesh['reg'=16,'ch'=8] {'ch'}, dimensions={1}, use_global_device_ids=true | all-gather | bytes 958464 | tf_op jit(solution)/shard_map/all_gather | solution.py:134
  127.3 1.9 collective-permute-start.7
  129.3 3.6 %collective-permute-start.6 = (f32[2,52,1]{2,1,0:T(8,128)S(1)}, f32[2,52,1]{2,1,0:T(8,128)S(1)}, u32[]{:S(2)}, u32[]{:S(2)}) collective-permute-start(f32[2,52,1]{2,1,0:T(8,128)S(1)} %get-tuple-element.55), channel_id=1, source_target_pairs={{8,0},{16,8},{24,16},{32,24},{40,32},{48,40},{56,48},{64,56},{72,6... | collective-permute-start | bytes 1256 | tf_op jit(solution)/shard_map/ppermute | solution.py:26
  132.9 0.8 pad_maximum_fusion.3
  133.8 10.6 %while.2 = (s32[]{:T(128)}, f32[2,15872]{1,0:T(2,128)S(1)}, s32[8,2]{0,1:T(2,128)S(1)}, f32[8,2,512]{2,1,0:T(2,128)S(1)}, s32[]{:T(128)}) while((s32[]{:T(128)}, f32[2,15872]{1,0:T(2,128)S(1)}, s32[8,2]{0,1:T(2,128)S(1)}, f32[8,2,512]{2,1,0:T(2,128)S(1)}, s32[]{:T(128)}) %tuple.53), condition=%wide.while_cond, body=%wide.while_body.sunk | while | flops 2 | bytes 8289 | solution.py:112
  134.4 0.7 bitcast_dynamic-update-slice_fusion.4
  135.7 0.7 bitcast_dynamic-update-slice_fusion.4
  137.0 0.7 bitcast_dynamic-update-slice_fusion.4
  138.4 0.7 bitcast_dynamic-update-slice_fusion.4
  139.7 0.7 bitcast_dynamic-update-slice_fusion.4
  141.0 0.7 bitcast_dynamic-update-slice_fusion.4
  142.3 0.7 bitcast_dynamic-update-slice_fusion.4
  143.6 0.7 bitcast_dynamic-update-slice_fusion.4
  144.4 9.2 %fusion.79 = f32[8,2,512]{2,1,0:T(2,128)S(1)} fusion(f32[8,2,512]{2,1,0:T(2,128)S(1)} %get-tuple-element.9, f32[8,512,512]{2,1,0:T(8,128)} %param.13), kind=kOutput, calls=%fused_computation.140 | convolution fusion | flops 50331648 | bytes 8454144 | tf_op jit(solution)/shard_map/sij,spj->spi/dot_general | solution.py:115
  153.9 1.1 fusion.1
  155.0 42.0 %psum.44 = f32[2,7680]{1,0:T(2,128)S(1)} all-reduce(f32[2,7680]{1,0:T(2,128)S(1)} %fusion.1), channel_id=1, replica_groups=mesh['reg'=16,'ch'=8] {'ch'}, use_global_device_ids=true, to_apply=%region_2.3 | all-reduce | flops 15360 | bytes 122880 | tf_op jit(solution)/shard_map/psum | solution.py:125
  197.1 1.5 fusion.2
  198.7 28.1 %all-reduce.1 = (f32[2,52]{1,0:T(2,128)S(1)}, f32[2,52]{1,0:T(2,128)S(1)}) all-reduce(f32[2,52]{1,0:T(2,128)S(1)} %get-tuple-element.54, f32[2,52]{1,0:T(2,128)S(1)} %fusion.2), channel_id=1, replica_groups=mesh['reg'=16,'ch'=8] {'reg'}, use_global_device_ids=true, to_apply=%region_6.7 | all-reduce | flops 208 | bytes 1664 | tf_op jit(solution)/shard_map/psum | solution.py:35
  227.3 2.5 collective-permute-start.2
  229.8 3.3 %collective-permute-start.3 = (f32[2,4096]{1,0:T(2,128)S(1)}, f32[2,4096]{1,0:T(2,128)S(1)}, u32[]{:S(2)}, u32[]{:S(2)}) collective-permute-start(f32[2,4096]{1,0:T(2,128)S(1)} %get-tuple-element.64), channel_id=1, source_target_pairs={{8,0},{16,8},{24,16},{32,24},{40,32},{48,40},{56,48},{64,56},{72,6... | collective-permute-start | bytes 98312 | tf_op jit(solution)/shard_map/ppermute | solution.py:26
  233.1 0.8 copy.84
  234.0 2.8 collective-permute-done.3
  236.8 10.6 %while.3 = (s32[]{:T(128)}, f32[2,15872]{1,0:T(2,128)S(1)}, s32[8,2]{0,1:T(2,128)S(1)}, f32[8,2,512]{2,1,0:T(2,128)S(1)}, s32[]{:T(128)}) while((s32[]{:T(128)}, f32[2,15872]{1,0:T(2,128)S(1)}, s32[8,2]{0,1:T(2,128)S(1)}, f32[8,2,512]{2,1,0:T(2,128)S(1)}, s32[]{:T(128)}) %tuple.59), condition=%wide.while_cond.1, body=%wide.while_body.1.sunk | while | flops 2 | bytes 8289 | solution.py:112
  237.4 0.7 bitcast_dynamic-update-slice_fusion.5
  238.7 0.7 bitcast_dynamic-update-slice_fusion.5
  240.1 0.7 bitcast_dynamic-update-slice_fusion.5
  241.4 0.7 bitcast_dynamic-update-slice_fusion.5
  242.7 0.7 bitcast_dynamic-update-slice_fusion.5
  244.0 0.7 bitcast_dynamic-update-slice_fusion.5
  245.3 0.7 bitcast_dynamic-update-slice_fusion.5
  247.4 9.2 %fusion.80 = f32[8,2,512]{2,1,0:T(2,128)S(1)} fusion(f32[8,2,512]{2,1,0:T(2,128)S(1)} %get-tuple-element.17, f32[8,512,512]{2,1,0:T(8,128)} %param.13), kind=kOutput, calls=%fused_computation.141 | convolution fusion | flops 50331648 | bytes 8454144 | tf_op jit(solution)/shard_map/sij,spj->spi/dot_general | solution.py:115
  256.9 1.1 fusion
  258.0 37.8 %psum.47 = f32[2,7680]{1,0:T(2,128)S(1)} all-reduce(f32[2,7680]{1,0:T(2,128)S(1)} %fusion), channel_id=1, replica_groups=mesh['reg'=16,'ch'=8] {'ch'}, use_global_device_ids=true, to_apply=%region_8.9 | all-reduce | flops 15360 | bytes 122880 | tf_op jit(solution)/shard_map/psum | solution.py:125
  296.0 0.8 fusion.43
  (109 shorter events, 14.0 us)
Async XLA Ops:
  0.6 16.1 %copy-start = (s32[416,4]{0,1:T(4,128)S(1)}, s32[416,4]{0,1:T(4,128)}, u32[]{:S(2)}) copy-start(s32[416,4]{0,1:T(4,128)} %param.19) | copy-start | bytes 19972
  0.6 55.2 %copy-start.3 = (f32[2,7680]{1,0:T(2,128)S(1)}, f32[2,7680]{1,0:T(2,128)}, u32[]{:S(2)}) copy-start(f32[2,7680]{1,0:T(2,128)} %param.11) | copy-start | bytes 184324
  0.7 55.2 %copy-start.11 = (s32[52]{0:T(128)S(1)}, s32[52]{0:T(128)}, u32[]{:S(2)}) copy-start(s32[52]{0:T(128)} %param.16) | copy-start | bytes 628
  0.7 55.2 %copy-start.4 = (f32[7680]{0:T(1024)S(1)}, f32[7680]{0:T(1024)}, u32[]{:S(2)}) copy-start(f32[7680]{0:T(1024)} %param.12) | copy-start | bytes 92164
  0.7 55.2 %copy-start.1 = (f32[52,7680]{1,0:T(8,128)S(1)}, f32[52,7680]{1,0:T(8,128)}, u32[]{:S(2)}) copy-start(f32[52,7680]{1,0:T(8,128)} %param.15) | copy-start | bytes 4792324
  1.9 85.5 %collective-permute-start.5 = (f32[2,52,1]{2,1,0:T(8,128)S(1)}, f32[2,52,1]{2,1,0:T(8,128)}, u32[]{:S(2)}, u32[]{:S(2)}) collective-permute-start(f32[2,52,1]{2,1,0:T(8,128)S(1)} %get-tuple-element.58), channel_id=1, source_target_pairs={{0,8},{8,16},{16,24},{24,32},{32,40},{40,48},{48,56},{56,64},{64,7... | collective-permute-start | bytes 1256 | tf_op jit(solution)/shard_map/ppermute | solution.py:24
  3.8 81.7 %copy-start.12 = (s32[8,2]{0,1:T(2,128)S(1)}, s32[8,2]{0,1:T(2,128)}, u32[]{:S(2)}) copy-start(s32[8,2]{0,1:T(2,128)} %param.14) | copy-start | bytes 196
  3.9 84.4 %collective-permute-start.4 = (f32[2,52,1]{2,1,0:T(8,128)S(1)}, f32[2,52,1]{2,1,0:T(8,128)}, u32[]{:S(2)}, u32[]{:S(2)}) collective-permute-start(f32[2,52,1]{2,1,0:T(8,128)S(1)} %get-tuple-element.60), channel_id=1, source_target_pairs={{8,0},{16,8},{24,16},{32,24},{40,32},{48,40},{56,48},{64,56},{72,6... | collective-permute-start | bytes 1256 | tf_op jit(solution)/shard_map/ppermute | solution.py:26
  9.0 124.0 %collective-permute-start = (f32[2,4096]{1,0:T(2,128)}, f32[2,4096]{1,0:T(2,128)}, u32[]{:S(2)}, u32[]{:S(2)}) collective-permute-start(f32[2,4096]{1,0:T(2,128)} %get-tuple-element.67), channel_id=1, source_target_pairs={{0,8},{8,16},{16,24},{24,32},{32,40},{40,48},{48,56},{56,64},{64,7... | collective-permute-start | bytes 98312 | tf_op jit(solution)/shard_map/ppermute | solution.py:24
  10.9 122.1 %collective-permute-start.1 = (f32[2,4096]{1,0:T(2,128)}, f32[2,4096]{1,0:T(2,128)}, u32[]{:S(2)}, u32[]{:S(2)}) collective-permute-start(f32[2,4096]{1,0:T(2,128)} %get-tuple-element.68), channel_id=1, source_target_pairs={{8,0},{16,8},{24,16},{32,24},{40,32},{48,40},{56,48},{64,56},{72,6... | collective-permute-start | bytes 98312 | tf_op jit(solution)/shard_map/ppermute | solution.py:26
  57.4 29.7 %copy-start.13 = (f32[52]{0:T(128)S(1)}, f32[52]{0:T(128)}, u32[]{:S(2)}) copy-start(f32[52]{0:T(128)} %param.18) | copy-start | bytes 628
  86.4 0.6 copy-start.5
  86.4 0.6 copy-start.7
  86.4 0.6 copy-start.9
  87.4 39.4 %copy-start.6 = (bf16[52,416]{1,0:T(8,128)(2,1)S(1)}, bf16[52,416]{1,0:T(8,128)(2,1)}, u32[]{:S(2)}) copy-start(bf16[52,416]{1,0:T(8,128)(2,1)} %copy-done.5) | copy-start | bytes 129796
  87.4 39.4 %copy-start.8 = (bf16[52,416]{1,0:T(8,128)(2,1)S(1)}, bf16[52,416]{1,0:T(8,128)(2,1)}, u32[]{:S(2)}) copy-start(bf16[52,416]{1,0:T(8,128)(2,1)} %copy-done.7) | copy-start | bytes 129796
  87.4 39.4 %copy-start.10 = (bf16[52,416]{1,0:T(8,128)(2,1)S(1)}, bf16[52,416]{1,0:T(8,128)(2,1)}, u32[]{:S(2)}) copy-start(bf16[52,416]{1,0:T(8,128)(2,1)} %copy-done.9) | copy-start | bytes 129796
  127.3 99.6 %collective-permute-start.7 = (f32[2,52,1]{2,1,0:T(8,128)S(1)}, f32[2,52,1]{2,1,0:T(8,128)S(1)}, u32[]{:S(2)}, u32[]{:S(2)}) collective-permute-start(f32[2,52,1]{2,1,0:T(8,128)S(1)} %get-tuple-element.53), channel_id=1, source_target_pairs={{0,8},{8,16},{16,24},{24,32},{32,40},{40,48},{48,56},{56,64},{64,7... | collective-permute-start | bytes 1256 | tf_op jit(solution)/shard_map/ppermute | solution.py:24
  129.3 97.7 %collective-permute-start.6 = (f32[2,52,1]{2,1,0:T(8,128)S(1)}, f32[2,52,1]{2,1,0:T(8,128)S(1)}, u32[]{:S(2)}, u32[]{:S(2)}) collective-permute-start(f32[2,52,1]{2,1,0:T(8,128)S(1)} %get-tuple-element.55), channel_id=1, source_target_pairs={{8,0},{16,8},{24,16},{32,24},{40,32},{48,40},{56,48},{64,56},{72,6... | collective-permute-start | bytes 1256 | tf_op jit(solution)/shard_map/ppermute | solution.py:26
  197.1 35.9 %copy-start.2 = (f32[2,52,512]{2,0,1:T(2,128)S(1)}, f32[2,52,512]{2,0,1:T(2,128)}, u32[]{:S(2)}) copy-start(f32[2,52,512]{2,0,1:T(2,128)} %param.17) | copy-start | bytes 638980
  227.3 6.7 %collective-permute-start.2 = (f32[2,4096]{1,0:T(2,128)S(1)}, f32[2,4096]{1,0:T(2,128)S(1)}, u32[]{:S(2)}, u32[]{:S(2)}) collective-permute-start(f32[2,4096]{1,0:T(2,128)S(1)} %get-tuple-element.63), channel_id=1, source_target_pairs={{0,8},{8,16},{16,24},{24,32},{32,40},{40,48},{48,56},{56,64},{64,7... | collective-permute-start | bytes 98312 | tf_op jit(solution)/shard_map/ppermute | solution.py:24
  229.8 7.0 %collective-permute-start.3 = (f32[2,4096]{1,0:T(2,128)S(1)}, f32[2,4096]{1,0:T(2,128)S(1)}, u32[]{:S(2)}, u32[]{:S(2)}) collective-permute-start(f32[2,4096]{1,0:T(2,128)S(1)} %get-tuple-element.64), channel_id=1, source_target_pairs={{8,0},{16,8},{24,16},{32,24},{40,32},{48,40},{56,48},{64,56},{72,6... | collective-permute-start | bytes 98312 | tf_op jit(solution)/shard_map/ppermute | solution.py:26
where the time goes:
time: 300 us; the launch traced here: 297 us
  blocking collectives  212 us (71%)
  local copies, waits for them, and re-layouts  25.8 us (9%)
  matrix products  24.9 us (8%)
  starting transfers between devices  22.4 us (7%)
  other arithmetic  7.38 us (2%)
    psum x2, blocking collectives, local(): inner_out = energy * inner_vec + lax.psum(inner_part, 'ch')  79.9 us
    all_gather x2, blocking collectives, local(): lax.all_gather(halves, 'ch', axis=1, tiled=True)  76.3 us
    psum x2, blocking collectives, spread(): return lax.psum(kept, axis)  56.2 us
    gather x48, local copies, waits for them, and re-layouts  21.1 us
    dot_general x2, matrix products, local(): products = jnp.einsum('sij,spj->spi', blocks, pieces, precision=PRECISE)  18.4 us
    ppermute x4, starting transfers between devices, with_halo(): lax.ppermute(head, axis, [((i + 1) % count, i) for i in range(ends)])  14.2 us
    ppermute x4, starting transfers between devices, with_halo(): lax.ppermute(tail, axis, [(i, (i + 1) % count) for i in range(ends)])  8.24 us
  transfers between devices with their start and end apart: 8, of which 1 were waited for; matrix products, arithmetic and copies ran while one was open for 12% of the time, Pallas kernels for 0%

commit v1 on v0

v1 whole, which is shorter than its diff:
```python
import functools

import jax
import jax.numpy as jnp
from jax import lax
from jax.experimental import pallas as pl
from jax.experimental.pallas import tpu as pltpu
from jax.sharding import PartitionSpec as P

BLOCKS_PER_SYMM = 4
NLAM = 3
TIME_STEP = 0.05
GRID_STEP = 0.5
BOUNDARY_RADIUS = 20.0
FIRST = TIME_STEP
SECOND = TIME_STEP / 2
LANES = 128
HALO_BLOCKS = 7
HALO_ROWS = 8 * HALO_BLOCKS
WINDOW = 64
F32 = jnp.float32
NT = (((1,), (1,)), ((), ()))


def params(megabytes):
    return pltpu.CompilerParams(vmem_limit_bytes=megabytes * 2**20)


def lane_index(shape):
    return lax.broadcasted_iota(jnp.int32, shape, len(shape) - 1)


def row_index(shape):
    return lax.broadcasted_iota(jnp.int32, shape, len(shape) - 2)


def square(rows):
    count = rows.shape[0]
    if count < LANES:
        rows = jnp.concatenate([rows, jnp.zeros((LANES - count, LANES), F32)], axis=0)
    return rows.T


def wide(column):
    return jnp.broadcast_to(column, (column.shape[0], LANES))


def boundary_sum(vec_rows, surf_ref, sym, first_tile, tiles):
    chan = surf_ref.shape[0]
    sums = [jnp.zeros((chan, LANES), F32) for _ in range(2)]
    for tile in range(tiles):
        here = ((first_tile + tile) // 16).astype(F32)
        values = jnp.where(sym == here, surf_ref[:, LANES * tile : LANES * (tile + 1)], 0.0)
        for part in range(2):
            sums[part] = sums[part] + values * vec_rows(tile, part)
    return [jnp.sum(total, axis=1, keepdims=True) for total in sums]


def surface_rows(slope, surf_ref, sym, first_tile, tiles, out_ref):
    columns = [wide(column) for column in slope]
    for tile in range(tiles):
        here = ((first_tile + tile) // 16).astype(F32)
        values = jnp.where(sym == here, surf_ref[:, LANES * tile : LANES * (tile + 1)], 0.0)
        rows = [jnp.sum(values * columns[part], axis=0, keepdims=True) for part in range(2)]
        at = slice(2 * tile, 2 * tile + 2)
        out_ref[at, :] = out_ref[at, :] + jnp.concatenate(rows, axis=0)


def turn_rows(rows):
    count = rows.shape[0]
    even = row_index(rows.shape) % 2 == 0
    return jnp.where(even, pltpu.roll(rows, count - 1, 0), -pltpu.roll(rows, 1, 0))


def turn_lanes(cells):
    other = pltpu.roll(cells, WINDOW, 1)
    return jnp.where(lane_index(cells.shape) < WINDOW, other, -other)


def start_kernel(idx_ref, u_ref, surf_ref, sym_ref, energy_ref, w_ref, first_ref, left_ref, right_ref, rows_ref, cols_ref, edge_ref, wt_ref):
    reg = idx_ref[0]
    tiles = u_ref.shape[1] // LANES
    chan = surf_ref.shape[0]
    head = jnp.zeros((1, LANES - chan), F32)
    sym_row = jnp.concatenate([sym_ref[...].astype(F32), head], axis=1)
    energy_row = jnp.concatenate([energy_ref[...], head], axis=1)
    base = square(jnp.concatenate([sym_row, energy_row], axis=0))
    sym = wide(base[:chan, 0:1])
    for tile in range(tiles):
        rows_ref[2 * tile : 2 * tile + 2, :] = u_ref[:, LANES * tile : LANES * (tile + 1)]
    partial = boundary_sum(
        lambda tile, part: u_ref[part : part + 1, LANES * tile : LANES * (tile + 1)],
        surf_ref, sym, reg * tiles, tiles,
    )
    for part in range(2):
        for piece in range(w_ref.shape[2] // LANES):
            cells = w_ref[part, :, LANES * piece : LANES * (piece + 1)]
            cells = jnp.concatenate([cells, jnp.zeros((LANES - chan, LANES), F32)], axis=0)
            wt_ref[part, LANES * piece : LANES * (piece + 1), :] = cells.T
    lane = lane_index((chan, LANES))
    cols = jnp.where(lane == 0, sym, 0.0)
    cols = jnp.where(lane == 1, wide(base[:chan, 1:2]), cols)
    for part in range(2):
        cols = jnp.where(lane == 2 + part, wide(partial[part]), cols)
    cols = jnp.concatenate([cols, jnp.zeros((cols_ref.shape[0] - chan, LANES), F32)], axis=0)
    cols_ref[...] = cols
    back = jnp.concatenate([cols, jnp.zeros((LANES - cols.shape[0], LANES), F32)], axis=0).T
    partial_rows = back[2:4, :]
    count = w_ref.shape[2]
    spot = lambda part, point: wt_ref[part, point : point + 1, :]
    zeros = jnp.zeros((2, LANES), F32)
    left_ref[:HALO_ROWS, :] = rows_ref[:HALO_ROWS, :]
    left_ref[HALO_ROWS:, :] = jnp.concatenate([partial_rows, spot(0, 0), spot(0, 1), spot(1, 0), spot(1, 1), zeros], axis=0)
    right_ref[:HALO_ROWS, :] = rows_ref[2 * tiles - HALO_ROWS :, :]
    right_ref[HALO_ROWS:, :] = jnp.concatenate(
        [partial_rows, spot(0, count - 2), spot(0, count - 1), spot(1, count - 2), spot(1, count - 1), zeros], axis=0
    )
    cell0 = jnp.concatenate([spot(0, 0), spot(1, 0)], axis=0)
    cell1 = jnp.concatenate([spot(0, 1), spot(1, 1)], axis=0)
    shifted = pltpu.roll(jnp.concatenate([cell0] * 4, axis=0), WINDOW, 1)[0:2]
    group = 8
    first_ref[0:group] = jnp.broadcast_to((partial_rows + shifted)[None], (group, 2, LANES))
    others = first_ref.shape[0] - group
    first_ref[group:] = jnp.broadcast_to((cell1 + shifted)[None], (others, 2, LANES))
    windows = count // WINDOW
    zero = jnp.zeros((1, LANES), F32)
    for window in range(windows):
        low, high = WINDOW * window - 1, WINDOW * (window + 1)
        edge_ref[4 * window : 4 * window + 4, :] = jnp.concatenate(
            [
                spot(0, low) if window else zero,
                spot(1, low) if window else zero,
                spot(0, high) if window < windows - 1 else zero,
                spot(1, high) if window < windows - 1 else zero,
            ],
            axis=0,
        )
    edge_ref[4 * windows : 4 * windows + 8, :] = jnp.concatenate([cell1, cell0, sym_row, energy_row, zeros], axis=0)


def expand_states(left_ref, mine_ref, right_ref, states_ref):
    shape = (8, 4 * LANES)
    keep = row_index(shape) // 2 == lane_index(shape) // LANES
    blocks = mine_ref.shape[0] // 8
    for column in range(2 * HALO_BLOCKS + blocks):
        if column < HALO_BLOCKS:
            rows = left_ref[8 * column : 8 * column + 8, :]
        elif column < HALO_BLOCKS + blocks:
            at = 8 * (column - HALO_BLOCKS)
            rows = mine_ref[at : at + 8, :]
        else:
            at = 8 * (column - HALO_BLOCKS - blocks)
            rows = right_ref[at : at + 8, :]
        whole = jnp.where(keep, jnp.concatenate([rows] * 4, axis=1), 0.0)
        lead = whole.astype(jnp.bfloat16).astype(F32)
        states_ref[column] = jnp.concatenate([lead, whole - lead], axis=0).astype(jnp.bfloat16)


def add_block(pattern_ref, idx_ref, block_ref, states_ref, sums_ref):
    step = pl.program_id(0)
    rows = sums_ref.shape[0]
    column = jnp.clip(pattern_ref[step, 1] - idx_ref[0] * rows + HALO_BLOCKS, 0, states_ref.shape[0] - 1)
    row = jnp.clip(pattern_ref[step, 0], 0, rows - 1)
    state = states_ref[column]
    block = block_ref[0]
    lead = block.astype(jnp.bfloat16)
    rest = (block - lead.astype(F32)).astype(jnp.bfloat16)
    product = lax.dot_general(state, lead, NT, preferred_element_type=F32)
    product = product + lax.dot_general(state, rest, NT, preferred_element_type=F32)
    sums_ref[row] = sums_ref[row] + (product[:8] + product[8:])


def fold_sums(sums_ref, out_ref):
    shape = (8, LANES)
    for row in range(sums_ref.shape[0]):
        total = sums_ref[row]
        total = total + pltpu.roll(total, 4, 0)
        total = total + pltpu.roll(total, 2, 0)
        picked = jnp.zeros(shape, F32)
        for piece in range(4):
            picked = jnp.where(row_index(shape) // 2 == piece, total[:, LANES * piece : LANES * (piece + 1)], picked)
        out_ref[8 * row : 8 * row + 8, :] = picked


def dipole_kernel(pattern_ref, idx_ref, block_ref, mine_ref, left_ref, right_ref, out_ref, states_ref, sums_ref):
    step = pl.program_id(0)

    @pl.when(step == 0)
    def _():
        expand_states(left_ref, mine_ref, right_ref, states_ref)
        sums_ref[...] = jnp.zeros(sums_ref.shape, F32)

    add_block(pattern_ref, idx_ref, block_ref, states_ref, sums_ref)

    @pl.when(step == pl.num_programs(0) - 1)
    def _():
        fold_sums(sums_ref, out_ref)


def pack_kernel(idx_ref, dipole_ref, surf_ref, cols_ref, edge_ref, w_ref, first_ref, left_ref, right_ref, message_ref, side_ref, total_ref):
    reg, ch = idx_ref[0], idx_ref[1]
    chan = surf_ref.shape[0]
    padded = cols_ref.shape[0]
    tiles = surf_ref.shape[1] // LANES
    windows = message_ref.shape[0]
    regs = first_ref.shape[0] // windows
    sym = wide(cols_ref[:chan, 0:1])
    received = first_ref[ch]
    lane2 = lane_index((2, LANES))
    low = jnp.where(lane2 < WINDOW, received, 0.0)
    cell0 = jnp.where(lane2 < WINDOW, pltpu.roll(jnp.concatenate([received] * 4, axis=0), WINDOW, 1)[0:2], 0.0)
    cell1 = jnp.where(reg == 0, edge_ref[4 * windows : 4 * windows + 2, :], low)
    whole = jnp.zeros((2, LANES), F32)
    for source in range(regs):
        whole = whole + first_ref[source * windows + ch]
    whole = jnp.where((lane2 < WINDOW) & (reg == 0), whole, 0.0)
    beside = left_ref[HALO_ROWS : HALO_ROWS + 2, :] + right_ref[HALO_ROWS : HALO_ROWS + 2, :]
    side = square(
        jnp.concatenate(
            [
                cell0, cell1, beside, whole,
                left_ref[HALO_ROWS + 2 : HALO_ROWS + 4, :], right_ref[HALO_ROWS + 2 : HALO_ROWS + 4, :],
                left_ref[HALO_ROWS + 4 : HALO_ROWS + 6, :], right_ref[HALO_ROWS + 4 : HALO_ROWS + 6, :],
            ],
            axis=0,
        )
    )[:chan]
    symmetry, energy = cols_ref[:chan, 0:1], cols_ref[:chan, 1:2]
    radius = BOUNDARY_RADIUS + GRID_STEP
    potential = symmetry * (symmetry + 1.0) / (2.0 * radius * radius) + energy
    slope, start = [], []
    for part in range(2):
        here, beyond = side[:, part : part + 1], side[:, 2 + part : 3 + part]
        boundary = cols_ref[:chan, 2 + part : 3 + part] + side[:, 4 + part : 5 + part]
        slope.append(here - boundary)
        start.append(-2.0 * (beyond - 2.0 * here + boundary) + potential * here)
    lane = lane_index((chan, LANES))
    out = jnp.where((lane >= 6) & (lane < 16), side, 0.0)
    for part in range(2):
        out = jnp.where(lane == part, wide(start[part]), out)
    out = jnp.where(lane == 2, sym, out)
    out = jnp.where(lane == 3, wide(energy), out)
    side_ref[...] = jnp.concatenate([out, jnp.zeros((padded - chan, LANES), F32)], axis=0)
    total_ref[...] = dipole_ref[...]
    surface_rows(slope, surf_ref, sym, reg * tiles, tiles, total_ref)
    lines = total_ref.shape[0]
    total = total_ref[...]
    tail = jnp.concatenate([edge_ref[4 * windows + 4 : 4 * windows + 6, :], whole, jnp.zeros((6, LANES), F32)], axis=0)
    half = lane < WINDOW
    for window in range(windows):
        message_ref[window, :lines, :] = total
        at = LANES * (window // 2)
        one, two = w_ref[0, :, at : at + LANES], w_ref[1, :, at : at + LANES]
        if window % 2 == 0:
            cells = jnp.where(half, one, pltpu.roll(two, WINDOW, 1))
        else:
            cells = jnp.where(half, pltpu.roll(one, WINDOW, 1), two)
        message_ref[window, lines : lines + padded, :] = jnp.concatenate(
            [cells, jnp.zeros((padded - chan, LANES), F32)], axis=0
        )
        edges = edge_ref[4 * window : 4 * window + 4, :]
        if window == 0:
            edges = jnp.concatenate([left_ref[HALO_ROWS + 3 : HALO_ROWS + 4, :], left_ref[HALO_ROWS + 5 : HALO_ROWS + 6, :], edges[2:4]], axis=0)
        if window == windows - 1:
            edges = jnp.concatenate([edges[0:2], right_ref[HALO_ROWS + 2 : HALO_ROWS + 3, :], right_ref[HALO_ROWS + 4 : HALO_ROWS + 5, :]], axis=0)
        message_ref[window, lines + padded :, :] = jnp.concatenate([edges, cell0, tail], axis=0)


def doubled(energy_ref, rows_ref):
    for tile in range(energy_ref.shape[0]):
        rows_ref[2 * tile : 2 * tile + 2, :] = jnp.broadcast_to(energy_ref[tile : tile + 1, :], (2, LANES))


def update_kernel(idx_ref, received_ref, u_ref, energy_ref, surf_ref, cols_ref, out_ref, left_ref, right_ref, energy_rows_ref):
    reg = idx_ref[0]
    lines = u_ref.shape[0]
    tiles = lines // 2
    chan = surf_ref.shape[0]
    doubled(energy_ref, energy_rows_ref)
    image = energy_rows_ref[...] * u_ref[...]
    for source in range(received_ref.shape[0]):
        image = image + received_ref[source, :lines, :]
    out_ref[...] = FIRST * turn_rows(image)
    sym = wide(cols_ref[:chan, 0:1])
    partial = boundary_sum(
        lambda tile, part: out_ref[2 * tile + part : 2 * tile + part + 1, :], surf_ref, sym, reg * tiles, tiles
    )
    lane = lane_index((chan, LANES))
    cols = jnp.where(lane == 0, wide(partial[0]), 0.0)
    cols = jnp.where(lane == 1, wide(partial[1]), cols)
    rows = jnp.concatenate([cols, jnp.zeros((LANES - chan, LANES), F32)], axis=0).T[0:8, :]
    left_ref[:HALO_ROWS, :] = out_ref[:HALO_ROWS, :]
    left_ref[HALO_ROWS:, :] = rows
    right_ref[:HALO_ROWS, :] = out_ref[lines - HALO_ROWS :, :]
    right_ref[HALO_ROWS:, :] = rows


def stencil(cells, lows, highs, potential, seams):
    count = cells.shape[1]
    lane = lane_index(cells.shape)
    below, above = pltpu.roll(cells, 1, 1), pltpu.roll(cells, count - 1, 1)
    for (first, last), low, high in zip(seams, lows, highs):
        below = jnp.where(lane == first, low, below)
        above = jnp.where(lane == last, high, above)
    return -2.0 * (above - 2.0 * cells + below) + potential * cells


def outer_kernel(idx_ref, received_ref, mats_ref, w_ref, side_ref, cross_ref, start_ref, plain_ref, edge_ref):
    reg, ch = idx_ref[0], idx_ref[1]
    groups, padded = cross_ref.shape[0], cross_ref.shape[1]
    chan, count = w_ref.shape[1], w_ref.shape[2]
    rows = groups * padded
    lines = received_ref.shape[1] - padded - 16
    cells = received_ref[:, lines : lines + padded, :].reshape(rows, LANES)
    flipped = received_ref[:, lines + padded :, :].reshape(groups * 16, LANES).T
    extra = jnp.concatenate(
        [pltpu.roll(flipped[:padded], (LANES - 16 * group) % LANES, 1) for group in range(groups)], axis=0
    )
    first_point = reg * count + ch * WINDOW
    lane = lane_index((1, LANES))
    point = (first_point + lane % WINDOW + 1).astype(F32)
    radius = BOUNDARY_RADIUS + GRID_STEP * point
    extra_point = jnp.where(lane < 2, first_point, jnp.where(lane < 4, first_point + WINDOW + 1, 1)).astype(F32)
    extra_ratio = BOUNDARY_RADIUS / (BOUNDARY_RADIUS + GRID_STEP * extra_point)
    ratio = BOUNDARY_RADIUS / radius

    def mix(states, scale):
        totals = jnp.dot(mats_ref[...], states.astype(jnp.bfloat16), preferred_element_type=F32)
        mixed = totals[:rows] + scale * totals[rows : 2 * rows] + scale * scale * totals[2 * rows :]
        return mixed.astype(jnp.bfloat16).astype(F32)

    symmetry, energy = extra[:, 6:7], extra[:, 7:8]
    potential = symmetry * (symmetry + 1.0) / (2.0 * radius * radius) + energy
    mixed = mix(jnp.concatenate([cells, extra], axis=1), jnp.concatenate([ratio, extra_ratio], axis=1))
    main, beside = mixed[:, :LANES], mixed[:, LANES:]
    edge_ref[...] = beside
    start_ref[...] = edge_ref[pl.ds(pl.multiple_of(ch * padded, 8), padded), :]
    inner_end = (reg == 0) & (ch == 0)
    seams = ((0, WINDOW - 1), (WINDOW, 2 * WINDOW - 1))
    lows = [jnp.where(inner_end, extra[:, 8 + part : 9 + part], extra[:, part : part + 1]) for part in range(2)]
    highs = [extra[:, 2 + part : 3 + part] for part in range(2)]
    first = FIRST * turn_lanes(stencil(cells, lows, highs, potential, seams) + main)
    later = mix(first, ratio)
    cross = FIRST * turn_lanes(main)
    mixed_lows = [jnp.where(inner_end, 0.0, beside[:, part : part + 1]) for part in range(2)]
    mixed_highs = [beside[:, 2 + part : 3 + part] for part in range(2)]
    lows = [FIRST * mixed_lows[1], -FIRST * mixed_lows[0]]
    highs = [FIRST * mixed_highs[1], -FIRST * mixed_highs[0]]
    cross = cross + SECOND * turn_lanes(stencil(cross, lows, highs, potential, seams) + later)
    cross_ref[...] = cross.reshape(groups, padded, LANES)

    side = side_ref[...][:chan]
    symmetry, energy = side[:, 2:3], side[:, 3:4]
    lane = lane_index((1, count))
    radius = BOUNDARY_RADIUS + GRID_STEP * (reg * count + lane + 1).astype(F32)
    potential = symmetry * (symmetry + 1.0) / (2.0 * radius * radius) + energy

    def potential_at(index):
        there = BOUNDARY_RADIUS + GRID_STEP * (reg * count + index + 1).astype(F32)
        return symmetry * (symmetry + 1.0) / (2.0 * there * there) + energy

    last = (reg + 1) * count >= cross_end(count)
    images, lows, highs = [], [], []
    for part in range(2):
        values = w_ref[part]
        at = 8 + 4 * part
        low2, low1, high1, high2 = (side[:, at + i : at + i + 1] for i in range(4))
        low = jnp.where(reg == 0, side[:, 6 + part : 7 + part], low1)
        images.append(stencil(values, [low], [high1], potential, ((0, count - 1),)))
        under = -2.0 * (values[:, 0:1] - 2.0 * low1 + low2) + potential_at(jnp.int32(-1)) * low1
        over = -2.0 * (high2 - 2.0 * high1 + values[:, count - 1 : count]) + potential_at(jnp.int32(count)) * high1
        lows.append(jnp.where(reg == 0, 0.0, under))
        highs.append(jnp.where(last, 0.0, over))
    turned = [FIRST * images[1], -FIRST * images[0]]
    lows = [FIRST * lows[1], -FIRST * lows[0]]
    highs = [FIRST * highs[1], -FIRST * highs[0]]
    again = [stencil(turned[p], [lows[p]], [highs[p]], potential, ((0, count - 1),)) for p in range(2)]
    plain_ref[0] = w_ref[0] + turned[0] + SECOND * again[1]
    plain_ref[1] = w_ref[1] + turned[1] - SECOND * again[0]


def cross_end(count):
    return 16 * count


def second_kernel(
    pattern_ref, idx_ref, block_ref, mine_ref, left_ref, right_ref, own_ref, surf_ref, side_ref, start_ref, cross_ref,
    message_ref, states_ref, sums_ref, total_ref,
):
    step = pl.program_id(0)

    @pl.when(step == 0)
    def _():
        expand_states(left_ref, mine_ref, right_ref, states_ref)
        sums_ref[...] = jnp.zeros(sums_ref.shape, F32)

    add_block(pattern_ref, idx_ref, block_ref, states_ref, sums_ref)

    @pl.when(step == pl.num_programs(0) - 1)
    def _():
        reg = idx_ref[0]
        chan = surf_ref.shape[0]
        tiles = surf_ref.shape[1] // LANES
        fold_sums(sums_ref, total_ref)
        ends = own_ref[HALO_ROWS:, :] + left_ref[HALO_ROWS:, :] + right_ref[HALO_ROWS:, :]
        boundary = square(ends)[:chan]
        mixed = start_ref[:chan, :]
        side = side_ref[:chan, :]
        image = [side[:, part : part + 1] + mixed[:, 4 + part : 5 + part] for part in range(2)]
        slope = [FIRST * image[1] - boundary[:, 0:1], -FIRST * image[0] - boundary[:, 1:2]]
        surface_rows(slope, surf_ref, wide(side[:, 2:3]), reg * tiles, tiles, total_ref)
        lines = total_ref.shape[0]
        for group in range(message_ref.shape[0]):
            message_ref[group, :lines, :] = total_ref[...]
            message_ref[group, lines:, :] = cross_ref[group]


def finish_kernel(idx_ref, received_ref, u_ref, first_ref, energy_ref, plain_ref, ends_ref, inner_ref, outer_ref, energy_rows_ref):
    reg = idx_ref[0]
    lines = u_ref.shape[0]
    chan = plain_ref.shape[1]
    doubled(energy_ref, energy_rows_ref)
    image = energy_rows_ref[...] * first_ref[...]
    sources = received_ref.shape[0]
    for source in range(sources):
        image = image + received_ref[source, :lines, :]
    total = u_ref[...] + first_ref[...] + SECOND * turn_rows(image)
    energy_rows_ref[...] = total
    for tile in range(lines // 2):
        inner_ref[:, LANES * tile : LANES * (tile + 1)] = energy_rows_ref[2 * tile : 2 * tile + 2, :]
    columns = square(ends_ref[...])[:chan]
    lane = lane_index((chan, LANES))
    half = lane < WINDOW
    for piece in range(sources // 2):
        even = received_ref[2 * piece, lines : lines + chan, :]
        odd = received_ref[2 * piece + 1, lines : lines + chan, :]
        one = jnp.where(half, even, pltpu.roll(odd, WINDOW, 1))
        two = jnp.where(half, pltpu.roll(even, WINDOW, 1), odd)
        at = slice(LANES * piece, LANES * (piece + 1))
        one = plain_ref[0, :, at] + one
        two = plain_ref[1, :, at] + two
        if piece == 0:
            here = (lane == 0) & (reg == 0)
            one = one + jnp.where(here, -2.0 * SECOND * columns[:, 1:2], 0.0)
            two = two + jnp.where(here, 2.0 * SECOND * columns[:, 0:1], 0.0)
        outer_ref[0, :, at] = one
        outer_ref[1, :, at] = two


def build_mats(source, order_list, weight, groups, chan_local, padded):
    def lay(values, fill):
        values = values.reshape(groups, chan_local, values.shape[1])
        values = jnp.pad(values, ((0, 0), (0, padded - chan_local), (0, 0)), constant_values=fill)
        return values.reshape(groups * padded, -1)

    place = (source // chan_local) * padded + source % chan_local
    place, order_list, weight = lay(place, 0), lay(order_list, NLAM), lay(weight, 0)
    onehot = place[:, :, None] == jnp.arange(groups * padded, dtype=jnp.int32)[None, None, :]
    matrices = []
    for order in range(NLAM):
        picked = jnp.where(order_list == order, weight, 0.0)
        matrices.append(jnp.sum(jnp.where(onehot, picked[:, :, None], 0.0), axis=1).astype(jnp.bfloat16))
    return jnp.concatenate(matrices, axis=0)


def shape_of(*shape):
    return jax.ShapeDtypeStruct(shape, F32)


def local(
    inner_state, energy, blocks, pattern, surface, channel_symmetry, outer_state, channel_energy,
    couple_source, couple_order, couple_weight, *, regs, groups,
):
    tile_len = inner_state.shape[1]
    lines = 2 * tile_len // LANES
    block_len = blocks.shape[1]
    block_rows = tile_len // block_len
    chan = outer_state.shape[1]
    count = outer_state.shape[2]
    padded = -(-chan // 8) * 8
    devices = regs * groups
    idx = jnp.stack([lax.axis_index("reg"), lax.axis_index("ch")]).astype(jnp.int32)
    smem = pl.BlockSpec(memory_space=pltpu.SMEM)
    vmem = pl.BlockSpec(memory_space=pltpu.VMEM)
    halo = HALO_ROWS + 8
    energy_rows = energy.reshape(lines // 2, LANES)

    first_msg, left, right, rows, cols, edges = pl.pallas_call(
        start_kernel,
        out_shape=(
            shape_of(devices, 2, LANES), shape_of(halo, LANES), shape_of(halo, LANES), shape_of(lines, LANES),
            shape_of(padded, LANES), shape_of(4 * groups + 8, LANES),
        ),
        in_specs=[smem] + [vmem] * 5,
        out_specs=(vmem,) * 6,
        scratch_shapes=[pltpu.VMEM((2, count, LANES), F32)],
        compiler_params=params(32),
        name="start",
    )(idx, inner_state, surface, channel_symmetry.reshape(1, chan), channel_energy.reshape(1, chan), outer_state)

    firsts = lax.all_to_all(first_msg, ("reg", "ch"), 0, 0)
    up = [(i, i + 1) for i in range(regs - 1)]
    down = [(i + 1, i) for i in range(regs - 1)]
    from_left = lax.ppermute(right, "reg", up)
    from_right = lax.ppermute(left, "reg", down)
    mats = build_mats(couple_source, couple_order, couple_weight, groups, chan, padded)

    whole = lambda *shape: pl.BlockSpec(shape, lambda step, *_: (0,) * len(shape))
    block_spec = pl.BlockSpec((1, block_len, block_len), lambda step, *_: (step, 0, 0))
    states = pltpu.VMEM((2 * HALO_BLOCKS + block_rows, 16, block_len), jnp.bfloat16)
    sums = pltpu.VMEM((block_rows, 8, block_len), F32)
    dipole = pl.pallas_call(
        dipole_kernel,
        grid_spec=pltpu.PrefetchScalarGridSpec(
            num_scalar_prefetch=2,
            grid=(blocks.shape[0],),
            in_specs=[block_spec, whole(lines, LANES), whole(halo, LANES), whole(halo, LANES)],
            out_specs=whole(lines, LANES),
            scratch_shapes=[states, sums],
        ),
        out_shape=shape_of(lines, LANES),
        compiler_params=params(32),
        name="dipole",
    )(pattern, idx, blocks, rows, from_left, from_right)

    message, side = pl.pallas_call(
        pack_kernel,
        out_shape=(shape_of(groups, lines + padded + 16, LANES), shape_of(padded, LANES)),
        in_specs=[smem] + [vmem] * 8,
        out_specs=(vmem,) * 2,
        scratch_shapes=[pltpu.VMEM((lines, LANES), F32)],
        compiler_params=params(32),
        name="pack",
    )(idx, dipole, surface, cols, edges, outer_state, firsts, from_left, from_right)
    received = lax.all_to_all(message, "ch", 0, 0)

    first, left, right = pl.pallas_call(
        update_kernel,
        out_shape=(shape_of(lines, LANES), shape_of(halo, LANES), shape_of(halo, LANES)),
        in_specs=[smem] + [vmem] * 5,
        out_specs=(vmem,) * 3,
        scratch_shapes=[pltpu.VMEM((lines, LANES), F32)],
        compiler_params=params(32),
        name="update",
    )(idx, received, rows, energy_rows, surface, cols)
    from_left = lax.ppermute(right, "reg", up)
    from_right = lax.ppermute(left, "reg", down)

    cross, start, plain = pl.pallas_call(
        outer_kernel,
        out_shape=(shape_of(groups, padded, LANES), shape_of(padded, LANES), shape_of(2, chan, count)),
        in_specs=[smem] + [vmem] * 4,
        out_specs=(vmem,) * 3,
        scratch_shapes=[pltpu.VMEM((groups * padded, LANES), F32)],
        compiler_params=params(48),
        name="outer",
    )(idx, received, mats, outer_state, side)

    message = pl.pallas_call(
        second_kernel,
        grid_spec=pltpu.PrefetchScalarGridSpec(
            num_scalar_prefetch=2,
            grid=(blocks.shape[0],),
            in_specs=[
                block_spec, whole(lines, LANES), whole(halo, LANES), whole(halo, LANES), whole(halo, LANES),
                whole(chan, tile_len), whole(padded, LANES), whole(padded, LANES), whole(groups, padded, LANES),
            ],
            out_specs=whole(groups, lines + padded, LANES),
            scratch_shapes=[states, sums, pltpu.VMEM((lines, LANES), F32)],
        ),
        out_shape=shape_of(groups, lines + padded, LANES),
        compiler_params=params(32),
        name="second",
    )(pattern, idx, blocks, first, from_left, from_right, left, surface, side, start, cross)

    ends = left[HALO_ROWS:] + from_right[HALO_ROWS:]
    step = 2
    while step < regs:
        pairs = [(i + step, i) for i in range(0, regs, 2 * step)]
        ends = ends + lax.ppermute(ends, "reg", pairs)
        step *= 2
    received = lax.all_to_all(message, "ch", 0, 0)

    return pl.pallas_call(
        finish_kernel,
        out_shape=(shape_of(2, tile_len), shape_of(2, chan, count)),
        in_specs=[smem] + [vmem] * 6,
        out_specs=(vmem,) * 2,
        scratch_shapes=[pltpu.VMEM((lines, LANES), F32)],
        compiler_params=params(32),
        name="finish",
    )(idx, received, rows, first, energy_rows, plain, ends)


def solution(mesh):
    return jax.shard_map(
        functools.partial(local, regs=mesh.shape["reg"], groups=mesh.shape["ch"]),
        mesh=mesh,
        in_specs=(
            P(None, "reg"),
            P("reg"),
            P(("reg", "ch"), None, None),
            P(("reg", "ch"), None),
            P("ch", "reg"),
            P("ch"),
            P(None, "ch", "reg"),
            P("ch"),
            P(),
            P(),
            P(),
        ),
        out_specs=(P(None, "reg"), P(None, "ch", "reg")),
        check_vma=False,
    )
```

time: 300 us -> 102 us (0.34)
  the two profiles are of different devices: /device:TPU:6 before, /device:TPU:16 now
where the time goes in v1:
time: 102 us
  starting transfers between devices  36.1 us (35%)
  waiting for transfers between devices  28.9 us (28%)
  Pallas kernels  19.5 us (19%)
  local copies, waits for them, and re-layouts  13.5 us (13%)
  other arithmetic  2.95 us (3%)
    ppermute x3, waiting for transfers between devices, local(): ends = ends + lax.ppermute(ends, 'reg', pairs)  18.1 us
    all_to_all x2, starting transfers between devices, local(): received = lax.all_to_all(message, 'ch', 0, 0)  13.9 us
    unnamed x30, local copies, waits for them, and re-layouts  12.1 us
    all_to_all x1, starting transfers between devices, local(): firsts = lax.all_to_all(first_msg, ('reg', 'ch'), 0, 0)  10.3 us
    all_to_all x2, waiting for transfers between devices, local(): received = lax.all_to_all(message, 'ch', 0, 0)  8.13 us
    pallas_call x1, Pallas kernels, local(): pl.pallas_call(second_kernel, grid_spec=pltpu.PrefetchScalarGridSpec(num_...  5.56 us
    ppermute x2, starting transfers between devices, local(): from_left = lax.ppermute(right, 'reg', up)  5.52 us
    pallas_call x1, Pallas kernels, local(): pl.pallas_call(dipole_kernel, grid_spec=pltpu.PrefetchScalarGridSpec(num_...  3.93 us
  transfers between devices with their start and end apart: 10, of which 6 were waited for; matrix products, arithmetic and copies ran while one was open for 4% of the time, Pallas kernels for 7%

profile of v1, /device:TPU:16, one launch (start us, length us, event | category | flops | bytes accessed | tf_op | source)
XLA Modules:
  0.0 101.8 jit_solution(6333970716313767901)
XLA Ops:
  0.6 1.0 copy.23.w_ref
  1.6 0.1 pad_add_fusion.idx_ref
  1.7 1.5 %copy-done.2 = f32[52,7680]{1,0:T(8,128)S(1)} copy-done((f32[52,7680]{1,0:T(8,128)S(1)}, f32[52,7680]{1,0:T(8,128)}, u32[]{:S(2)}) %copy-start.2) | copy-done | bytes 1597464
  3.2 0.8 copy-done.5
  4.0 0.7 copy-done.6
  4.6 0.7 copy-done.7
  5.3 2.1 %start.1 = (f32[128,2,128]{2,1,0:T(2,128)}, f32[64,128]{1,0:T(8,128)S(1)}, f32[64,128]{1,0:T(8,128)S(1)}, f32[120,128]{1,0:T(8,128)S(1)}, f32[56,128]{1,0:T(8,128)S(1)}, /*index=5*/f32[40,128]{1,0:T(8,128)S(1)}) custom-call(s32[2]{0:T(128)S(1)} %pad_add_fusion.idx_ref, f32[2,7680]{1,0:T(2,128)S(1)} %copy-done.5, f32[52,7680]{1,0:T(8,128)S(1)} %copy-done.2, ...), custom_call_target="tpu_custom_call" | custom-call | tf_op jit(solution)/shard_map/start/pallas_call | solution.py:488
  7.4 10.3 %all-to-all-start = ((f32[128,2,128]{2,1,0:T(2,128)}), f32[128,2,128]{2,1,0:T(2,128)S(1)}, u32[]{:S(2)}, u32[]{:S(2)}) async-start(f32[128,2,128]{2,1,0:T(2,128)} %get-tuple-element.21), calls=%async_computation | async-start | bytes 262144 | tf_op jit(solution)/shard_map/all_to_all | solution.py:501
  17.7 2.1 %collective-permute-start = (f32[64,128]{1,0:T(8,128)S(1)}, f32[64,128]{1,0:T(8,128)S(1)}, u32[]{:S(2)}, u32[]{:S(2)}) collective-permute-start(f32[64,128]{1,0:T(8,128)S(1)} %get-tuple-element.17), channel_id=1, source_target_pairs={{0,8},{8,16},{16,24},{24,32},{32,40},{40,48},{48,56},{56,64},{64,7... | collective-permute-start | bytes 98312 | tf_op jit(solution)/shard_map/ppermute | solution.py:504
  19.8 1.3 %collective-permute-start.1 = (f32[64,128]{1,0:T(8,128)S(1)}, f32[64,128]{1,0:T(8,128)S(1)}, u32[]{:S(2)}, u32[]{:S(2)}) collective-permute-start(f32[64,128]{1,0:T(8,128)S(1)} %get-tuple-element.18), channel_id=1, source_target_pairs={{8,0},{16,8},{24,16},{32,24},{40,32},{48,40},{56,48},{64,56},{72,6... | collective-permute-start | bytes 98312 | tf_op jit(solution)/shard_map/ppermute | solution.py:505
  21.1 0.8 copy.27.pattern_ref
  21.9 0.0 collective-permute-done.left_ref
  21.9 2.0 %collective-permute-done.1.right_ref = f32[64,128]{1,0:T(8,128)S(1)} collective-permute-done((f32[64,128]{1,0:T(8,128)S(1)}, f32[64,128]{1,0:T(8,128)S(1)}, u32[]{:S(2)}, u32[]{:S(2)}) %collective-permute-start.1) | collective-permute-done | bytes 32800 | tf_op jit(solution)/shard_map/ppermute | solution.py:505
  23.8 3.4 %copy-done = f32[8,512,512]{2,1,0:T(8,128)S(1)} copy-done((f32[8,512,512]{2,1,0:T(8,128)S(1)}, f32[8,512,512]{2,1,0:T(8,128)}, u32[]{:S(2)}) %copy-start) | copy-done | bytes 8388632
  27.2 3.9 %dipole.1.dipole_ref = f32[120,128]{1,0:T(8,128)S(1)} custom-call(s32[8,2]{1,0:T(8,128)S(1)} %copy.27.pattern_ref, s32[2]{0:T(128)S(1)} %pad_add_fusion.idx_ref, f32[8,512,512]{2,1,0:T(8,128)S(1)} %copy-done, f32[120,128]{1,0:T(8,128)S(1)} %get-tuple-element.16.mine_ref.u_ref, f32[64,128]{1,0:T(8,128)S(1)} %collective-permute-done.left_ref, ...), custom_call_target="tpu_custom_call" | custom-call | tf_op jit(solution)/shard_map/dipole/pallas_call | solution.py:512
  31.2 0.0 copy-start.11
  31.2 0.0 copy-start.12
  31.2 0.0 copy-start.13
  31.2 0.0 copy-start.4
  31.2 2.3 %pack.1 = (f32[8,192,128]{2,1,0:T(8,128)}, f32[56,128]{1,0:T(8,128)S(1)}) custom-call(s32[2]{0:T(128)S(1)} %pad_add_fusion.idx_ref, f32[120,128]{1,0:T(8,128)S(1)} %dipole.1.dipole_ref, f32[52,7680]{1,0:T(8,128)S(1)} %copy-done.3, f32[56,128]{1,0:T(8,128)S(1)} %get-tuple-element.19.cols_ref, f32[40,128]{1,0:T(8,128)S(1)} %get-tuple-element.20.edge_ref, ...), custom_call_target="tpu_custom_call" | custom-call | tf_op jit(solution)/shard_map/pack/pallas_call | solution.py:526
  33.5 7.7 %all-to-all-start.1 = ((f32[8,192,128]{2,1,0:T(8,128)}), f32[8,192,128]{2,1,0:T(8,128)S(1)}, u32[]{:S(2)}, u32[]{:S(2)}) async-start(f32[8,192,128]{2,1,0:T(8,128)} %get-tuple-element.22), calls=%async_computation.1 | async-start | bytes 1572864 | tf_op jit(solution)/shard_map/all_to_all | solution.py:535
  41.2 0.1 reshape.72
  41.3 0.1 reshape.71
  41.4 0.1 select_n.56
  41.6 0.1 reshape.70
  41.6 0.1 eq.50
  41.7 0.1 select_n.62
  41.8 0.1 select_n.59
  41.9 2.6 %select_reduce_fusion.2 = (bf16[448,448]{1,0:T(8,128)(2,1)}, bf16[448,448]{1,0:T(8,128)(2,1)}, bf16[448,448]{1,0:T(8,128)(2,1)}) fusion(f32[448,4]{0,1:T(4,128)S(1)} %select_n.56, s32[448,4]{0,1:T(4,128)S(1)} %eq.50, f32[448,4]{0,1:T(4,128)S(1)} %select_n.62, f32[448,4]{0,1:T(4,128)S(1)} %select_n.59), kind=kLoop, calls=%fused_computation.2 | loop fusion | flops 5017600 | bytes 1232896 | tf_op jit(solution)/shard_map/reduce_sum | solution.py:462
  44.5 8.1 %all-to-all-done.1.received_ref = f32[8,192,128]{2,1,0:T(8,128)S(1)} async-done(((f32[8,192,128]{2,1,0:T(8,128)}), f32[8,192,128]{2,1,0:T(8,128)S(1)}, u32[]{:S(2)}, u32[]{:S(2)}) %all-to-all-start.1) | async-done | bytes 786464 | tf_op jit(solution)/shard_map/all_to_all | solution.py:535
  52.7 1.4 %update.1 = (f32[120,128]{1,0:T(8,128)S(1)}, f32[64,128]{1,0:T(8,128)S(1)}, f32[64,128]{1,0:T(8,128)S(1)}) custom-call(s32[2]{0:T(128)S(1)} %pad_add_fusion.idx_ref, f32[8,192,128]{2,1,0:T(8,128)S(1)} %all-to-all-done.1.received_ref, f32[120,128]{1,0:T(8,128)S(1)} %get-tuple-element.16.mine_ref.u_ref, f32[60,128]{1,0:T(8,128)S(1)} %bitcast.19, ...), custom_call_target="tpu_custom_call" | custom-call | tf_op jit(solution)/shard_map/update/pallas_call | solution.py:537
  54.0 3.5 %collective-permute-start.2 = (f32[64,128]{1,0:T(8,128)S(1)}, f32[64,128]{1,0:T(8,128)S(1)}, u32[]{:S(2)}, u32[]{:S(2)}) collective-permute-start(f32[64,128]{1,0:T(8,128)S(1)} %get-tuple-element.24), channel_id=1, source_target_pairs={{0,8},{8,16},{16,24},{24,32},{32,40},{40,48},{48,56},{56,64},{64,7... | collective-permute-start | bytes 98312 | tf_op jit(solution)/shard_map/ppermute | solution.py:546
  57.5 1.3 %collective-permute-start.3 = (f32[64,128]{1,0:T(8,128)S(1)}, f32[64,128]{1,0:T(8,128)S(1)}, u32[]{:S(2)}, u32[]{:S(2)}) collective-permute-start(f32[64,128]{1,0:T(8,128)S(1)} %get-tuple-element.25.own_ref), channel_id=1, source_target_pairs={{8,0},{16,8},{24,16},{32,24},{40,32},{48,40},{56,48},{64,56},{72,6... | collective-permute-start | bytes 98312 | tf_op jit(solution)/shard_map/ppermute | solution.py:547
  58.8 0.2 pad_maximum_fusion.mats_ref
  59.0 2.9 %outer.1 = (f32[8,56,128]{2,1,0:T(8,128)S(1)}, f32[56,128]{1,0:T(8,128)S(1)}, f32[2,52,512]{2,1,0:T(8,128)S(1)}) custom-call(s32[2]{0:T(128)S(1)} %pad_add_fusion.idx_ref, f32[8,192,128]{2,1,0:T(8,128)S(1)} %all-to-all-done.1.received_ref, bf16[1344,448]{1,0:T(8,128)(2,1)S(1)} %pad_maximum_fusion.mats_ref, f32[2,52,512]{2,1,0:T(8,128)S(1)} %copy.23.w_ref, ...), custom_call_target="tpu_custom_call" | custom-call | tf_op jit(solution)/shard_map/outer/pallas_call | solution.py:549
  61.9 0.0 collective-permute-done.2.left_ref
  61.9 0.6 collective-permute-done.3.right_ref
  62.6 3.4 %copy-done.1 = f32[8,512,512]{2,1,0:T(8,128)S(1)} copy-done((f32[8,512,512]{2,1,0:T(8,128)S(1)}, f32[8,512,512]{2,1,0:T(8,128)}, u32[]{:S(2)}) %copy-start.1) | copy-done | bytes 8388632
  66.0 5.6 %second.1 = f32[8,176,128]{2,1,0:T(8,128)} custom-call(s32[8,2]{1,0:T(8,128)S(1)} %copy.27.pattern_ref, s32[2]{0:T(128)S(1)} %pad_add_fusion.idx_ref, f32[8,512,512]{2,1,0:T(8,128)S(1)} %copy-done.1, f32[120,128]{1,0:T(8,128)S(1)} %get-tuple-element.23.mine_ref.first_ref, f32[64,128]{1,0:T(8,128)S(1)} %collective-permute-done.2.left_ref, ...), custom_call_target="tpu_custom_call" | custom-call | tf_op jit(solution)/shard_map/second/pallas_call | solution.py:559
  71.5 6.1 %all-to-all-start.2 = ((f32[8,176,128]{2,1,0:T(8,128)}), f32[8,176,128]{2,1,0:T(8,128)S(1)}, u32[]{:S(2)}, u32[]{:S(2)}) async-start(f32[8,176,128]{2,1,0:T(8,128)} %second.1), calls=%async_computation.2 | async-start | bytes 1441792 | tf_op jit(solution)/shard_map/all_to_all | solution.py:582
  77.6 1.3 %collective-permute-start.4 = (f32[8,128]{1,0:T(8,128)S(1)}, f32[8,128]{1,0:T(8,128)S(1)}, u32[]{:S(2)}, u32[]{:S(2)}) collective-permute-start(f32[8,128]{1,0:T(8,128)S(1)} %slice_add_fusion), channel_id=1, source_target_pairs={{16,0},{48,32},{80,64},{112,96},{17,1},{49,33},{81,65},{113,97},{1... | collective-permute-start | bytes 12296 | tf_op jit(solution)/shard_map/ppermute | solution.py:580
  78.9 5.7 %collective-permute-done.4 = f32[8,128]{1,0:T(8,128)S(1)} collective-permute-done((f32[8,128]{1,0:T(8,128)S(1)}, f32[8,128]{1,0:T(8,128)S(1)}, u32[]{:S(2)}, u32[]{:S(2)}) %collective-permute-start.4) | collective-permute-done | bytes 4128 | tf_op jit(solution)/shard_map/ppermute | solution.py:580
  84.6 1.3 %collective-permute-start.5 = (f32[8,128]{1,0:T(8,128)S(1)}, f32[8,128]{1,0:T(8,128)S(1)}, u32[]{:S(2)}, u32[]{:S(2)}) collective-permute-start(f32[8,128]{1,0:T(8,128)S(1)} %add.31), channel_id=1, source_target_pairs={{32,0},{96,64},{33,1},{97,65},{34,2},{98,66},{35,3},{99,67},{36,4}... | collective-permute-start | bytes 12296 | tf_op jit(solution)/shard_map/ppermute | solution.py:580
  85.9 6.0 %collective-permute-done.5 = f32[8,128]{1,0:T(8,128)S(1)} collective-permute-done((f32[8,128]{1,0:T(8,128)S(1)}, f32[8,128]{1,0:T(8,128)S(1)}, u32[]{:S(2)}, u32[]{:S(2)}) %collective-permute-start.5) | collective-permute-done | bytes 4128 | tf_op jit(solution)/shard_map/ppermute | solution.py:580
  91.9 1.3 %collective-permute-start.6 = (f32[8,128]{1,0:T(8,128)S(1)}, f32[8,128]{1,0:T(8,128)S(1)}, u32[]{:S(2)}, u32[]{:S(2)}) collective-permute-start(f32[8,128]{1,0:T(8,128)S(1)} %add.32), channel_id=1, source_target_pairs={{64,0},{65,1},{66,2},{67,3},{68,4},{69,5},{70,6},{71,7}} | collective-permute-start | bytes 12296 | tf_op jit(solution)/shard_map/ppermute | solution.py:580
  93.2 6.4 %collective-permute-done.6 = f32[8,128]{1,0:T(8,128)S(1)} collective-permute-done((f32[8,128]{1,0:T(8,128)S(1)}, f32[8,128]{1,0:T(8,128)S(1)}, u32[]{:S(2)}, u32[]{:S(2)}) %collective-permute-start.6) | collective-permute-done | bytes 4128 | tf_op jit(solution)/shard_map/ppermute | solution.py:580
  99.6 1.3 %finish.1 = (f32[2,7680]{1,0:T(2,128)}, f32[2,52,512]{2,1,0:T(8,128)S(1)}) custom-call(s32[2]{0:T(128)S(1)} %pad_add_fusion.idx_ref, f32[8,176,128]{2,1,0:T(8,128)S(1)} %all-to-all-done.2.received_ref, f32[120,128]{1,0:T(8,128)S(1)} %get-tuple-element.16.mine_ref.u_ref, f32[120,128]{1,0:T(8,128)S(1)} %get-tuple-element.23.mine_ref.first_ref, ...), custom_call_target="tpu_custom_call" | custom-call | tf_op jit(solution)/shard_map/finish/pallas_call | solution.py:584
  101.0 0.8 copy.28
  (27 shorter events, 0.1 us)
Async XLA Ops:
  1.7 1.5 %copy-start.2 = (f32[52,7680]{1,0:T(8,128)S(1)}, f32[52,7680]{1,0:T(8,128)}, u32[]{:S(2)}) copy-start(f32[52,7680]{1,0:T(8,128)} %surf_ref.7) | copy-start | bytes 4792324
  3.2 0.8 copy-start.5
  4.0 0.7 copy-start.6
  4.6 0.7 copy-start.7
  7.4 23.8 %all-to-all-start = ((f32[128,2,128]{2,1,0:T(2,128)}), f32[128,2,128]{2,1,0:T(2,128)S(1)}, u32[]{:S(2)}, u32[]{:S(2)}) async-start(f32[128,2,128]{2,1,0:T(2,128)} %get-tuple-element.21), calls=%async_computation | async-start | bytes 262144 | tf_op jit(solution)/shard_map/all_to_all | solution.py:501
  17.7 4.1 %collective-permute-start = (f32[64,128]{1,0:T(8,128)S(1)}, f32[64,128]{1,0:T(8,128)S(1)}, u32[]{:S(2)}, u32[]{:S(2)}) collective-permute-start(f32[64,128]{1,0:T(8,128)S(1)} %get-tuple-element.17), channel_id=1, source_target_pairs={{0,8},{8,16},{16,24},{24,32},{32,40},{40,48},{48,56},{56,64},{64,7... | collective-permute-start | bytes 98312 | tf_op jit(solution)/shard_map/ppermute | solution.py:504
  19.8 4.0 %collective-permute-start.1 = (f32[64,128]{1,0:T(8,128)S(1)}, f32[64,128]{1,0:T(8,128)S(1)}, u32[]{:S(2)}, u32[]{:S(2)}) collective-permute-start(f32[64,128]{1,0:T(8,128)S(1)} %get-tuple-element.18), channel_id=1, source_target_pairs={{8,0},{16,8},{24,16},{32,24},{40,32},{48,40},{56,48},{64,56},{72,6... | collective-permute-start | bytes 98312 | tf_op jit(solution)/shard_map/ppermute | solution.py:505
  23.8 3.4 %copy-start = (f32[8,512,512]{2,1,0:T(8,128)S(1)}, f32[8,512,512]{2,1,0:T(8,128)}, u32[]{:S(2)}) copy-start(f32[8,512,512]{2,1,0:T(8,128)} %block_ref.3) | copy-start | bytes 25165828
  27.2 4.0 %copy-start.3 = (f32[52,7680]{1,0:T(8,128)S(1)}, f32[52,7680]{1,0:T(8,128)}, u32[]{:S(2)}) copy-start(f32[52,7680]{1,0:T(8,128)} %surf_ref.7) | copy-start | bytes 4792324
  31.2 10.1 %copy-start.11 = (f32[416,4]{0,1:T(4,128)S(1)}, f32[416,4]{0,1:T(4,128)}, u32[]{:S(2)}) copy-start(f32[416,4]{0,1:T(4,128)} %param.21) | copy-start | bytes 19972
  31.2 10.2 %copy-start.12 = (s32[416,4]{0,1:T(4,128)S(1)}, s32[416,4]{0,1:T(4,128)}, u32[]{:S(2)}) copy-start(s32[416,4]{0,1:T(4,128)} %param.20) | copy-start | bytes 19972
  31.2 10.3 %copy-start.13 = (s32[416,4]{0,1:T(4,128)S(1)}, s32[416,4]{0,1:T(4,128)}, u32[]{:S(2)}) copy-start(s32[416,4]{0,1:T(4,128)} %param.19) | copy-start | bytes 19972
  31.2 21.5 %copy-start.4 = (f32[7680]{0:T(1024)S(1)}, f32[7680]{0:T(1024)}, u32[]{:S(2)}) copy-start(f32[7680]{0:T(1024)} %param.12) | copy-start | bytes 92164
  33.5 19.1 %all-to-all-start.1 = ((f32[8,192,128]{2,1,0:T(8,128)}), f32[8,192,128]{2,1,0:T(8,128)S(1)}, u32[]{:S(2)}, u32[]{:S(2)}) async-start(f32[8,192,128]{2,1,0:T(8,128)} %get-tuple-element.22), calls=%async_computation.1 | async-start | bytes 1572864 | tf_op jit(solution)/shard_map/all_to_all | solution.py:535
  52.7 6.1 %copy-start.8 = (bf16[448,448]{1,0:T(8,128)(2,1)S(1)}, bf16[448,448]{1,0:T(8,128)(2,1)}, u32[]{:S(2)}) copy-start(bf16[448,448]{1,0:T(8,128)(2,1)} %get-tuple-element.34) | copy-start | bytes 1204228
  52.7 6.1 %copy-start.9 = (bf16[448,448]{1,0:T(8,128)(2,1)S(1)}, bf16[448,448]{1,0:T(8,128)(2,1)}, u32[]{:S(2)}) copy-start(bf16[448,448]{1,0:T(8,128)(2,1)} %get-tuple-element.35) | copy-start | bytes 1204228
  52.7 6.2 %copy-start.10 = (bf16[448,448]{1,0:T(8,128)(2,1)S(1)}, bf16[448,448]{1,0:T(8,128)(2,1)}, u32[]{:S(2)}) copy-start(bf16[448,448]{1,0:T(8,128)(2,1)} %get-tuple-element.36) | copy-start | bytes 1204228
  54.0 7.9 %collective-permute-start.2 = (f32[64,128]{1,0:T(8,128)S(1)}, f32[64,128]{1,0:T(8,128)S(1)}, u32[]{:S(2)}, u32[]{:S(2)}) collective-permute-start(f32[64,128]{1,0:T(8,128)S(1)} %get-tuple-element.24), channel_id=1, source_target_pairs={{0,8},{8,16},{16,24},{24,32},{32,40},{40,48},{48,56},{56,64},{64,7... | collective-permute-start | bytes 98312 | tf_op jit(solution)/shard_map/ppermute | solution.py:546
  57.5 5.1 %collective-permute-start.3 = (f32[64,128]{1,0:T(8,128)S(1)}, f32[64,128]{1,0:T(8,128)S(1)}, u32[]{:S(2)}, u32[]{:S(2)}) collective-permute-start(f32[64,128]{1,0:T(8,128)S(1)} %get-tuple-element.25.own_ref), channel_id=1, source_target_pairs={{8,0},{16,8},{24,16},{32,24},{40,32},{48,40},{56,48},{64,56},{72,6... | collective-permute-start | bytes 98312 | tf_op jit(solution)/shard_map/ppermute | solution.py:547
  62.6 3.4 %copy-start.1 = (f32[8,512,512]{2,1,0:T(8,128)S(1)}, f32[8,512,512]{2,1,0:T(8,128)}, u32[]{:S(2)}) copy-start(f32[8,512,512]{2,1,0:T(8,128)} %block_ref.3) | copy-start | bytes 25165828
  71.5 28.1 %all-to-all-start.2 = ((f32[8,176,128]{2,1,0:T(8,128)}), f32[8,176,128]{2,1,0:T(8,128)S(1)}, u32[]{:S(2)}, u32[]{:S(2)}) async-start(f32[8,176,128]{2,1,0:T(8,128)} %second.1), calls=%async_computation.2 | async-start | bytes 1441792 | tf_op jit(solution)/shard_map/all_to_all | solution.py:582
  77.6 6.9 %collective-permute-start.4 = (f32[8,128]{1,0:T(8,128)S(1)}, f32[8,128]{1,0:T(8,128)S(1)}, u32[]{:S(2)}, u32[]{:S(2)}) collective-permute-start(f32[8,128]{1,0:T(8,128)S(1)} %slice_add_fusion), channel_id=1, source_target_pairs={{16,0},{48,32},{80,64},{112,96},{17,1},{49,33},{81,65},{113,97},{1... | collective-permute-start | bytes 12296 | tf_op jit(solution)/shard_map/ppermute | solution.py:580
  84.6 7.3 %collective-permute-start.5 = (f32[8,128]{1,0:T(8,128)S(1)}, f32[8,128]{1,0:T(8,128)S(1)}, u32[]{:S(2)}, u32[]{:S(2)}) collective-permute-start(f32[8,128]{1,0:T(8,128)S(1)} %add.31), channel_id=1, source_target_pairs={{32,0},{96,64},{33,1},{97,65},{34,2},{98,66},{35,3},{99,67},{36,4}... | collective-permute-start | bytes 12296 | tf_op jit(solution)/shard_map/ppermute | solution.py:580
  91.9 7.7 %collective-permute-start.6 = (f32[8,128]{1,0:T(8,128)S(1)}, f32[8,128]{1,0:T(8,128)S(1)}, u32[]{:S(2)}, u32[]{:S(2)}) collective-permute-start(f32[8,128]{1,0:T(8,128)S(1)} %add.32), channel_id=1, source_target_pairs={{64,0},{65,1},{66,2},{67,3},{68,4},{69,5},{70,6},{71,7}} | collective-permute-start | bytes 12296 | tf_op jit(solution)/shard_map/ppermute | solution.py:580

commit v2 on v1

v2 whole, which is shorter than its diff:
```python
import functools

import jax
import jax.numpy as jnp
from jax import lax
from jax.experimental import pallas as pl
from jax.experimental.pallas import tpu as pltpu
from jax.sharding import PartitionSpec as P

BLOCKS_PER_SYMM = 4
NLAM = 3
TIME_STEP = 0.05
GRID_STEP = 0.5
BOUNDARY_RADIUS = 20.0
FIRST = TIME_STEP
SECOND = TIME_STEP / 2
LANES = 128
HALO_BLOCKS = 7
HALO_ROWS = 8 * HALO_BLOCKS
WINDOW = 64
F32 = jnp.float32
NT = (((1,), (1,)), ((), ()))


def params(megabytes):
    return pltpu.CompilerParams(vmem_limit_bytes=megabytes * 2**20)


def lane_index(shape):
    return lax.broadcasted_iota(jnp.int32, shape, len(shape) - 1)


def row_index(shape):
    return lax.broadcasted_iota(jnp.int32, shape, len(shape) - 2)


def square(rows):
    count = rows.shape[0]
    if count < LANES:
        rows = jnp.concatenate([rows, jnp.zeros((LANES - count, LANES), F32)], axis=0)
    return rows.T


def wide(column):
    return jnp.broadcast_to(column, (column.shape[0], LANES))


def cells_of(w_ref, part, piece, chan):
    pieces = w_ref.shape[0] // (2 * chan)
    return w_ref[pl.ds(2 * piece + part, chan, stride=2 * pieces), :]


def boundary_sum(vec_rows, surf_ref, sym, first_tile, tiles):
    chan = surf_ref.shape[0]
    sums = [jnp.zeros((chan, LANES), F32) for _ in range(2)]
    for tile in range(tiles):
        here = ((first_tile + tile) // 16).astype(F32)
        values = jnp.where(sym == here, surf_ref[:, LANES * tile : LANES * (tile + 1)], 0.0)
        for part in range(2):
            sums[part] = sums[part] + values * vec_rows(tile, part)
    return [jnp.sum(total, axis=1, keepdims=True) for total in sums]


def surface_rows(slope, surf_ref, sym, first_tile, tiles, out_ref):
    columns = [wide(column) for column in slope]
    for tile in range(tiles):
        here = ((first_tile + tile) // 16).astype(F32)
        values = jnp.where(sym == here, surf_ref[:, LANES * tile : LANES * (tile + 1)], 0.0)
        rows = [jnp.sum(values * columns[part], axis=0, keepdims=True) for part in range(2)]
        at = slice(2 * tile, 2 * tile + 2)
        out_ref[at, :] = out_ref[at, :] + jnp.concatenate(rows, axis=0)


def turn_rows(rows):
    count = rows.shape[0]
    even = row_index(rows.shape) % 2 == 0
    return jnp.where(even, pltpu.roll(rows, count - 1, 0), -pltpu.roll(rows, 1, 0))


def turn_lanes(cells):
    other = pltpu.roll(cells, WINDOW, 1)
    return jnp.where(lane_index(cells.shape) < WINDOW, other, -other)


def start_kernel(
    idx_ref, u_hbm, surf_hbm, w_hbm, energy_hbm, sym_hbm, level_hbm,
    first_ref, left_ref, right_ref, rows_ref, cols_ref, edge_ref, doubled_ref,
    wt_ref, u_ref, surf_ref, w_ref, energy_ref, sym_ref, level_ref, sems,
):
    copies = [
        pltpu.make_async_copy(source, target, sems.at[i])
        for i, (source, target) in enumerate(
            [
                (sym_hbm, sym_ref), (level_hbm, level_ref), (w_hbm, w_ref), (energy_hbm, energy_ref), (u_hbm, u_ref),
                (surf_hbm, surf_ref),
            ]
        )
    ]
    for copy in copies:
        copy.start()
    reg = idx_ref[0]
    tiles = u_ref.shape[1] // LANES
    chan = surf_ref.shape[0]
    copies[0].wait()
    copies[1].wait()
    head = jnp.zeros((1, LANES - chan), F32)
    sym_row = jnp.concatenate([sym_ref[...].astype(F32), head], axis=1)
    energy_row = jnp.concatenate([level_ref[...], head], axis=1)
    base = square(jnp.concatenate([sym_row, energy_row], axis=0))
    sym = wide(base[:chan, 0:1])
    copies[2].wait()
    for part in range(2):
        for piece in range(wt_ref.shape[1] // LANES):
            cells = cells_of(w_ref, part, piece, chan)
            cells = jnp.concatenate([cells, jnp.zeros((LANES - chan, LANES), F32)], axis=0)
            wt_ref[part, LANES * piece : LANES * (piece + 1), :] = cells.T
    copies[3].wait()
    for tile in range(tiles):
        doubled_ref[2 * tile : 2 * tile + 2, :] = jnp.broadcast_to(energy_ref[tile : tile + 1, :], (2, LANES))
    copies[4].wait()
    for tile in range(tiles):
        rows_ref[2 * tile : 2 * tile + 2, :] = u_ref[:, LANES * tile : LANES * (tile + 1)]
    copies[5].wait()
    partial = boundary_sum(
        lambda tile, part: u_ref[part : part + 1, LANES * tile : LANES * (tile + 1)],
        surf_ref, sym, reg * tiles, tiles,
    )
    lane = lane_index((chan, LANES))
    cols = jnp.where(lane == 0, sym, 0.0)
    cols = jnp.where(lane == 1, wide(base[:chan, 1:2]), cols)
    for part in range(2):
        cols = jnp.where(lane == 2 + part, wide(partial[part]), cols)
    cols = jnp.concatenate([cols, jnp.zeros((cols_ref.shape[0] - chan, LANES), F32)], axis=0)
    cols_ref[...] = cols
    back = jnp.concatenate([cols, jnp.zeros((LANES - cols.shape[0], LANES), F32)], axis=0).T
    partial_rows = back[2:4, :]
    count = wt_ref.shape[1]
    spot = lambda part, point: wt_ref[part, point : point + 1, :]
    zeros = jnp.zeros((2, LANES), F32)
    left_ref[:HALO_ROWS, :] = rows_ref[:HALO_ROWS, :]
    left_ref[HALO_ROWS:, :] = jnp.concatenate([partial_rows, spot(0, 0), spot(0, 1), spot(1, 0), spot(1, 1), zeros], axis=0)
    right_ref[:HALO_ROWS, :] = rows_ref[2 * tiles - HALO_ROWS :, :]
    right_ref[HALO_ROWS:, :] = jnp.concatenate(
        [partial_rows, spot(0, count - 2), spot(0, count - 1), spot(1, count - 2), spot(1, count - 1), zeros], axis=0
    )
    cell0 = jnp.concatenate([spot(0, 0), spot(1, 0)], axis=0)
    cell1 = jnp.concatenate([spot(0, 1), spot(1, 1)], axis=0)
    shifted = pltpu.roll(jnp.concatenate([cell0] * 4, axis=0), WINDOW, 1)[0:2]
    first_ref[0] = partial_rows + shifted
    others = first_ref.shape[0] - 1
    first_ref[1:] = jnp.broadcast_to((cell1 + shifted)[None], (others, 2, LANES))
    windows = count // WINDOW
    zero = jnp.zeros((1, LANES), F32)
    for window in range(windows):
        low, high = WINDOW * window - 1, WINDOW * (window + 1)
        edge_ref[4 * window : 4 * window + 4, :] = jnp.concatenate(
            [
                spot(0, low) if window else zero,
                spot(1, low) if window else zero,
                spot(0, high) if window < windows - 1 else zero,
                spot(1, high) if window < windows - 1 else zero,
            ],
            axis=0,
        )
    edge_ref[4 * windows : 4 * windows + 8, :] = jnp.concatenate([cell1, cell0, sym_row, energy_row, zeros], axis=0)


def add_blocks(idx_ref, pattern_hbm, blocks, mine_ref, left_ref, right_ref, out_ref, pattern_ref, states_ref, sums_ref, sem):
    count, block_len = pattern_ref.shape[1], sums_ref.shape[2]
    rows = mine_ref.shape[0] // 8
    pieces = block_len // LANES
    copy = pltpu.make_async_copy(pattern_hbm, pattern_ref, sem)
    copy.start()
    for column in range(HALO_BLOCKS):
        states_ref[column] = left_ref[8 * column : 8 * column + 8, :]
        states_ref[HALO_BLOCKS + rows + column] = right_ref[8 * column : 8 * column + 8, :]
    for column in range(rows):
        states_ref[HALO_BLOCKS + column] = mine_ref[8 * column : 8 * column + 8, :]
    sums_ref[...] = jnp.zeros(sums_ref.shape, F32)
    copy.wait()
    for i in range(count):
        row = jnp.clip(pattern_ref[0, i], 0, rows - 1)
        column = jnp.clip(pattern_ref[1, i] - idx_ref[0] * rows + HALO_BLOCKS, 0, states_ref.shape[0] - 1)
        tile = states_ref[column]
        state = jnp.concatenate([tile[2 * piece : 2 * piece + 2, :] for piece in range(pieces)], axis=1)
        lead = state.astype(jnp.bfloat16).astype(F32)
        state = jnp.concatenate([lead, state - lead, jnp.zeros((12, block_len), F32)], axis=0).astype(jnp.bfloat16)
        block = blocks(i)
        lead = block.astype(jnp.bfloat16)
        rest = (block - lead.astype(F32)).astype(jnp.bfloat16)
        product = lax.dot_general(state, lead, NT, preferred_element_type=F32)
        product = product + lax.dot_general(state, rest, NT, preferred_element_type=F32)
        sums_ref[row] = sums_ref[row] + product[:8]
    shape = (8, LANES)
    for row in range(rows):
        total = sums_ref[row]
        total = total + pltpu.roll(total, 6, 0)
        picked = jnp.zeros(shape, F32)
        for piece in range(pieces):
            values = total[:, LANES * piece : LANES * (piece + 1)]
            values = pltpu.roll(values, 2 * piece, 0) if piece else values
            picked = jnp.where(row_index(shape) // 2 == piece, values, picked)
        out_ref[8 * row : 8 * row + 8, :] = picked


def fetched(blocks_hbm, first, held_ref, sems):
    copies = [pltpu.make_async_copy(blocks_hbm.at[first + i], held_ref.at[i], sems.at[i]) for i in range(held_ref.shape[0])]
    for copy in copies:
        copy.start()

    def block(i):
        copies[i - first].wait()
        return held_ref[i - first]

    return block


def dipole_kernel(
    idx_ref, pattern_hbm, blocks_hbm, mine_ref, left_ref, right_ref, out_ref,
    pattern_ref, states_ref, sums_ref, sem, held_ref, sems,
):
    block = fetched(blocks_hbm, 0, held_ref, sems)
    add_blocks(idx_ref, pattern_hbm, block, mine_ref, left_ref, right_ref, out_ref, pattern_ref, states_ref, sums_ref, sem)


def pack_kernel(idx_ref, dipole_ref, surf_ref, cols_ref, edge_ref, w_ref, first_ref, left_ref, right_ref, message_ref, side_ref, total_ref):
    reg = idx_ref[0]
    chan = surf_ref.shape[0]
    padded = cols_ref.shape[0]
    tiles = surf_ref.shape[1] // LANES
    windows = message_ref.shape[0]
    regs = first_ref.shape[0]
    sym = wide(cols_ref[:chan, 0:1])
    received = first_ref[0]
    lane2 = lane_index((2, LANES))
    low = jnp.where(lane2 < WINDOW, received, 0.0)
    cell0 = jnp.where(lane2 < WINDOW, pltpu.roll(jnp.concatenate([received] * 4, axis=0), WINDOW, 1)[0:2], 0.0)
    cell1 = jnp.where(reg == 0, edge_ref[4 * windows : 4 * windows + 2, :], low)
    whole = jnp.zeros((2, LANES), F32)
    for source in range(regs):
        whole = whole + first_ref[source]
    whole = jnp.where((lane2 < WINDOW) & (reg == 0), whole, 0.0)
    beside = left_ref[HALO_ROWS : HALO_ROWS + 2, :] + right_ref[HALO_ROWS : HALO_ROWS + 2, :]
    side = square(
        jnp.concatenate(
            [
                cell0, cell1, beside, whole,
                left_ref[HALO_ROWS + 2 : HALO_ROWS + 4, :], right_ref[HALO_ROWS + 2 : HALO_ROWS + 4, :],
                left_ref[HALO_ROWS + 4 : HALO_ROWS + 6, :], right_ref[HALO_ROWS + 4 : HALO_ROWS + 6, :],
            ],
            axis=0,
        )
    )[:chan]
    symmetry, energy = cols_ref[:chan, 0:1], cols_ref[:chan, 1:2]
    radius = BOUNDARY_RADIUS + GRID_STEP
    potential = symmetry * (symmetry + 1.0) / (2.0 * radius * radius) + energy
    slope, start = [], []
    for part in range(2):
        here, beyond = side[:, part : part + 1], side[:, 2 + part : 3 + part]
        boundary = cols_ref[:chan, 2 + part : 3 + part] + side[:, 4 + part : 5 + part]
        slope.append(here - boundary)
        start.append(-2.0 * (beyond - 2.0 * here + boundary) + potential * here)
    lane = lane_index((chan, LANES))
    out = jnp.where((lane >= 6) & (lane < 16), side, 0.0)
    for part in range(2):
        out = jnp.where(lane == part, wide(start[part]), out)
    out = jnp.where(lane == 2, sym, out)
    out = jnp.where(lane == 3, wide(energy), out)
    side_ref[...] = jnp.concatenate([out, jnp.zeros((padded - chan, LANES), F32)], axis=0)
    total_ref[...] = dipole_ref[...]
    surface_rows(slope, surf_ref, sym, reg * tiles, tiles, total_ref)
    lines = total_ref.shape[0]
    total = total_ref[...]
    tail = jnp.concatenate([edge_ref[4 * windows + 4 : 4 * windows + 6, :], whole, jnp.zeros((6, LANES), F32)], axis=0)
    half = lane < WINDOW
    for window in range(windows):
        message_ref[window, :lines, :] = total
        one, two = (cells_of(w_ref, part, window // 2, chan) for part in range(2))
        if window % 2 == 0:
            cells = jnp.where(half, one, pltpu.roll(two, WINDOW, 1))
        else:
            cells = jnp.where(half, pltpu.roll(one, WINDOW, 1), two)
        message_ref[window, lines : lines + padded, :] = jnp.concatenate(
            [cells, jnp.zeros((padded - chan, LANES), F32)], axis=0
        )
        edges = edge_ref[4 * window : 4 * window + 4, :]
        if window == 0:
            edges = jnp.concatenate([left_ref[HALO_ROWS + 3 : HALO_ROWS + 4, :], left_ref[HALO_ROWS + 5 : HALO_ROWS + 6, :], edges[2:4]], axis=0)
        if window == windows - 1:
            edges = jnp.concatenate([edges[0:2], right_ref[HALO_ROWS + 2 : HALO_ROWS + 3, :], right_ref[HALO_ROWS + 4 : HALO_ROWS + 5, :]], axis=0)
        message_ref[window, lines + padded :, :] = jnp.concatenate([edges, cell0, tail], axis=0)


def update_kernel(idx_ref, received_ref, u_ref, energy_ref, surf_ref, cols_ref, out_ref, left_ref, right_ref):
    reg = idx_ref[0]
    lines = u_ref.shape[0]
    tiles = lines // 2
    chan = surf_ref.shape[0]
    image = energy_ref[...] * u_ref[...]
    for source in range(received_ref.shape[0]):
        image = image + received_ref[source, :lines, :]
    out_ref[...] = FIRST * turn_rows(image)
    sym = wide(cols_ref[:chan, 0:1])
    partial = boundary_sum(
        lambda tile, part: out_ref[2 * tile + part : 2 * tile + part + 1, :], surf_ref, sym, reg * tiles, tiles
    )
    lane = lane_index((chan, LANES))
    cols = jnp.where(lane == 0, wide(partial[0]), 0.0)
    cols = jnp.where(lane == 1, wide(partial[1]), cols)
    rows = jnp.concatenate([cols, jnp.zeros((LANES - chan, LANES), F32)], axis=0).T[0:8, :]
    left_ref[:HALO_ROWS, :] = out_ref[:HALO_ROWS, :]
    left_ref[HALO_ROWS:, :] = rows
    right_ref[:HALO_ROWS, :] = out_ref[lines - HALO_ROWS :, :]
    right_ref[HALO_ROWS:, :] = rows


def stencil(cells, lows, highs, potential, seams):
    count = cells.shape[1]
    lane = lane_index(cells.shape)
    below, above = pltpu.roll(cells, 1, 1), pltpu.roll(cells, count - 1, 1)
    for (first, last), low, high in zip(seams, lows, highs):
        below = jnp.where(lane == first, low, below)
        above = jnp.where(lane == last, high, above)
    return -2.0 * (above - 2.0 * cells + below) + potential * cells


def outer_kernel(count, idx_ref, received_ref, mats_ref, blocks_hbm, cross_ref, start_ref, near_ref, edge_ref, sem):
    copy = pltpu.make_async_copy(blocks_hbm.at[: near_ref.shape[0]], near_ref, sem)
    copy.start()
    reg, ch = idx_ref[0], idx_ref[1]
    groups, padded = cross_ref.shape[0], cross_ref.shape[1]
    rows = groups * padded
    lines = received_ref.shape[1] - padded - 16
    cells = received_ref[:, lines : lines + padded, :].reshape(rows, LANES)
    flipped = received_ref[:, lines + padded :, :].reshape(groups * 16, LANES).T
    extra = jnp.concatenate(
        [pltpu.roll(flipped[:padded], (LANES - 16 * group) % LANES, 1) for group in range(groups)], axis=0
    )
    first_point = reg * count + ch * WINDOW
    lane = lane_index((1, LANES))
    point = (first_point + lane % WINDOW + 1).astype(F32)
    radius = BOUNDARY_RADIUS + GRID_STEP * point
    extra_point = jnp.where(lane < 2, first_point, jnp.where(lane < 4, first_point + WINDOW + 1, 1)).astype(F32)
    extra_ratio = BOUNDARY_RADIUS / (BOUNDARY_RADIUS + GRID_STEP * extra_point)
    ratio = BOUNDARY_RADIUS / radius

    def mix(states, scale):
        totals = jnp.dot(mats_ref[...], states.astype(jnp.bfloat16), preferred_element_type=F32)
        mixed = totals[:rows] + scale * totals[rows : 2 * rows] + scale * scale * totals[2 * rows :]
        return mixed.astype(jnp.bfloat16).astype(F32)

    symmetry, energy = extra[:, 6:7], extra[:, 7:8]
    potential = symmetry * (symmetry + 1.0) / (2.0 * radius * radius) + energy
    mixed = mix(jnp.concatenate([cells, extra], axis=1), jnp.concatenate([ratio, extra_ratio], axis=1))
    main, beside = mixed[:, :LANES], mixed[:, LANES:]
    edge_ref[...] = beside
    start_ref[...] = edge_ref[pl.ds(pl.multiple_of(ch * padded, 8), padded), :]
    inner_end = (reg == 0) & (ch == 0)
    seams = ((0, WINDOW - 1), (WINDOW, 2 * WINDOW - 1))
    lows = [jnp.where(inner_end, extra[:, 8 + part : 9 + part], extra[:, part : part + 1]) for part in range(2)]
    highs = [extra[:, 2 + part : 3 + part] for part in range(2)]
    first = FIRST * turn_lanes(stencil(cells, lows, highs, potential, seams) + main)
    later = mix(first, ratio)
    cross = FIRST * turn_lanes(main)
    mixed_lows = [jnp.where(inner_end, 0.0, beside[:, part : part + 1]) for part in range(2)]
    mixed_highs = [beside[:, 2 + part : 3 + part] for part in range(2)]
    lows = [FIRST * mixed_lows[1], -FIRST * mixed_lows[0]]
    highs = [FIRST * mixed_highs[1], -FIRST * mixed_highs[0]]
    cross = cross + SECOND * turn_lanes(stencil(cross, lows, highs, potential, seams) + later)
    cross_ref[...] = cross.reshape(groups, padded, LANES)
    copy.wait()


def plain_part(regs, reg, w_ref, side_ref, plain_ref):
    chan, count = plain_ref.shape[1], plain_ref.shape[2]
    side = side_ref[...][:chan]
    symmetry, energy = side[:, 2:3], side[:, 3:4]
    lane = lane_index((1, count))
    radius = BOUNDARY_RADIUS + GRID_STEP * (reg * count + lane + 1).astype(F32)
    potential = symmetry * (symmetry + 1.0) / (2.0 * radius * radius) + energy

    def potential_at(index):
        there = BOUNDARY_RADIUS + GRID_STEP * (reg * count + index + 1).astype(F32)
        return symmetry * (symmetry + 1.0) / (2.0 * there * there) + energy

    last = reg == regs - 1
    images, lows, highs = [], [], []
    values_of = [
        jnp.concatenate([cells_of(w_ref, part, piece, chan) for piece in range(count // LANES)], axis=1) for part in range(2)
    ]
    for part in range(2):
        values = values_of[part]
        at = 8 + 4 * part
        low2, low1, high1, high2 = (side[:, at + i : at + i + 1] for i in range(4))
        low = jnp.where(reg == 0, side[:, 6 + part : 7 + part], low1)
        images.append(stencil(values, [low], [high1], potential, ((0, count - 1),)))
        under = -2.0 * (values[:, 0:1] - 2.0 * low1 + low2) + potential_at(jnp.int32(-1)) * low1
        over = -2.0 * (high2 - 2.0 * high1 + values[:, count - 1 : count]) + potential_at(jnp.int32(count)) * high1
        lows.append(jnp.where(reg == 0, 0.0, under))
        highs.append(jnp.where(last, 0.0, over))
    turned = [FIRST * images[1], -FIRST * images[0]]
    lows = [FIRST * lows[1], -FIRST * lows[0]]
    highs = [FIRST * highs[1], -FIRST * highs[0]]
    again = [stencil(turned[p], [lows[p]], [highs[p]], potential, ((0, count - 1),)) for p in range(2)]
    plain_ref[0] = values_of[0] + turned[0] + SECOND * again[1]
    plain_ref[1] = values_of[1] + turned[1] - SECOND * again[0]


def second_kernel(
    idx_ref, pattern_hbm, near_ref, blocks_hbm, mine_ref, left_ref, right_ref, own_ref, surf_ref, side_ref, start_ref, cross_ref,
    message_ref, pattern_ref, states_ref, sums_ref, sem, held_ref, sems, total_ref,
):
    near = near_ref.shape[0]
    rest = fetched(blocks_hbm, near, held_ref, sems)
    block = lambda i: near_ref[i] if i < near else rest(i)
    add_blocks(idx_ref, pattern_hbm, block, mine_ref, left_ref, right_ref, total_ref, pattern_ref, states_ref, sums_ref, sem)
    reg = idx_ref[0]
    chan = surf_ref.shape[0]
    tiles = surf_ref.shape[1] // LANES
    ends = own_ref[HALO_ROWS:, :] + left_ref[HALO_ROWS:, :] + right_ref[HALO_ROWS:, :]
    boundary = square(ends)[:chan]
    mixed = start_ref[:chan, :]
    side = side_ref[:chan, :]
    image = [side[:, part : part + 1] + mixed[:, 4 + part : 5 + part] for part in range(2)]
    slope = [FIRST * image[1] - boundary[:, 0:1], -FIRST * image[0] - boundary[:, 1:2]]
    surface_rows(slope, surf_ref, wide(side[:, 2:3]), reg * tiles, tiles, total_ref)
    lines = total_ref.shape[0]
    for group in range(message_ref.shape[0]):
        message_ref[group, :lines, :] = total_ref[...]
        message_ref[group, lines:, :] = cross_ref[group]


def finish_kernel(idx_ref, received_ref, u_ref, first_ref, energy_ref, plain_ref, ends_ref, inner_ref, outer_ref, total_ref):
    reg = idx_ref[0]
    lines = u_ref.shape[0]
    chan = plain_ref.shape[1]
    image = energy_ref[...] * first_ref[...]
    sources = received_ref.shape[0]
    for source in range(sources):
        image = image + received_ref[source, :lines, :]
    total = u_ref[...] + first_ref[...] + SECOND * turn_rows(image)
    total_ref[...] = total
    for tile in range(lines // 2):
        inner_ref[:, LANES * tile : LANES * (tile + 1)] = total_ref[2 * tile : 2 * tile + 2, :]
    columns = square(ends_ref[...])[:chan]
    lane = lane_index((chan, LANES))
    half = lane < WINDOW
    for piece in range(sources // 2):
        even = received_ref[2 * piece, lines : lines + chan, :]
        odd = received_ref[2 * piece + 1, lines : lines + chan, :]
        one = jnp.where(half, even, pltpu.roll(odd, WINDOW, 1))
        two = jnp.where(half, pltpu.roll(even, WINDOW, 1), odd)
        at = slice(LANES * piece, LANES * (piece + 1))
        one = plain_ref[0, :, at] + one
        two = plain_ref[1, :, at] + two
        if piece == 0:
            here = (lane == 0) & (reg == 0)
            one = one + jnp.where(here, -2.0 * SECOND * columns[:, 1:2], 0.0)
            two = two + jnp.where(here, 2.0 * SECOND * columns[:, 0:1], 0.0)
        for part, cells in enumerate((one, two)):
            outer_ref[pl.ds(2 * piece + part, chan, stride=sources), :] = cells


def aside_kernel(regs, idx_ref, table_ref, w_ref, side_ref, mats_ref, plain_ref):
    plain_part(regs, idx_ref[0], w_ref, side_ref, plain_ref)
    build_mats(table_ref, mats_ref)


def build_mats(table_ref, mats_ref):
    rows = mats_ref.shape[0] // NLAM
    span = table_ref.shape[1]
    entries = table_ref.shape[0] // 4
    for first in range(0, rows, LANES):
        count = min(LANES, rows - first)
        columns = square(table_ref[:, first : first + LANES])[:count]
        here = lane_index((count, span)).astype(F32)
        sums = [jnp.zeros((count, span), F32) for _ in range(NLAM)]
        for entry in range(entries):
            hit = columns[:, entry : entry + 1] == here
            order = columns[:, entries + entry : entries + entry + 1]
            weight = columns[:, 2 * entries + entry : 2 * entries + entry + 1]
            for level in range(NLAM):
                picked = jnp.where(order == level, weight, 0.0)
                sums[level] = sums[level] + jnp.where(hit, picked, 0.0)
        for level in range(NLAM):
            at = level * rows + first
            mats_ref[at : at + count, :] = sums[level][:, :rows].astype(jnp.bfloat16)


def coupling_table(source, order_list, weight, groups, chan, padded):
    place = (source // chan) * padded + source % chan
    rows = jnp.concatenate([place.T.astype(F32), order_list.T.astype(F32), weight.T, jnp.zeros_like(weight.T)], axis=0)
    rows = rows.reshape(rows.shape[0], groups, chan)
    rows = jnp.pad(rows, ((0, 0), (0, 0), (0, padded - chan))).reshape(rows.shape[0], groups * padded)
    return jnp.pad(rows, ((0, 0), (0, -rows.shape[1] % LANES)))


def shape_of(*shape):
    return jax.ShapeDtypeStruct(shape, F32)


def local(
    inner_state, energy, blocks, pattern, surface, channel_symmetry, outer_state, channel_energy,
    couple_source, couple_order, couple_weight, *, regs, groups,
):
    tile_len = inner_state.shape[1]
    lines = 2 * tile_len // LANES
    block_len = blocks.shape[1]
    block_rows = tile_len // block_len
    chan = outer_state.shape[1]
    count = outer_state.shape[2]
    padded = -(-chan // 8) * 8
    idx = jnp.stack([lax.axis_index("reg"), lax.axis_index("ch")]).astype(jnp.int32)
    smem = pl.BlockSpec(memory_space=pltpu.SMEM)
    vmem = pl.BlockSpec(memory_space=pltpu.VMEM)
    hbm = pl.BlockSpec(memory_space=pltpu.HBM)
    far = lambda array: pltpu.with_memory_space_constraint(array, pltpu.HBM)
    halo = HALO_ROWS + 8
    pieces = count // LANES
    cells = outer_state.reshape(2, chan, pieces, LANES).transpose(1, 2, 0, 3).reshape(2 * chan * pieces, LANES)
    near = blocks.shape[0] * 5 // 8
    places = far(pattern.T)

    first_msg, left, right, rows, cols, edges, energy_rows = pl.pallas_call(
        start_kernel,
        out_shape=(
            shape_of(regs, 2, LANES), shape_of(halo, LANES), shape_of(halo, LANES), shape_of(lines, LANES),
            shape_of(padded, LANES), shape_of(4 * groups + 8, LANES), shape_of(lines, LANES),
        ),
        in_specs=[smem] + [hbm] * 6,
        out_specs=(vmem,) * 7,
        scratch_shapes=[
            pltpu.VMEM((2, count, LANES), F32), pltpu.VMEM((2, tile_len), F32), pltpu.VMEM((chan, tile_len), F32),
            pltpu.VMEM(cells.shape, F32), pltpu.VMEM((lines // 2, LANES), F32),
            pltpu.VMEM((1, chan), jnp.int32), pltpu.VMEM((1, chan), F32), pltpu.SemaphoreType.DMA((6,)),
        ],
        compiler_params=params(8),
        name="start",
    )(idx, far(inner_state), far(surface), far(cells), far(energy.reshape(lines // 2, LANES)),
      far(channel_symmetry.reshape(1, chan)), far(channel_energy.reshape(1, chan)))

    firsts = lax.all_to_all(first_msg, "reg", 0, 0)
    up = [(i, i + 1) for i in range(regs - 1)]
    down = [(i + 1, i) for i in range(regs - 1)]
    from_left = lax.ppermute(right, "reg", up)
    from_right = lax.ppermute(left, "reg", down)
    block_scratch = [
        pltpu.SMEM(places.shape, jnp.int32),
        pltpu.VMEM((2 * HALO_BLOCKS + block_rows, 8, LANES), F32),
        pltpu.VMEM((block_rows, 8, block_len), F32),
        pltpu.SemaphoreType.DMA,
    ]
    held = lambda blocks: [pltpu.VMEM((blocks, block_len, block_len), F32), pltpu.SemaphoreType.DMA((blocks,))]
    dipole = pl.pallas_call(
        dipole_kernel,
        out_shape=shape_of(lines, LANES),
        in_specs=[smem, hbm, hbm] + [vmem] * 3,
        out_specs=vmem,
        scratch_shapes=block_scratch + held(blocks.shape[0]),
        compiler_params=params(16),
        name="dipole",
    )(idx, places, far(blocks), rows, from_left, from_right)

    message, side = pl.pallas_call(
        pack_kernel,
        out_shape=(shape_of(groups, lines + padded + 16, LANES), shape_of(padded, LANES)),
        in_specs=[smem] + [vmem] * 8,
        out_specs=(vmem,) * 2,
        scratch_shapes=[pltpu.VMEM((lines, LANES), F32)],
        compiler_params=params(8),
        name="pack",
    )(idx, dipole, surface, cols, edges, cells, firsts, from_left, from_right)
    received = lax.all_to_all(message, "ch", 0, 0)

    table = coupling_table(couple_source, couple_order, couple_weight, groups, chan, padded)
    mats, plain = pl.pallas_call(
        functools.partial(aside_kernel, regs),
        out_shape=(
            jax.ShapeDtypeStruct((NLAM * groups * padded, groups * padded), jnp.bfloat16), shape_of(2, chan, count),
        ),
        in_specs=[smem] + [vmem] * 3,
        out_specs=(vmem,) * 2,
        compiler_params=params(8),
        name="aside",
    )(idx, table, cells, side)
    received, mats = lax.optimization_barrier((received, mats))

    first, left, right = pl.pallas_call(
        update_kernel,
        out_shape=(shape_of(lines, LANES), shape_of(halo, LANES), shape_of(halo, LANES)),
        in_specs=[smem] + [vmem] * 5,
        out_specs=(vmem,) * 3,
        compiler_params=params(8),
        name="update",
    )(idx, received, rows, energy_rows, surface, cols)
    from_left = lax.ppermute(right, "reg", up)
    from_right = lax.ppermute(left, "reg", down)

    cross, start, near_blocks = pl.pallas_call(
        functools.partial(outer_kernel, count),
        out_shape=(shape_of(groups, padded, LANES), shape_of(padded, LANES), shape_of(near, block_len, block_len)),
        in_specs=[smem] + [vmem] * 2 + [hbm],
        out_specs=(vmem,) * 3,
        scratch_shapes=[pltpu.VMEM((groups * padded, LANES), F32), pltpu.SemaphoreType.DMA],
        compiler_params=params(12),
        name="outer",
    )(idx, received, mats, far(blocks))

    ends = left[HALO_ROWS:] + from_right[HALO_ROWS:]
    steps = [1 << i for i in range(1, regs.bit_length() - 1)]

    def gather_ends(ends, step):
        pairs = [(i + step, i) for i in range(0, regs, 2 * step)]
        return ends + lax.ppermute(ends, "reg", pairs)

    ends = gather_ends(ends, steps[0])
    cross, ends = lax.optimization_barrier((cross, ends))
    ends = gather_ends(ends, steps[1])
    message = pl.pallas_call(
        second_kernel,
        out_shape=shape_of(groups, lines + padded, LANES),
        in_specs=[smem, hbm, vmem, hbm] + [vmem] * 8,
        out_specs=vmem,
        scratch_shapes=block_scratch + held(blocks.shape[0] - near) + [pltpu.VMEM((lines, LANES), F32)],
        compiler_params=params(16),
        name="second",
    )(idx, places, near_blocks, far(blocks), first, from_left, from_right, left, surface, side, start, cross)
    message, ends = lax.optimization_barrier((message, ends))
    received = lax.all_to_all(message, "ch", 0, 0)
    for step in steps[2:]:
        ends = gather_ends(ends, step)

    inner, outer = pl.pallas_call(
        finish_kernel,
        out_shape=(shape_of(2, tile_len), shape_of(*cells.shape)),
        in_specs=[smem] + [vmem] * 6,
        out_specs=(vmem,) * 2,
        scratch_shapes=[pltpu.VMEM((lines, LANES), F32)],
        compiler_params=params(8),
        name="finish",
    )(idx, received, rows, first, energy_rows, plain, ends)
    return inner, outer.reshape(chan, pieces, 2, LANES).transpose(2, 0, 1, 3).reshape(2, chan, count)


def solution(mesh):
    return jax.shard_map(
        functools.partial(local, regs=mesh.shape["reg"], groups=mesh.shape["ch"]),
        mesh=mesh,
        in_specs=(
            P(None, "reg"),
            P("reg"),
            P(("reg", "ch"), None, None),
            P(("reg", "ch"), None),
            P("ch", "reg"),
            P("ch"),
            P(None, "ch", "reg"),
            P("ch"),
            P(),
            P(),
            P(),
        ),
        out_specs=(P(None, "reg"), P(None, "ch", "reg")),
        check_vma=False,
    )
```

time: 102 us -> 84.3 us (0.83)
  the two profiles are of different devices: /device:TPU:16 before, /device:TPU:6 now
where the time goes in v2:
time: 84.3 us; the launch traced here: 83.8 us
  starting transfers between devices  31.2 us (37%)
  Pallas kernels  25.4 us (30%)
  waiting for transfers between devices  23.4 us (28%)
  local copies, waits for them, and re-layouts  2.71 us (3%)
  between operations  0.93 us (1%)
    all_to_all x2, waiting for transfers between devices, local(): received = lax.all_to_all(message, 'ch', 0, 0)  23.4 us
    all_to_all x2, starting transfers between devices, local(): received = lax.all_to_all(message, 'ch', 0, 0)  11.2 us
    all_to_all x1, starting transfers between devices, local(): firsts = lax.all_to_all(first_msg, 'reg', 0, 0)  5.82 us
    ppermute x2, starting transfers between devices, local(): from_right = lax.ppermute(left, 'reg', down)  5.57 us
    pallas_call x1, Pallas kernels, local(): pl.pallas_call(second_kernel, out_shape=shape_of(groups, lines + padded,...  5.42 us
    pallas_call x1, Pallas kernels, local(): pl.pallas_call(dipole_kernel, out_shape=shape_of(lines, LANES), in_specs=...  5.05 us
    ppermute x2, starting transfers between devices, local(): from_left = lax.ppermute(right, 'reg', up)  4.33 us
    ppermute x3, starting transfers between devices, gather_ends(): return ends + lax.ppermute(ends, 'reg', pairs)  4.26 us
  transfers between devices with their start and end apart: 10, of which 2 were waited for; matrix products, arithmetic and copies ran while one was open for 0% of the time, Pallas kernels for 20%

profile of v2, /device:TPU:6, one launch (start us, length us, event | category | flops | bytes accessed | tf_op | source)
XLA Modules:
  0.0 83.8 jit_solution(1044533491841286506)
XLA Ops:
  0.6 0.1 pad_add_fusion.idx_ref
  0.7 0.0 copy-start
  0.7 0.0 copy-start.1
  0.7 3.5 %start.1 = (f32[16,2,128]{2,1,0:T(2,128)}, f32[64,128]{1,0:T(8,128)S(1)}, f32[64,128]{1,0:T(8,128)S(1)}, f32[120,128]{1,0:T(8,128)S(1)}, f32[56,128]{1,0:T(8,128...) custom-call(s32[2]{0:T(128)S(1)} %pad_add_fusion.idx_ref, f32[2,7680]{1,0:T(2,128)} %u_hbm.1, f32[52,7680]{1,0:T(8,128)} %surf_ref.5, ...), custom_call_target="tpu_custom_call" | custom-call | tf_op jit(solution)/shard_map/start/pallas_call | solution.py:524
  4.2 1.9 %collective-permute-start = (f32[64,128]{1,0:T(8,128)S(1)}, f32[64,128]{1,0:T(8,128)S(1)}, u32[]{:S(2)}, u32[]{:S(2)}) collective-permute-start(f32[64,128]{1,0:T(8,128)S(1)} %get-tuple-element.28), channel_id=1, source_target_pairs={{0,8},{8,16},{16,24},{24,32},{32,40},{40,48},{48,56},{56,64},{64,7... | collective-permute-start | bytes 98312 | tf_op jit(solution)/shard_map/ppermute | solution.py:545
  6.1 3.6 %collective-permute-start.1 = (f32[64,128]{1,0:T(8,128)S(1)}, f32[64,128]{1,0:T(8,128)S(1)}, u32[]{:S(2)}, u32[]{:S(2)}) collective-permute-start(f32[64,128]{1,0:T(8,128)S(1)} %get-tuple-element.29), channel_id=1, source_target_pairs={{8,0},{16,8},{24,16},{32,24},{40,32},{48,40},{56,48},{64,56},{72,6... | collective-permute-start | bytes 98312 | tf_op jit(solution)/shard_map/ppermute | solution.py:546
  9.8 5.8 %all-to-all-start = ((f32[16,2,128]{2,1,0:T(2,128)}), f32[16,2,128]{2,1,0:T(2,128)S(1)}, u32[]{:S(2)}, u32[]{:S(2)}) async-start(f32[16,2,128]{2,1,0:T(2,128)} %get-tuple-element.32), calls=%async_computation | async-start | bytes 32768 | tf_op jit(solution)/shard_map/all_to_all | solution.py:542
  15.6 0.0 collective-permute-done.left_ref
  15.6 0.0 collective-permute-done.1.right_ref
  15.6 0.0 copy-start.5
  15.6 0.0 copy-start.6
  15.6 0.0 copy-start.4
  15.6 5.0 %dipole.1.dipole_ref = f32[120,128]{1,0:T(8,128)S(1)} custom-call(s32[2]{0:T(128)S(1)} %pad_add_fusion.idx_ref, s32[2,8]{1,0:T(2,128)} %bitcast.26, f32[8,512,512]{2,1,0:T(8,128)} %blocks_hbm.5, f32[120,128]{1,0:T(8,128)S(1)} %get-tuple-element.27.mine_ref.u_ref, f32[64,128]{1,0:T(8,128)S(1)} %collective-permute-done.left_ref, ...), custom_call_target="tpu_custom_call" | custom-call | tf_op jit(solution)/shard_map/dipole/pallas_call | solution.py:554
  20.7 0.0 all-to-all-done.first_ref
  20.7 0.0 copy-done
  20.7 0.0 copy-done.1
  20.7 2.3 %pack.1 = (f32[8,192,128]{2,1,0:T(8,128)}, f32[56,128]{1,0:T(8,128)S(1)}) custom-call(s32[2]{0:T(128)S(1)} %pad_add_fusion.idx_ref, f32[120,128]{1,0:T(8,128)S(1)} %dipole.1.dipole_ref, f32[52,7680]{1,0:T(8,128)S(1)} %copy-done, f32[56,128]{1,0:T(8,128)S(1)} %get-tuple-element.30.cols_ref, f32[40,128]{1,0:T(8,128)S(1)} %get-tuple-element.31.edge_ref, ...), custom_call_target="tpu_custom_call" | custom-call | tf_op jit(solution)/shard_map/pack/pallas_call | solution.py:564
  23.0 7.6 %all-to-all-start.1 = ((f32[8,192,128]{2,1,0:T(8,128)}), f32[8,192,128]{2,1,0:T(8,128)S(1)}, u32[]{:S(2)}, u32[]{:S(2)}) async-start(f32[8,192,128]{2,1,0:T(8,128)} %get-tuple-element.33), calls=%async_computation.1 | async-start | bytes 1572864 | tf_op jit(solution)/shard_map/all_to_all | solution.py:573
  30.7 0.1 pad.13.clone
  30.8 0.0 copy-done.5
  30.8 0.0 copy-done.6
  30.8 0.0 copy-done.4
  30.8 0.1 maximum_maximum_fusion
  30.9 0.1 reshape.36
  31.0 0.1 reshape.37
  31.1 3.4 %aside.1 = (bf16[1344,448]{1,0:T(8,128)(2,1)S(1)}, f32[2,52,512]{2,1,0:T(8,128)S(1)}) custom-call(s32[2]{0:T(128)S(1)} %pad_add_fusion.idx_ref, f32[16,512]{1,0:T(8,128)S(1)} %pad.9.table_ref, f32[416,128]{1,0:T(8,128)S(1)} %bitcast.23, f32[56,128]{1,0:T(8,128)S(1)} %get-tuple-element.34.side_ref), custom_call_target="tpu_custom_call" | custom-call | tf_op jit(solution)/shard_map/aside/pallas_call | solution.py:576
  34.5 0.0 copy-start.2
  34.5 1.1 %copy-done.2 = bf16[1344,448]{1,0:T(8,128)(2,1)} copy-done((bf16[1344,448]{1,0:T(8,128)(2,1)}, bf16[1344,448]{1,0:T(8,128)(2,1)S(1)}, u32[]{:S(2)}) %copy-start.2) | copy-done | bytes 1204248
  35.6 9.8 %all-to-all-done.1.received_ref = f32[8,192,128]{2,1,0:T(8,128)S(1)} async-done(((f32[8,192,128]{2,1,0:T(8,128)}), f32[8,192,128]{2,1,0:T(8,128)S(1)}, u32[]{:S(2)}, u32[]{:S(2)}) %all-to-all-start.1) | async-done | bytes 786464 | tf_op jit(solution)/shard_map/all_to_all | solution.py:573
  45.4 1.3 %update.1 = (f32[120,128]{1,0:T(8,128)S(1)}, f32[64,128]{1,0:T(8,128)S(1)}, f32[64,128]{1,0:T(8,128)S(1)}) custom-call(s32[2]{0:T(128)S(1)} %pad_add_fusion.idx_ref, f32[8,192,128]{2,1,0:T(8,128)S(1)} %all-to-all-done.1.received_ref, f32[120,128]{1,0:T(8,128)S(1)} %get-tuple-element.27.mine_ref.u_ref, f32[120,128]{1,0:T(8,128)S(1)} %get-tuple-element.39.energy_ref, ...), custom_call_target="tpu_custom_call" | custom-call | tf_op jit(solution)/shard_map/update/pallas_call | solution.py:588
  46.7 1.9 %collective-permute-start.3 = (f32[64,128]{1,0:T(8,128)S(1)}, f32[64,128]{1,0:T(8,128)S(1)}, u32[]{:S(2)}, u32[]{:S(2)}) collective-permute-start(f32[64,128]{1,0:T(8,128)S(1)} %get-tuple-element.42.own_ref), channel_id=1, source_target_pairs={{8,0},{16,8},{24,16},{32,24},{40,32},{48,40},{56,48},{64,56},{72,6... | collective-permute-start | bytes 98312 | tf_op jit(solution)/shard_map/ppermute | solution.py:597
  48.6 2.4 %collective-permute-start.2 = (f32[64,128]{1,0:T(8,128)S(1)}, f32[64,128]{1,0:T(8,128)S(1)}, u32[]{:S(2)}, u32[]{:S(2)}) collective-permute-start(f32[64,128]{1,0:T(8,128)S(1)} %get-tuple-element.41), channel_id=1, source_target_pairs={{0,8},{8,16},{16,24},{24,32},{32,40},{40,48},{48,56},{56,64},{64,7... | collective-permute-start | bytes 98312 | tf_op jit(solution)/shard_map/ppermute | solution.py:596
  51.0 0.0 collective-permute-done.3.right_ref
  51.0 2.8 %collective-permute-start.4 = (f32[8,128]{1,0:T(8,128)S(1)}, f32[8,128]{1,0:T(8,128)S(1)}, u32[]{:S(2)}, u32[]{:S(2)}) collective-permute-start(f32[8,128]{1,0:T(8,128)S(1)} %slice_add_fusion), channel_id=1, source_target_pairs={{16,0},{48,32},{80,64},{112,96},{17,1},{49,33},{81,65},{113,97},{1... | collective-permute-start | bytes 12296 | tf_op jit(solution)/shard_map/ppermute | solution.py:614
  53.8 0.0 copy-start.3
  53.8 1.3 %copy-done.3 = bf16[1344,448]{1,0:T(8,128)(2,1)S(1)} copy-done((bf16[1344,448]{1,0:T(8,128)(2,1)S(1)}, bf16[1344,448]{1,0:T(8,128)(2,1)}, u32[]{:S(2)}) %copy-start.3) | copy-done | bytes 1204248
  55.1 3.0 %outer.1 = (f32[8,56,128]{2,1,0:T(8,128)S(1)}, f32[56,128]{1,0:T(8,128)S(1)}, f32[5,512,512]{2,1,0:T(8,128)S(1)}) custom-call(s32[2]{0:T(128)S(1)} %pad_add_fusion.idx_ref, f32[8,192,128]{2,1,0:T(8,128)S(1)} %all-to-all-done.1.received_ref, bf16[1344,448]{1,0:T(8,128)(2,1)S(1)} %copy-done.3, f32[8,512,512]{2,1,0:T(8,128)} %blocks_hbm.5), custom_call_target="tpu_custom_call" | custom-call | tf_op jit(solution)/shard_map/outer/pallas_call | solution.py:599
  58.2 0.0 collective-permute-done.4
  58.2 0.8 %collective-permute-start.5 = (f32[8,128]{1,0:T(8,128)S(1)}, f32[8,128]{1,0:T(8,128)S(1)}, u32[]{:S(2)}, u32[]{:S(2)}) collective-permute-start(f32[8,128]{1,0:T(8,128)S(1)} %add.29), channel_id=1, source_target_pairs={{32,0},{96,64},{33,1},{97,65},{34,2},{98,66},{35,3},{99,67},{36,4}... | collective-permute-start | bytes 12296 | tf_op jit(solution)/shard_map/ppermute | solution.py:614
  59.1 0.0 collective-permute-done.2.left_ref
  59.1 5.4 %second.1 = f32[8,176,128]{2,1,0:T(8,128)} custom-call(s32[2]{0:T(128)S(1)} %pad_add_fusion.idx_ref, s32[2,8]{1,0:T(2,128)} %bitcast.27, f32[5,512,512]{2,1,0:T(8,128)S(1)} %get-tuple-element.38.near_ref, f32[8,512,512]{2,1,0:T(8,128)} %blocks_hbm.5, f32[120,128]{1,0:T(8,128)S(1)} %get-tuple-element.40.mine_ref.first_ref, ...), custom_call_target="tpu_custom_call" | custom-call | tf_op jit(solution)/shard_map/second/pallas_call | solution.py:619
  64.5 0.0 collective-permute-done.5
  64.5 3.6 %all-to-all-start.2 = ((f32[8,176,128]{2,1,0:T(8,128)}), f32[8,176,128]{2,1,0:T(8,128)S(1)}, u32[]{:S(2)}, u32[]{:S(2)}) async-start(f32[8,176,128]{2,1,0:T(8,128)} %second.1), calls=%async_computation.2 | async-start | bytes 1441792 | tf_op jit(solution)/shard_map/all_to_all | solution.py:629
  68.1 0.7 collective-permute-start.6
  68.7 0.0 collective-permute-done.6
  68.8 13.6 %all-to-all-done.2.received_ref = f32[8,176,128]{2,1,0:T(8,128)S(1)} async-done(((f32[8,176,128]{2,1,0:T(8,128)}), f32[8,176,128]{2,1,0:T(8,128)S(1)}, u32[]{:S(2)}, u32[]{:S(2)}) %all-to-all-start.2) | async-done | bytes 720928 | tf_op jit(solution)/shard_map/all_to_all | solution.py:629
  82.4 1.4 %finish.1 = (f32[2,7680]{1,0:T(2,128)}, f32[416,128]{1,0:T(8,128)}) custom-call(s32[2]{0:T(128)S(1)} %pad_add_fusion.idx_ref, f32[8,176,128]{2,1,0:T(8,128)S(1)} %all-to-all-done.2.received_ref, f32[120,128]{1,0:T(8,128)S(1)} %get-tuple-element.27.mine_ref.u_ref, f32[120,128]{1,0:T(8,128)S(1)} %get-tuple-element.40.mine_ref.first_ref, ...), custom_call_target="tpu_custom_call" | custom-call | tf_op jit(solution)/shard_map/finish/pallas_call | solution.py:633
  (8 shorter events, 0.1 us)
Async XLA Ops:
  0.7 20.0 %copy-start = (f32[52,7680]{1,0:T(8,128)S(1)}, f32[52,7680]{1,0:T(8,128)}, u32[]{:S(2)}) copy-start(f32[52,7680]{1,0:T(8,128)} %surf_ref.5) | copy-start | bytes 4792324
  0.7 20.0 %copy-start.1 = (f32[2,52,512]{2,0,1:T(2,128)S(1)}, f32[2,52,512]{2,0,1:T(2,128)}, u32[]{:S(2)}) copy-start(f32[2,52,512]{2,0,1:T(2,128)} %param.17) | copy-start | bytes 638980
  4.2 11.4 %collective-permute-start = (f32[64,128]{1,0:T(8,128)S(1)}, f32[64,128]{1,0:T(8,128)S(1)}, u32[]{:S(2)}, u32[]{:S(2)}) collective-permute-start(f32[64,128]{1,0:T(8,128)S(1)} %get-tuple-element.28), channel_id=1, source_target_pairs={{0,8},{8,16},{16,24},{24,32},{32,40},{40,48},{48,56},{56,64},{64,7... | collective-permute-start | bytes 98312 | tf_op jit(solution)/shard_map/ppermute | solution.py:545
  6.1 9.5 %collective-permute-start.1 = (f32[64,128]{1,0:T(8,128)S(1)}, f32[64,128]{1,0:T(8,128)S(1)}, u32[]{:S(2)}, u32[]{:S(2)}) collective-permute-start(f32[64,128]{1,0:T(8,128)S(1)} %get-tuple-element.29), channel_id=1, source_target_pairs={{8,0},{16,8},{24,16},{32,24},{40,32},{48,40},{56,48},{64,56},{72,6... | collective-permute-start | bytes 98312 | tf_op jit(solution)/shard_map/ppermute | solution.py:546
  9.8 10.9 %all-to-all-start = ((f32[16,2,128]{2,1,0:T(2,128)}), f32[16,2,128]{2,1,0:T(2,128)S(1)}, u32[]{:S(2)}, u32[]{:S(2)}) async-start(f32[16,2,128]{2,1,0:T(2,128)} %get-tuple-element.32), calls=%async_computation | async-start | bytes 32768 | tf_op jit(solution)/shard_map/all_to_all | solution.py:542
  15.6 15.2 %copy-start.5 = (s32[416,4]{0,1:T(4,128)S(1)}, s32[416,4]{0,1:T(4,128)}, u32[]{:S(2)}) copy-start(s32[416,4]{0,1:T(4,128)} %param.19) | copy-start | bytes 19972
  15.6 15.2 %copy-start.6 = (s32[416,4]{0,1:T(4,128)S(1)}, s32[416,4]{0,1:T(4,128)}, u32[]{:S(2)}) copy-start(s32[416,4]{0,1:T(4,128)} %param.20) | copy-start | bytes 19972
  15.6 15.2 %copy-start.4 = (f32[416,4]{0,1:T(4,128)S(1)}, f32[416,4]{0,1:T(4,128)}, u32[]{:S(2)}) copy-start(f32[416,4]{0,1:T(4,128)} %param.21) | copy-start | bytes 19972
  23.0 22.4 %all-to-all-start.1 = ((f32[8,192,128]{2,1,0:T(8,128)}), f32[8,192,128]{2,1,0:T(8,128)S(1)}, u32[]{:S(2)}, u32[]{:S(2)}) async-start(f32[8,192,128]{2,1,0:T(8,128)} %get-tuple-element.33), calls=%async_computation.1 | async-start | bytes 1572864 | tf_op jit(solution)/shard_map/all_to_all | solution.py:573
  34.5 1.1 %copy-start.2 = (bf16[1344,448]{1,0:T(8,128)(2,1)}, bf16[1344,448]{1,0:T(8,128)(2,1)S(1)}, u32[]{:S(2)}) copy-start(bf16[1344,448]{1,0:T(8,128)(2,1)S(1)} %get-tuple-element.37.mats_ref) | copy-start | bytes 3612676
  46.7 4.4 %collective-permute-start.3 = (f32[64,128]{1,0:T(8,128)S(1)}, f32[64,128]{1,0:T(8,128)S(1)}, u32[]{:S(2)}, u32[]{:S(2)}) collective-permute-start(f32[64,128]{1,0:T(8,128)S(1)} %get-tuple-element.42.own_ref), channel_id=1, source_target_pairs={{8,0},{16,8},{24,16},{32,24},{40,32},{48,40},{56,48},{64,56},{72,6... | collective-permute-start | bytes 98312 | tf_op jit(solution)/shard_map/ppermute | solution.py:597
  48.6 10.5 %collective-permute-start.2 = (f32[64,128]{1,0:T(8,128)S(1)}, f32[64,128]{1,0:T(8,128)S(1)}, u32[]{:S(2)}, u32[]{:S(2)}) collective-permute-start(f32[64,128]{1,0:T(8,128)S(1)} %get-tuple-element.41), channel_id=1, source_target_pairs={{0,8},{8,16},{16,24},{24,32},{32,40},{40,48},{48,56},{56,64},{64,7... | collective-permute-start | bytes 98312 | tf_op jit(solution)/shard_map/ppermute | solution.py:596
  51.0 7.2 %collective-permute-start.4 = (f32[8,128]{1,0:T(8,128)S(1)}, f32[8,128]{1,0:T(8,128)S(1)}, u32[]{:S(2)}, u32[]{:S(2)}) collective-permute-start(f32[8,128]{1,0:T(8,128)S(1)} %slice_add_fusion), channel_id=1, source_target_pairs={{16,0},{48,32},{80,64},{112,96},{17,1},{49,33},{81,65},{113,97},{1... | collective-permute-start | bytes 12296 | tf_op jit(solution)/shard_map/ppermute | solution.py:614
  53.8 1.3 %copy-start.3 = (bf16[1344,448]{1,0:T(8,128)(2,1)S(1)}, bf16[1344,448]{1,0:T(8,128)(2,1)}, u32[]{:S(2)}) copy-start(bf16[1344,448]{1,0:T(8,128)(2,1)} %copy-done.2) | copy-start | bytes 3612676
  58.2 6.3 %collective-permute-start.5 = (f32[8,128]{1,0:T(8,128)S(1)}, f32[8,128]{1,0:T(8,128)S(1)}, u32[]{:S(2)}, u32[]{:S(2)}) collective-permute-start(f32[8,128]{1,0:T(8,128)S(1)} %add.29), channel_id=1, source_target_pairs={{32,0},{96,64},{33,1},{97,65},{34,2},{98,66},{35,3},{99,67},{36,4}... | collective-permute-start | bytes 12296 | tf_op jit(solution)/shard_map/ppermute | solution.py:614
  64.5 17.9 %all-to-all-start.2 = ((f32[8,176,128]{2,1,0:T(8,128)}), f32[8,176,128]{2,1,0:T(8,128)S(1)}, u32[]{:S(2)}, u32[]{:S(2)}) async-start(f32[8,176,128]{2,1,0:T(8,128)} %second.1), calls=%async_computation.2 | async-start | bytes 1441792 | tf_op jit(solution)/shard_map/all_to_all | solution.py:629
  68.1 0.7 collective-permute-start.6

commit v3 on v2

--- a/solution.py
+++ b/solution.py
@@ -82,17 +82,23 @@
     return jnp.where(lane_index(cells.shape) < WINDOW, other, -other)
 
 
+def sort_sides(reg, pair_ref, next_ref, left_ref, right_ref):
+    odd = reg % 2 == 1
+    left_ref[...] = jnp.where(odd, pair_ref[...], next_ref[...])
+    right_ref[...] = jnp.where(odd, next_ref[...], pair_ref[...])
+
+
 def start_kernel(
-    idx_ref, u_hbm, surf_hbm, w_hbm, energy_hbm, sym_hbm, level_hbm,
-    first_ref, left_ref, right_ref, rows_ref, cols_ref, edge_ref, doubled_ref,
-    wt_ref, u_ref, surf_ref, w_ref, energy_ref, sym_ref, level_ref, sems,
+    idx_ref, pattern_hbm, u_hbm, surf_hbm, w_hbm, energy_hbm, sym_hbm, level_hbm,
+    first_ref, pair_ref, next_ref, rows_ref, cols_ref, edge_ref, doubled_ref, ints_ref,
+    left_ref, right_ref, wt_ref, u_ref, surf_ref, w_ref, energy_ref, sym_ref, level_ref, pattern_ref, sems,
 ):
     copies = [
         pltpu.make_async_copy(source, target, sems.at[i])
         for i, (source, target) in enumerate(
             [
                 (sym_hbm, sym_ref), (level_hbm, level_ref), (w_hbm, w_ref), (energy_hbm, energy_ref), (u_hbm, u_ref),
-                (surf_hbm, surf_ref),
+                (surf_hbm, surf_ref), (pattern_hbm, pattern_ref),
             ]
         )
     ]
@@ -143,6 +149,7 @@
     right_ref[HALO_ROWS:, :] = jnp.concatenate(
         [partial_rows, spot(0, count - 2), spot(0, count - 1), spot(1, count - 2), spot(1, count - 1), zeros], axis=0
     )
+    sort_sides(reg, left_ref, right_ref, pair_ref, next_ref)
     cell0 = jnp.concatenate([spot(0, 0), spot(1, 0)], axis=0)
     cell1 = jnp.concatenate([spot(0, 1), spot(1, 1)], axis=0)
     shifted = pltpu.roll(jnp.concatenate([cell0] * 4, axis=0), WINDOW, 1)[0:2]
@@ -163,24 +170,27 @@
             axis=0,
         )
     edge_ref[4 * windows : 4 * windows + 8, :] = jnp.concatenate([cell1, cell0, sym_row, energy_row, zeros], axis=0)
-
-
-def add_blocks(idx_ref, pattern_hbm, blocks, mine_ref, left_ref, right_ref, out_ref, pattern_ref, states_ref, sums_ref, sem):
-    count, block_len = pattern_ref.shape[1], sums_ref.shape[2]
+    copies[6].wait()
+    ints_ref[0], ints_ref[1] = idx_ref[0], idx_ref[1]
+    held = pattern_ref.shape[1]
+    for i in range(held):
+        ints_ref[2 + i] = pattern_ref[0, i]
+        ints_ref[2 + held + i] = pattern_ref[1, i]
+
+
+def add_blocks(ints_ref, count, blocks, mine_ref, left_ref, right_ref, out_ref, states_ref, sums_ref):
+    block_len = sums_ref.shape[2]
     rows = mine_ref.shape[0] // 8
     pieces = block_len // LANES
-    copy = pltpu.make_async_copy(pattern_hbm, pattern_ref, sem)
-    copy.start()
     for column in range(HALO_BLOCKS):
         states_ref[column] = left_ref[8 * column : 8 * column + 8, :]
         states_ref[HALO_BLOCKS + rows + column] = right_ref[8 * column : 8 * column + 8, :]
     for column in range(rows):
         states_ref[HALO_BLOCKS + column] = mine_ref[8 * column : 8 * column + 8, :]
     sums_ref[...] = jnp.zeros(sums_ref.shape, F32)
-    copy.wait()
     for i in range(count):
-        row = jnp.clip(pattern_ref[0, i], 0, rows - 1)
-        column = jnp.clip(pattern_ref[1, i] - idx_ref[0] * rows + HALO_BLOCKS, 0, states_ref.shape[0] - 1)
+        row = jnp.clip(ints_ref[2 + i], 0, rows - 1)
+        column = jnp.clip(ints_ref[2 + count + i] - ints_ref[0] * rows + HALO_BLOCKS, 0, states_ref.shape[0] - 1)
         tile = states_ref[column]
         state = jnp.concatenate([tile[2 * piece : 2 * piece + 2, :] for piece in range(pieces)], axis=1)
         lead = state.astype(jnp.bfloat16).astype(F32)
@@ -216,19 +226,23 @@
 
 
 def dipole_kernel(
-    idx_ref, pattern_hbm, blocks_hbm, mine_ref, left_ref, right_ref, out_ref,
-    pattern_ref, states_ref, sums_ref, sem, held_ref, sems,
+    ints_ref, blocks_hbm, mine_ref, pair_ref, next_ref, out_ref, left_ref, right_ref, states_ref, sums_ref, held_ref, sems
 ):
+    sort_sides(ints_ref[0], pair_ref, next_ref, left_ref, right_ref)
     block = fetched(blocks_hbm, 0, held_ref, sems)
-    add_blocks(idx_ref, pattern_hbm, block, mine_ref, left_ref, right_ref, out_ref, pattern_ref, states_ref, sums_ref, sem)
-
-
-def pack_kernel(idx_ref, dipole_ref, surf_ref, cols_ref, edge_ref, w_ref, first_ref, left_ref, right_ref, message_ref, side_ref, total_ref):
+    add_blocks(ints_ref, held_ref.shape[0], block, mine_ref, left_ref, right_ref, out_ref, states_ref, sums_ref)
+
+
+def pack_kernel(
+    idx_ref, dipole_ref, surf_ref, cols_ref, edge_ref, w_ref, first_ref, pair_ref, next_ref,
+    message_hbm, side_ref, left_ref, right_ref, total_ref, message_ref, sems,
+):
+    sort_sides(idx_ref[0], pair_ref, next_ref, left_ref, right_ref)
     reg = idx_ref[0]
     chan = surf_ref.shape[0]
     padded = cols_ref.shape[0]
     tiles = surf_ref.shape[1] // LANES
-    windows = message_ref.shape[0]
+    windows = message_hbm.shape[0]
     regs = first_ref.shape[0]
     sym = wide(cols_ref[:chan, 0:1])
     received = first_ref[0]
@@ -267,20 +281,15 @@
     out = jnp.where(lane == 2, sym, out)
     out = jnp.where(lane == 3, wide(energy), out)
     side_ref[...] = jnp.concatenate([out, jnp.zeros((padded - chan, LANES), F32)], axis=0)
-    total_ref[...] = dipole_ref[...]
-    surface_rows(slope, surf_ref, sym, reg * tiles, tiles, total_ref)
-    lines = total_ref.shape[0]
-    total = total_ref[...]
     tail = jnp.concatenate([edge_ref[4 * windows + 4 : 4 * windows + 6, :], whole, jnp.zeros((6, LANES), F32)], axis=0)
     half = lane < WINDOW
     for window in range(windows):
-        message_ref[window, :lines, :] = total
         one, two = (cells_of(w_ref, part, window // 2, chan) for part in range(2))
         if window % 2 == 0:
             cells = jnp.where(half, one, pltpu.roll(two, WINDOW, 1))
         else:
             cells = jnp.where(half, pltpu.roll(one, WINDOW, 1), two)
-        message_ref[window, lines : lines + padded, :] = jnp.concatenate(
+        message_ref[window, :padded, :] = jnp.concatenate(
             [cells, jnp.zeros((padded - chan, LANES), F32)], axis=0
         )
         edges = edge_ref[4 * window : 4 * window + 4, :]
@@ -288,10 +297,22 @@
             edges = jnp.concatenate([left_ref[HALO_ROWS + 3 : HALO_ROWS + 4, :], left_ref[HALO_ROWS + 5 : HALO_ROWS + 6, :], edges[2:4]], axis=0)
         if window == windows - 1:
             edges = jnp.concatenate([edges[0:2], right_ref[HALO_ROWS + 2 : HALO_ROWS + 3, :], right_ref[HALO_ROWS + 4 : HALO_ROWS + 5, :]], axis=0)
-        message_ref[window, lines + padded :, :] = jnp.concatenate([edges, cell0, tail], axis=0)
-
-
-def update_kernel(idx_ref, received_ref, u_ref, energy_ref, surf_ref, cols_ref, out_ref, left_ref, right_ref):
+        message_ref[window, padded:, :] = jnp.concatenate([edges, cell0, tail], axis=0)
+    lines = total_ref.shape[0]
+    outer_copy = pltpu.make_async_copy(message_ref, message_hbm.at[:, lines:], sems.at[windows])
+    outer_copy.start()
+    total_ref[...] = dipole_ref[...]
+    surface_rows(slope, surf_ref, sym, reg * tiles, tiles, total_ref)
+    copies = [pltpu.make_async_copy(total_ref, message_hbm.at[window, :lines], sems.at[window]) for window in range(windows)]
+    for copy in copies:
+        copy.start()
+    for copy in copies + [outer_copy]:
+        copy.wait()
+
+
+def update_kernel(
+    idx_ref, received_ref, u_ref, energy_ref, surf_ref, cols_ref, out_ref, pair_ref, next_ref, left_ref, right_ref
+):
     reg = idx_ref[0]
     lines = u_ref.shape[0]
     tiles = lines // 2
@@ -312,6 +333,7 @@
     left_ref[HALO_ROWS:, :] = rows
     right_ref[:HALO_ROWS, :] = out_ref[lines - HALO_ROWS :, :]
     right_ref[HALO_ROWS:, :] = rows
+    sort_sides(reg, left_ref, right_ref, pair_ref, next_ref)
 
 
 def stencil(cells, lows, highs, potential, seams):
@@ -324,7 +346,25 @@
     return -2.0 * (above - 2.0 * cells + below) + potential * cells
 
 
-def outer_kernel(count, idx_ref, received_ref, mats_ref, blocks_hbm, cross_ref, start_ref, near_ref, edge_ref, sem):
+def mats_of(mats_hbm, mats_ref, sems):
+    rows = mats_ref.shape[0] // NLAM
+    spans = [pl.ds(level * rows, rows) for level in range(NLAM)]
+    copies = [pltpu.make_async_copy(mats_hbm.at[span], mats_ref.at[span], sems.at[i]) for i, span in enumerate(spans)]
+    for copy in copies:
+        copy.start()
+    waiting = set(range(NLAM))
+
+    def mats(level):
+        if level in waiting:
+            waiting.discard(level)
+            copies[level].wait()
+        return mats_ref[spans[level], :]
+
+    return mats
+
+
+def outer_kernel(count, idx_ref, received_ref, mats_hbm, blocks_hbm, cross_ref, start_ref, near_ref, edge_ref, mats_ref, sems, sem):
+    mats = mats_of(mats_hbm, mats_ref, sems)
     copy = pltpu.make_async_copy(blocks_hbm.at[: near_ref.shape[0]], near_ref, sem)
     copy.start()
     reg, ch = idx_ref[0], idx_ref[1]
@@ -345,8 +385,11 @@
     ratio = BOUNDARY_RADIUS / radius
 
     def mix(states, scale):
-        totals = jnp.dot(mats_ref[...], states.astype(jnp.bfloat16), preferred_element_type=F32)
-        mixed = totals[:rows] + scale * totals[rows : 2 * rows] + scale * scale * totals[2 * rows :]
+        states = states.astype(jnp.bfloat16)
+        mixed, power = 0.0, 1.0
+        for level in range(NLAM):
+            mixed = mixed + power * jnp.dot(mats(level), states, preferred_element_type=F32)
+            power = power * scale
         return mixed.astype(jnp.bfloat16).astype(F32)
 
     symmetry, energy = extra[:, 6:7], extra[:, 7:8]
@@ -407,14 +450,17 @@
 
 
 def second_kernel(
-    idx_ref, pattern_hbm, near_ref, blocks_hbm, mine_ref, left_ref, right_ref, own_ref, surf_ref, side_ref, start_ref, cross_ref,
-    message_ref, pattern_ref, states_ref, sums_ref, sem, held_ref, sems, total_ref,
+    ints_ref, near_ref, blocks_hbm, mine_ref, pair_ref, next_ref, own_ref, surf_ref, side_ref, start_ref, cross_ref,
+    message_hbm, left_ref, right_ref, states_ref, sums_ref, held_ref, sems, total_ref, out_sems,
 ):
+    sort_sides(ints_ref[0], pair_ref, next_ref, left_ref, right_ref)
     near = near_ref.shape[0]
     rest = fetched(blocks_hbm, near, held_ref, sems)
+    outer_copy = pltpu.make_async_copy(cross_ref, message_hbm.at[:, total_ref.shape[0] :], out_sems.at[message_hbm.shape[0]])
+    outer_copy.start()
     block = lambda i: near_ref[i] if i < near else rest(i)
-    add_blocks(idx_ref, pattern_hbm, block, mine_ref, left_ref, right_ref, total_ref, pattern_ref, states_ref, sums_ref, sem)
-    reg = idx_ref[0]
+    add_blocks(ints_ref, near + held_ref.shape[0], block, mine_ref, left_ref, right_ref, total_ref, states_ref, sums_ref)
+    reg = ints_ref[0]
     chan = surf_ref.shape[0]
     tiles = surf_ref.shape[1] // LANES
     ends = own_ref[HALO_ROWS:, :] + left_ref[HALO_ROWS:, :] + right_ref[HALO_ROWS:, :]
@@ -425,9 +471,12 @@
     slope = [FIRST * image[1] - boundary[:, 0:1], -FIRST * image[0] - boundary[:, 1:2]]
     surface_rows(slope, surf_ref, wide(side[:, 2:3]), reg * tiles, tiles, total_ref)
     lines = total_ref.shape[0]
-    for group in range(message_ref.shape[0]):
-        message_ref[group, :lines, :] = total_ref[...]
-        message_ref[group, lines:, :] = cross_ref[group]
+    groups = message_hbm.shape[0]
+    copies = [pltpu.make_async_copy(total_ref, message_hbm.at[group, :lines], out_sems.at[group]) for group in range(groups)]
+    for copy in copies:
+        copy.start()
+    for copy in copies + [outer_copy]:
+        copy.wait()
 
 
 def finish_kernel(idx_ref, received_ref, u_ref, first_ref, energy_ref, plain_ref, ends_ref, inner_ref, outer_ref, total_ref):
@@ -519,116 +568,120 @@
     pieces = count // LANES
     cells = outer_state.reshape(2, chan, pieces, LANES).transpose(1, 2, 0, 3).reshape(2 * chan * pieces, LANES)
     near = blocks.shape[0] * 5 // 8
-    places = far(pattern.T)
-
-    first_msg, left, right, rows, cols, edges, energy_rows = pl.pallas_call(
+
+    both = [pltpu.VMEM((halo, LANES), F32)] * 2
+    first_msg, pair, other, rows, cols, edges, energy_rows, ints = pl.pallas_call(
         start_kernel,
         out_shape=(
             shape_of(regs, 2, LANES), shape_of(halo, LANES), shape_of(halo, LANES), shape_of(lines, LANES),
             shape_of(padded, LANES), shape_of(4 * groups + 8, LANES), shape_of(lines, LANES),
+            jax.ShapeDtypeStruct((2 + pattern.size,), jnp.int32),
         ),
-        in_specs=[smem] + [hbm] * 6,
-        out_specs=(vmem,) * 7,
-        scratch_shapes=[
+        in_specs=[smem] + [hbm] * 7,
+        out_specs=(vmem,) * 7 + (smem,),
+        scratch_shapes=both
+        + [
             pltpu.VMEM((2, count, LANES), F32), pltpu.VMEM((2, tile_len), F32), pltpu.VMEM((chan, tile_len), F32),
             pltpu.VMEM(cells.shape, F32), pltpu.VMEM((lines // 2, LANES), F32),
-            pltpu.VMEM((1, chan), jnp.int32), pltpu.VMEM((1, chan), F32), pltpu.SemaphoreType.DMA((6,)),
+            pltpu.VMEM((1, chan), jnp.int32), pltpu.VMEM((1, chan), F32), pltpu.SMEM((2, blocks.shape[0]), jnp.int32),
+            pltpu.SemaphoreType.DMA((7,)),
         ],
         compiler_params=params(8),
         name="start",
-    )(idx, far(inner_state), far(surface), far(cells), far(energy.reshape(lines // 2, LANES)),
+    )(idx, far(pattern.T), far(inner_state), far(surface), far(cells), far(energy.reshape(lines // 2, LANES)),
       far(channel_symmetry.reshape(1, chan)), far(channel_energy.reshape(1, chan)))
 
     firsts = lax.all_to_all(first_msg, "reg", 0, 0)
-    up = [(i, i + 1) for i in range(regs - 1)]
-    down = [(i + 1, i) for i in range(regs - 1)]
-    from_left = lax.ppermute(right, "reg", up)
-    from_right = lax.ppermute(left, "reg", down)
+    on_chip = [(i, i ^ 1) for i in range(regs)]
+    off_chip = [move for i in range(1, regs - 1, 2) for move in ((i, i + 1), (i + 1, i))]
+    from_pair = lax.ppermute(pair, "reg", on_chip)
+    from_other = lax.ppermute(other, "reg", off_chip)
     block_scratch = [
-        pltpu.SMEM(places.shape, jnp.int32),
         pltpu.VMEM((2 * HALO_BLOCKS + block_rows, 8, LANES), F32),
         pltpu.VMEM((block_rows, 8, block_len), F32),
-        pltpu.SemaphoreType.DMA,
     ]
     held = lambda blocks: [pltpu.VMEM((blocks, block_len, block_len), F32), pltpu.SemaphoreType.DMA((blocks,))]
     dipole = pl.pallas_call(
         dipole_kernel,
         out_shape=shape_of(lines, LANES),
-        in_specs=[smem, hbm, hbm] + [vmem] * 3,
+        in_specs=[smem, hbm] + [vmem] * 3,
         out_specs=vmem,
-        scratch_shapes=block_scratch + held(blocks.shape[0]),
+        scratch_shapes=both + block_scratch + held(blocks.shape[0]),
         compiler_params=params(16),
         name="dipole",
-    )(idx, places, far(blocks), rows, from_left, from_right)
+    )(ints, far(blocks), rows, from_pair, from_other)
 
     message, side = pl.pallas_call(
         pack_kernel,
         out_shape=(shape_of(groups, lines + padded + 16, LANES), shape_of(padded, LANES)),
         in_specs=[smem] + [vmem] * 8,
-        out_specs=(vmem,) * 2,
-        scratch_shapes=[pltpu.VMEM((lines, LANES), F32)],
+        out_specs=(hbm, vmem),
+        scratch_shapes=both
+        + [
+            pltpu.VMEM((lines, LANES), F32), pltpu.VMEM((groups, padded + 16, LANES), F32),
+            pltpu.SemaphoreType.DMA((groups + 1,)),
+        ],
         compiler_params=params(8),
         name="pack",
-    )(idx, dipole, surface, cols, edges, cells, firsts, from_left, from_right)
+    )(ints, dipole, surface, cols, edges, cells, firsts, from_pair, from_other)
     received = lax.all_to_all(message, "ch", 0, 0)
 
     table = coupling_table(couple_source, couple_order, couple_weight, groups, chan, padded)
+    mats_shape = (NLAM * groups * padded, groups * padded)
     mats, plain = pl.pallas_call(
         functools.partial(aside_kernel, regs),
-        out_shape=(
-            jax.ShapeDtypeStruct((NLAM * groups * padded, groups * padded), jnp.bfloat16), shape_of(2, chan, count),
-        ),
+        out_shape=(jax.ShapeDtypeStruct(mats_shape, jnp.bfloat16), shape_of(2, chan, count)),
         in_specs=[smem] + [vmem] * 3,
         out_specs=(vmem,) * 2,
         compiler_params=params(8),
         name="aside",
-    )(idx, table, cells, side)
+    )(ints, table, cells, side)
     received, mats = lax.optimization_barrier((received, mats))
 
-    first, left, right = pl.pallas_call(
+    first, pair, other = pl.pallas_call(
         update_kernel,
         out_shape=(shape_of(lines, LANES), shape_of(halo, LANES), shape_of(halo, LANES)),
         in_specs=[smem] + [vmem] * 5,
         out_specs=(vmem,) * 3,
+        scratch_shapes=both,
         compiler_params=params(8),
         name="update",
-    )(idx, received, rows, energy_rows, surface, cols)
-    from_left = lax.ppermute(right, "reg", up)
-    from_right = lax.ppermute(left, "reg", down)
-
+    )(ints, received, rows, energy_rows, surface, cols)
+    from_pair = lax.ppermute(pair, "reg", on_chip)
+    from_other = lax.ppermute(other, "reg", off_chip)
+
+    moves = [[(2, 0), (4, 6), (10, 8), (12, 14)], [(6, 0), (14, 8)], [(8, 0)]]
+    ends = pair[HALO_ROWS:] + from_pair[HALO_ROWS:]
+    ends = ends + lax.ppermute(ends, "reg", moves[0])
     cross, start, near_blocks = pl.pallas_call(
         functools.partial(outer_kernel, count),
         out_shape=(shape_of(groups, padded, LANES), shape_of(padded, LANES), shape_of(near, block_len, block_len)),
-        in_specs=[smem] + [vmem] * 2 + [hbm],
+        in_specs=[smem, vmem, hbm, hbm],
         out_specs=(vmem,) * 3,
-        scratch_shapes=[pltpu.VMEM((groups * padded, LANES), F32), pltpu.SemaphoreType.DMA],
-        compiler_params=params(12),
+        scratch_shapes=[
+            pltpu.VMEM((groups * padded, LANES), F32), pltpu.VMEM(mats_shape, jnp.bfloat16),
+            pltpu.SemaphoreType.DMA((NLAM,)), pltpu.SemaphoreType.DMA,
+        ],
+        compiler_params=params(16),
         name="outer",
-    )(idx, received, mats, far(blocks))
-
-    ends = left[HALO_ROWS:] + from_right[HALO_ROWS:]
-    steps = [1 << i for i in range(1, regs.bit_length() - 1)]
-
-    def gather_ends(ends, step):
-        pairs = [(i + step, i) for i in range(0, regs, 2 * step)]
-        return ends + lax.ppermute(ends, "reg", pairs)
-
-    ends = gather_ends(ends, steps[0])
+    )(ints, received, far(mats), far(blocks))
     cross, ends = lax.optimization_barrier((cross, ends))
-    ends = gather_ends(ends, steps[1])
+    ends = ends + lax.ppermute(ends, "reg", moves[1])
     message = pl.pallas_call(
         second_kernel,
         out_shape=shape_of(groups, lines + padded, LANES),
-        in_specs=[smem, hbm, vmem, hbm] + [vmem] * 8,
-        out_specs=vmem,
-        scratch_shapes=block_scratch + held(blocks.shape[0] - near) + [pltpu.VMEM((lines, LANES), F32)],
+        in_specs=[smem, vmem, hbm] + [vmem] * 8,
+        out_specs=hbm,
+        scratch_shapes=both
+        + block_scratch
+        + held(blocks.shape[0] - near)
+        + [pltpu.VMEM((lines, LANES), F32), pltpu.SemaphoreType.DMA((groups + 1,))],
         compiler_params=params(16),
         name="second",
-    )(idx, places, near_blocks, far(blocks), first, from_left, from_right, left, surface, side, start, cross)
+    )(ints, near_blocks, far(blocks), first, from_pair, from_other, pair, surface, side, start, cross)
     message, ends = lax.optimization_barrier((message, ends))
     received = lax.all_to_all(message, "ch", 0, 0)
-    for step in steps[2:]:
-        ends = gather_ends(ends, step)
+    ends = ends + lax.ppermute(ends, "reg", moves[2])
 
     inner, outer = pl.pallas_call(
         finish_kernel,
@@ -638,7 +691,7 @@
         scratch_shapes=[pltpu.VMEM((lines, LANES), F32)],
         compiler_params=params(8),
         name="finish",
-    )(idx, received, rows, first, energy_rows, plain, ends)
+    )(ints, received, rows, first, energy_rows, plain, ends)
     return inner, outer.reshape(chan, pieces, 2, LANES).transpose(2, 0, 1, 3).reshape(2, chan, count)
 
 

time: 84.3 us -> 78.8 us (0.935)
  the two profiles are of different devices: /device:TPU:6 before, /device:TPU:14 now
where the time goes in v3:
time: 78.8 us; the launch traced here: 78.4 us
  starting transfers between devices  29.1 us (37%)
  Pallas kernels  25.8 us (33%)
  waiting for transfers between devices  21 us (27%)
  local copies, waits for them, and re-layouts  1.37 us (2%)
  between operations  0.91 us (1%)
    all_to_all x2, waiting for transfers between devices, local(): received = lax.all_to_all(message, 'ch', 0, 0)  20.3 us
    all_to_all x2, starting transfers between devices, local(): received = lax.all_to_all(message, 'ch', 0, 0)  10.6 us
    ppermute x2, starting transfers between devices, local(): from_other = lax.ppermute(other, 'reg', off_chip)  5.71 us
    all_to_all x1, starting transfers between devices, local(): firsts = lax.all_to_all(first_msg, 'reg', 0, 0)  5.71 us
    pallas_call x1, Pallas kernels, local(): pl.pallas_call(second_kernel, out_shape=shape_of(groups, lines + padded,...  5.28 us
    ppermute x1, starting transfers between devices, local(): ends = ends + lax.ppermute(ends, 'reg', moves[1])  5.06 us
    pallas_call x1, Pallas kernels, local(): pl.pallas_call(dipole_kernel, out_shape=shape_of(lines, LANES), in_specs=...  5.04 us
    pallas_call x1, Pallas kernels, local(): pl.pallas_call(functools.partial(outer_kernel, count), out_shape=(shape_o...  3.51 us
  transfers between devices with their start and end apart: 10, of which 3 were waited for; matrix products, arithmetic and copies ran while one was open for 0% of the time, Pallas kernels for 22%

profile of v3, /device:TPU:14, one launch (start us, length us, event | category | flops | bytes accessed | tf_op | source)
XLA Modules:
  0.0 78.4 jit_solution(15982023669174966548)
XLA Ops:
  0.6 0.1 pad_add_fusion.idx_ref
  0.7 0.0 copy-start
  0.7 0.0 copy-start.1
  0.7 3.5 %start.1 = (f32[16,2,128]{2,1,0:T(2,128)}, f32[64,128]{1,0:T(8,128)S(1)}, f32[64,128]{1,0:T(8,128)S(1)}, f32[120,128]{1,0:T(8,128)S(1)}, f32[56,128]{1,0:T(8,128...) custom-call(s32[2]{0:T(128)S(1)} %pad_add_fusion.idx_ref, s32[2,8]{1,0:T(2,128)} %bitcast.26, ...), custom_call_target="tpu_custom_call" | custom-call | tf_op jit(solution)/shard_map/start/pallas_call | solution.py:573
  4.2 0.1 collective-permute-start
  4.3 2.8 %collective-permute-start.1 = (f32[64,128]{1,0:T(8,128)S(1)}, f32[64,128]{1,0:T(8,128)S(1)}, u32[]{:S(2)}, u32[]{:S(2)}) collective-permute-start(f32[64,128]{1,0:T(8,128)S(1)} %get-tuple-element.31), channel_id=1, source_target_pairs={{8,16},{16,8},{24,32},{32,24},{40,48},{48,40},{56,64},{64,56},{72,... | collective-permute-start | bytes 98312 | tf_op jit(solution)/shard_map/ppermute | solution.py:598
  7.1 5.7 %all-to-all-start = ((f32[16,2,128]{2,1,0:T(2,128)}), f32[16,2,128]{2,1,0:T(2,128)S(1)}, u32[]{:S(2)}, u32[]{:S(2)}) async-start(f32[16,2,128]{2,1,0:T(2,128)} %get-tuple-element.34), calls=%async_computation | async-start | bytes 32768 | tf_op jit(solution)/shard_map/all_to_all | solution.py:594
  12.9 0.0 collective-permute-done.pair_ref
  12.9 0.0 collective-permute-done.1.next_ref
  12.9 0.0 copy-start.4
  12.9 0.0 copy-start.5
  12.9 0.0 copy-start.3
  12.9 5.0 %dipole.1.dipole_ref = f32[120,128]{1,0:T(8,128)S(1)} custom-call(s32[18]{0:T(128)S(1)} %get-tuple-element.28.ints_ref.idx_ref, f32[8,512,512]{2,1,0:T(8,128)} %blocks_hbm.5, f32[120,128]{1,0:T(8,128)S(1)} %get-tuple-element.29.mine_ref.u_ref, f32[64,128]{1,0:T(8,128)S(1)} %collective-permute-done.pair_ref, f32[64,128]{1,0:T(8,128)S(1)} %collective-permute-done.1.next_ref), custom_call_target="tpu_custom_call" | custom-call | tf_op jit(solution)/shard_map/dipole/pallas_call | solution.py:604
  17.9 0.0 all-to-all-done.first_ref
  18.0 0.0 copy-done
  18.0 0.0 copy-done.1
  18.0 2.4 %pack.1 = (f32[8,192,128]{2,1,0:T(8,128)}, f32[56,128]{1,0:T(8,128)S(1)}) custom-call(s32[18]{0:T(128)S(1)} %get-tuple-element.28.ints_ref.idx_ref, f32[120,128]{1,0:T(8,128)S(1)} %dipole.1.dipole_ref, f32[52,7680]{1,0:T(8,128)S(1)} %copy-done, f32[56,128]{1,0:T(8,128)S(1)} %get-tuple-element.32.cols_ref, f32[40,128]{1,0:T(8,128)S(1)} %get-tuple-element.33.edge_ref, ...), custom_call_target="tpu_custom_call" | custom-call | tf_op jit(solution)/shard_map/pack/pallas_call | solution.py:614
  20.3 7.1 %all-to-all-start.1 = ((f32[8,192,128]{2,1,0:T(8,128)}), f32[8,192,128]{2,1,0:T(8,128)S(1)}, u32[]{:S(2)}, u32[]{:S(2)}) async-start(f32[8,192,128]{2,1,0:T(8,128)} %get-tuple-element.35), calls=%async_computation.1 | async-start | bytes 1572864 | tf_op jit(solution)/shard_map/all_to_all | solution.py:627
  27.4 0.1 pad.13.clone
  27.5 0.0 copy-done.4
  27.5 0.0 copy-done.5
  27.5 0.0 copy-done.3
  27.5 0.1 maximum_maximum_fusion
  27.6 0.1 reshape.36
  27.7 0.1 reshape.37
  27.8 3.4 %aside.1 = (bf16[1344,448]{1,0:T(8,128)(2,1)S(1)}, f32[2,52,512]{2,1,0:T(8,128)S(1)}) custom-call(s32[18]{0:T(128)S(1)} %get-tuple-element.28.ints_ref.idx_ref, f32[16,512]{1,0:T(8,128)S(1)} %pad.9.table_ref, f32[416,128]{1,0:T(8,128)S(1)} %bitcast.23, f32[56,128]{1,0:T(8,128)S(1)} %get-tuple-element.36.side_ref), custom_call_target="tpu_custom_call" | custom-call | tf_op jit(solution)/shard_map/aside/pallas_call | solution.py:631
  31.2 0.0 copy-start.2
  31.2 1.1 %copy-done.2 = bf16[1344,448]{1,0:T(8,128)(2,1)} copy-done((bf16[1344,448]{1,0:T(8,128)(2,1)}, bf16[1344,448]{1,0:T(8,128)(2,1)S(1)}, u32[]{:S(2)}) %copy-start.2) | copy-done | bytes 1204248
  32.3 9.8 %all-to-all-done.1.received_ref = f32[8,192,128]{2,1,0:T(8,128)S(1)} async-done(((f32[8,192,128]{2,1,0:T(8,128)}), f32[8,192,128]{2,1,0:T(8,128)S(1)}, u32[]{:S(2)}, u32[]{:S(2)}) %all-to-all-start.1) | async-done | bytes 786464 | tf_op jit(solution)/shard_map/all_to_all | solution.py:627
  42.1 1.3 %update.1 = (f32[120,128]{1,0:T(8,128)S(1)}, f32[64,128]{1,0:T(8,128)S(1)}, f32[64,128]{1,0:T(8,128)S(1)}) custom-call(s32[18]{0:T(128)S(1)} %get-tuple-element.28.ints_ref.idx_ref, f32[8,192,128]{2,1,0:T(8,128)S(1)} %all-to-all-done.1.received_ref, f32[120,128]{1,0:T(8,128)S(1)} %get-tuple-element.29.mine_ref.u_ref, ...), custom_call_target="tpu_custom_call" | custom-call | tf_op jit(solution)/shard_map/update/pallas_call | solution.py:641
  43.4 0.0 collective-permute-start.2
  43.4 2.9 %collective-permute-start.3 = (f32[64,128]{1,0:T(8,128)S(1)}, f32[64,128]{1,0:T(8,128)S(1)}, u32[]{:S(2)}, u32[]{:S(2)}) collective-permute-start(f32[64,128]{1,0:T(8,128)S(1)} %get-tuple-element.44), channel_id=1, source_target_pairs={{8,16},{16,8},{24,32},{32,24},{40,48},{48,40},{56,64},{64,56},{72,... | collective-permute-start | bytes 98312 | tf_op jit(solution)/shard_map/ppermute | solution.py:651
  46.3 0.0 collective-permute-done.2.pair_ref
  46.3 1.3 %collective-permute-start.4 = (f32[8,128]{1,0:T(8,128)S(1)}, f32[8,128]{1,0:T(8,128)S(1)}, u32[]{:S(2)}, u32[]{:S(2)}) collective-permute-start(f32[8,128]{1,0:T(8,128)S(1)} %slice_add_fusion), channel_id=1, source_target_pairs={{16,0},{32,48},{80,64},{96,112},{17,1},{33,49},{81,65},{97,113},{1... | collective-permute-start | bytes 12296 | tf_op jit(solution)/shard_map/ppermute | solution.py:655
  47.6 3.5 %outer.1 = (f32[8,56,128]{2,1,0:T(8,128)S(1)}, f32[56,128]{1,0:T(8,128)S(1)}, f32[5,512,512]{2,1,0:T(8,128)S(1)}) custom-call(s32[18]{0:T(128)S(1)} %get-tuple-element.28.ints_ref.idx_ref, f32[8,192,128]{2,1,0:T(8,128)S(1)} %all-to-all-done.1.received_ref, bf16[1344,448]{1,0:T(8,128)(2,1)} %copy-done.2, f32[8,512,512]{2,1,0:T(8,128)} %blocks_hbm.5), custom_call_target="tpu_custom_call" | custom-call | tf_op jit(solution)/shard_map/outer/pallas_call | solution.py:656
  51.1 0.7 collective-permute-done.4
  51.8 5.1 %collective-permute-start.5 = (f32[8,128]{1,0:T(8,128)S(1)}, f32[8,128]{1,0:T(8,128)S(1)}, u32[]{:S(2)}, u32[]{:S(2)}) collective-permute-start(f32[8,128]{1,0:T(8,128)S(1)} %add.29), channel_id=1, source_target_pairs={{48,0},{112,64},{49,1},{113,65},{50,2},{114,66},{51,3},{115,67},{5... | collective-permute-start | bytes 12296 | tf_op jit(solution)/shard_map/ppermute | solution.py:669
  56.9 0.0 collective-permute-done.3.next_ref
  56.9 5.3 %second.1 = f32[8,176,128]{2,1,0:T(8,128)} custom-call(s32[18]{0:T(128)S(1)} %get-tuple-element.28.ints_ref.idx_ref, f32[5,512,512]{2,1,0:T(8,128)S(1)} %get-tuple-element.40.near_ref, f32[8,512,512]{2,1,0:T(8,128)} %blocks_hbm.5, f32[120,128]{1,0:T(8,128)S(1)} %get-tuple-element.42.mine_ref.first_ref, f32[64,128]{1,0:T(8,128)S(1)} %collective-permute-done.2.pair_ref, ...), custom_call_target="tpu_custom_call" | custom-call | tf_op jit(solution)/shard_map/second/pallas_call | solution.py:670
  62.1 0.0 collective-permute-done.5
  62.2 3.6 %all-to-all-start.2 = ((f32[8,176,128]{2,1,0:T(8,128)}), f32[8,176,128]{2,1,0:T(8,128)S(1)}, u32[]{:S(2)}, u32[]{:S(2)}) async-start(f32[8,176,128]{2,1,0:T(8,128)} %second.1), calls=%async_computation.2 | async-start | bytes 1441792 | tf_op jit(solution)/shard_map/all_to_all | solution.py:683
  65.7 0.7 collective-permute-start.6
  66.4 0.0 collective-permute-done.6
  66.4 10.5 %all-to-all-done.2.received_ref = f32[8,176,128]{2,1,0:T(8,128)S(1)} async-done(((f32[8,176,128]{2,1,0:T(8,128)}), f32[8,176,128]{2,1,0:T(8,128)S(1)}, u32[]{:S(2)}, u32[]{:S(2)}) %all-to-all-start.2) | async-done | bytes 720928 | tf_op jit(solution)/shard_map/all_to_all | solution.py:683
  76.9 1.4 %finish.1 = (f32[2,7680]{1,0:T(2,128)}, f32[416,128]{1,0:T(8,128)}) custom-call(s32[18]{0:T(128)S(1)} %get-tuple-element.28.ints_ref.idx_ref, f32[8,176,128]{2,1,0:T(8,128)S(1)} %all-to-all-done.2.received_ref, f32[120,128]{1,0:T(8,128)S(1)} %get-tuple-element.29.mine_ref.u_ref, f32[120,128]{1,0:T(8,128)S(1)} %get-tuple-element.42.mine_ref.first_ref, ...), custom_call_target="tpu_custom_call" | custom-call | tf_op jit(solution)/shard_map/finish/pallas_call | solution.py:686
  (8 shorter events, 0.1 us)
Async XLA Ops:
  0.7 17.3 %copy-start = (f32[52,7680]{1,0:T(8,128)S(1)}, f32[52,7680]{1,0:T(8,128)}, u32[]{:S(2)}) copy-start(f32[52,7680]{1,0:T(8,128)} %surf_ref.5) | copy-start | bytes 4792324
  0.7 17.3 %copy-start.1 = (f32[2,52,512]{2,0,1:T(2,128)S(1)}, f32[2,52,512]{2,0,1:T(2,128)}, u32[]{:S(2)}) copy-start(f32[2,52,512]{2,0,1:T(2,128)} %param.17) | copy-start | bytes 638980
  4.2 8.6 %collective-permute-start = (f32[64,128]{1,0:T(8,128)S(1)}, f32[64,128]{1,0:T(8,128)S(1)}, u32[]{:S(2)}, u32[]{:S(2)}) collective-permute-start(f32[64,128]{1,0:T(8,128)S(1)} %get-tuple-element.30), channel_id=1, source_target_pairs={{0,8},{8,0},{16,24},{24,16},{32,40},{40,32},{48,56},{56,48},{64,72... | collective-permute-start | bytes 98312 | tf_op jit(solution)/shard_map/ppermute | solution.py:597
  4.3 8.6 %collective-permute-start.1 = (f32[64,128]{1,0:T(8,128)S(1)}, f32[64,128]{1,0:T(8,128)S(1)}, u32[]{:S(2)}, u32[]{:S(2)}) collective-permute-start(f32[64,128]{1,0:T(8,128)S(1)} %get-tuple-element.31), channel_id=1, source_target_pairs={{8,16},{16,8},{24,32},{32,24},{40,48},{48,40},{56,64},{64,56},{72,... | collective-permute-start | bytes 98312 | tf_op jit(solution)/shard_map/ppermute | solution.py:598
  7.1 10.8 %all-to-all-start = ((f32[16,2,128]{2,1,0:T(2,128)}), f32[16,2,128]{2,1,0:T(2,128)S(1)}, u32[]{:S(2)}, u32[]{:S(2)}) async-start(f32[16,2,128]{2,1,0:T(2,128)} %get-tuple-element.34), calls=%async_computation | async-start | bytes 32768 | tf_op jit(solution)/shard_map/all_to_all | solution.py:594
  12.9 14.6 %copy-start.4 = (s32[416,4]{0,1:T(4,128)S(1)}, s32[416,4]{0,1:T(4,128)}, u32[]{:S(2)}) copy-start(s32[416,4]{0,1:T(4,128)} %param.19) | copy-start | bytes 19972
  12.9 14.6 %copy-start.5 = (s32[416,4]{0,1:T(4,128)S(1)}, s32[416,4]{0,1:T(4,128)}, u32[]{:S(2)}) copy-start(s32[416,4]{0,1:T(4,128)} %param.20) | copy-start | bytes 19972
  12.9 14.6 %copy-start.3 = (f32[416,4]{0,1:T(4,128)S(1)}, f32[416,4]{0,1:T(4,128)}, u32[]{:S(2)}) copy-start(f32[416,4]{0,1:T(4,128)} %param.21) | copy-start | bytes 19972
  20.3 21.8 %all-to-all-start.1 = ((f32[8,192,128]{2,1,0:T(8,128)}), f32[8,192,128]{2,1,0:T(8,128)S(1)}, u32[]{:S(2)}, u32[]{:S(2)}) async-start(f32[8,192,128]{2,1,0:T(8,128)} %get-tuple-element.35), calls=%async_computation.1 | async-start | bytes 1572864 | tf_op jit(solution)/shard_map/all_to_all | solution.py:627
  31.2 1.1 %copy-start.2 = (bf16[1344,448]{1,0:T(8,128)(2,1)}, bf16[1344,448]{1,0:T(8,128)(2,1)S(1)}, u32[]{:S(2)}) copy-start(bf16[1344,448]{1,0:T(8,128)(2,1)S(1)} %get-tuple-element.39.mats_hbm) | copy-start | bytes 3612676
  43.4 2.9 %collective-permute-start.2 = (f32[64,128]{1,0:T(8,128)S(1)}, f32[64,128]{1,0:T(8,128)S(1)}, u32[]{:S(2)}, u32[]{:S(2)}) collective-permute-start(f32[64,128]{1,0:T(8,128)S(1)} %get-tuple-element.43.own_ref), channel_id=1, source_target_pairs={{0,8},{8,0},{16,24},{24,16},{32,40},{40,32},{48,56},{56,48},{64,72... | collective-permute-start | bytes 98312 | tf_op jit(solution)/shard_map/ppermute | solution.py:650
  43.4 13.5 %collective-permute-start.3 = (f32[64,128]{1,0:T(8,128)S(1)}, f32[64,128]{1,0:T(8,128)S(1)}, u32[]{:S(2)}, u32[]{:S(2)}) collective-permute-start(f32[64,128]{1,0:T(8,128)S(1)} %get-tuple-element.44), channel_id=1, source_target_pairs={{8,16},{16,8},{24,32},{32,24},{40,48},{48,40},{56,64},{64,56},{72,... | collective-permute-start | bytes 98312 | tf_op jit(solution)/shard_map/ppermute | solution.py:651
  46.3 5.5 %collective-permute-start.4 = (f32[8,128]{1,0:T(8,128)S(1)}, f32[8,128]{1,0:T(8,128)S(1)}, u32[]{:S(2)}, u32[]{:S(2)}) collective-permute-start(f32[8,128]{1,0:T(8,128)S(1)} %slice_add_fusion), channel_id=1, source_target_pairs={{16,0},{32,48},{80,64},{96,112},{17,1},{33,49},{81,65},{97,113},{1... | collective-permute-start | bytes 12296 | tf_op jit(solution)/shard_map/ppermute | solution.py:655
  51.8 10.4 %collective-permute-start.5 = (f32[8,128]{1,0:T(8,128)S(1)}, f32[8,128]{1,0:T(8,128)S(1)}, u32[]{:S(2)}, u32[]{:S(2)}) collective-permute-start(f32[8,128]{1,0:T(8,128)S(1)} %add.29), channel_id=1, source_target_pairs={{48,0},{112,64},{49,1},{113,65},{50,2},{114,66},{51,3},{115,67},{5... | collective-permute-start | bytes 12296 | tf_op jit(solution)/shard_map/ppermute | solution.py:669
  62.2 14.7 %all-to-all-start.2 = ((f32[8,176,128]{2,1,0:T(8,128)}), f32[8,176,128]{2,1,0:T(8,128)S(1)}, u32[]{:S(2)}, u32[]{:S(2)}) async-start(f32[8,176,128]{2,1,0:T(8,128)} %second.1), calls=%async_computation.2 | async-start | bytes 1441792 | tf_op jit(solution)/shard_map/all_to_all | solution.py:683
  65.7 0.7 collective-permute-start.6

commit v4 on v3

--- a/solution.py
+++ b/solution.py
@@ -80,6 +80,11 @@
 def turn_lanes(cells):
     other = pltpu.roll(cells, WINDOW, 1)
     return jnp.where(lane_index(cells.shape) < WINDOW, other, -other)
+
+
+def halved(values):
+    lead = values.astype(jnp.bfloat16).astype(F32)
+    return lead, values - lead
 
 
 def sort_sides(reg, pair_ref, next_ref, left_ref, right_ref):
@@ -178,7 +183,7 @@
         ints_ref[2 + held + i] = pattern_ref[1, i]
 
 
-def add_blocks(ints_ref, count, blocks, mine_ref, left_ref, right_ref, out_ref, states_ref, sums_ref):
+def sum_blocks(ints_ref, count, blocks, mine_ref, left_ref, right_ref, states_ref, sums_ref):
     block_len = sums_ref.shape[2]
     rows = mine_ref.shape[0] // 8
     pieces = block_len // LANES
@@ -201,6 +206,10 @@
         product = lax.dot_general(state, lead, NT, preferred_element_type=F32)
         product = product + lax.dot_general(state, rest, NT, preferred_element_type=F32)
         sums_ref[row] = sums_ref[row] + product[:8]
+
+
+def fold_sums(sums_ref, out_ref):
+    rows, pieces = sums_ref.shape[0], sums_ref.shape[2] // LANES
     shape = (8, LANES)
     for row in range(rows):
         total = sums_ref[row]
@@ -210,7 +219,7 @@
             values = total[:, LANES * piece : LANES * (piece + 1)]
             values = pltpu.roll(values, 2 * piece, 0) if piece else values
             picked = jnp.where(row_index(shape) // 2 == piece, values, picked)
-        out_ref[8 * row : 8 * row + 8, :] = picked
+        out_ref[8 * row : 8 * row + 8, :] = out_ref[8 * row : 8 * row + 8, :] + picked
 
 
 def fetched(blocks_hbm, first, held_ref, sems):
@@ -230,12 +239,14 @@
 ):
     sort_sides(ints_ref[0], pair_ref, next_ref, left_ref, right_ref)
     block = fetched(blocks_hbm, 0, held_ref, sems)
-    add_blocks(ints_ref, held_ref.shape[0], block, mine_ref, left_ref, right_ref, out_ref, states_ref, sums_ref)
+    sum_blocks(ints_ref, held_ref.shape[0], block, mine_ref, left_ref, right_ref, states_ref, sums_ref)
+    out_ref[...] = jnp.zeros(out_ref.shape, F32)
+    fold_sums(sums_ref, out_ref)
 
 
 def pack_kernel(
     idx_ref, dipole_ref, surf_ref, cols_ref, edge_ref, w_ref, first_ref, pair_ref, next_ref,
-    message_hbm, side_ref, left_ref, right_ref, total_ref, message_ref, sems,
+    message_hbm, side_ref, left_ref, right_ref, total_ref, packed_ref, message_ref, sems,
 ):
     sort_sides(idx_ref[0], pair_ref, next_ref, left_ref, right_ref)
     reg = idx_ref[0]
@@ -281,7 +292,10 @@
     out = jnp.where(lane == 2, sym, out)
     out = jnp.where(lane == 3, wide(energy), out)
     side_ref[...] = jnp.concatenate([out, jnp.zeros((padded - chan, LANES), F32)], axis=0)
-    tail = jnp.concatenate([edge_ref[4 * windows + 4 : 4 * windows + 6, :], whole, jnp.zeros((6, LANES), F32)], axis=0)
+    level = halved(edge_ref[4 * windows + 5 : 4 * windows + 6, :])
+    ends = halved(whole)
+    tail = [cell0, edge_ref[4 * windows + 4 : 4 * windows + 5, :], level[0], ends[0], level[1], ends[1], jnp.zeros((3, LANES), F32)]
+    gap = jnp.zeros((WINDOW - chan, LANES), F32)
     half = lane < WINDOW
     for window in range(windows):
         one, two = (cells_of(w_ref, part, window // 2, chan) for part in range(2))
@@ -289,21 +303,19 @@
             cells = jnp.where(half, one, pltpu.roll(two, WINDOW, 1))
         else:
             cells = jnp.where(half, pltpu.roll(one, WINDOW, 1), two)
-        message_ref[window, :padded, :] = jnp.concatenate(
-            [cells, jnp.zeros((padded - chan, LANES), F32)], axis=0
-        )
         edges = edge_ref[4 * window : 4 * window + 4, :]
         if window == 0:
             edges = jnp.concatenate([left_ref[HALO_ROWS + 3 : HALO_ROWS + 4, :], left_ref[HALO_ROWS + 5 : HALO_ROWS + 6, :], edges[2:4]], axis=0)
         if window == windows - 1:
             edges = jnp.concatenate([edges[0:2], right_ref[HALO_ROWS + 2 : HALO_ROWS + 3, :], right_ref[HALO_ROWS + 4 : HALO_ROWS + 5, :]], axis=0)
-        message_ref[window, padded:, :] = jnp.concatenate([edges, cell0, tail], axis=0)
-    lines = total_ref.shape[0]
+        message_ref[window] = jnp.concatenate([cells, gap, edges] + tail, axis=0).astype(jnp.bfloat16)
+    lines = packed_ref.shape[0]
     outer_copy = pltpu.make_async_copy(message_ref, message_hbm.at[:, lines:], sems.at[windows])
     outer_copy.start()
     total_ref[...] = dipole_ref[...]
     surface_rows(slope, surf_ref, sym, reg * tiles, tiles, total_ref)
-    copies = [pltpu.make_async_copy(total_ref, message_hbm.at[window, :lines], sems.at[window]) for window in range(windows)]
+    packed_ref[...] = jnp.concatenate(halved(total_ref[...]), axis=0).astype(jnp.bfloat16)
+    copies = [pltpu.make_async_copy(packed_ref, message_hbm.at[window, :lines], sems.at[window]) for window in range(windows)]
     for copy in copies:
         copy.start()
     for copy in copies + [outer_copy]:
@@ -319,7 +331,8 @@
     chan = surf_ref.shape[0]
     image = energy_ref[...] * u_ref[...]
     for source in range(received_ref.shape[0]):
-        image = image + received_ref[source, :lines, :]
+        values = received_ref[source, : 2 * lines, :].astype(F32)
+        image = image + (values[:lines] + values[lines:])
     out_ref[...] = FIRST * turn_rows(image)
     sym = wide(cols_ref[:chan, 0:1])
     partial = boundary_sum(
@@ -364,15 +377,15 @@
 
 
 def outer_kernel(count, idx_ref, received_ref, mats_hbm, blocks_hbm, cross_ref, start_ref, near_ref, edge_ref, mats_ref, sems, sem):
-    mats = mats_of(mats_hbm, mats_ref, sems)
     copy = pltpu.make_async_copy(blocks_hbm.at[: near_ref.shape[0]], near_ref, sem)
     copy.start()
+    mats = mats_of(mats_hbm, mats_ref, sems)
     reg, ch = idx_ref[0], idx_ref[1]
     groups, padded = cross_ref.shape[0], cross_ref.shape[1]
+    lines = received_ref.shape[1] - WINDOW - 16
     rows = groups * padded
-    lines = received_ref.shape[1] - padded - 16
-    cells = received_ref[:, lines : lines + padded, :].reshape(rows, LANES)
-    flipped = received_ref[:, lines + padded :, :].reshape(groups * 16, LANES).T
+    cells = received_ref[:, lines : lines + WINDOW, :].astype(F32)[:, :padded].reshape(rows, LANES)
+    flipped = received_ref[:, lines + WINDOW :, :].astype(F32).reshape(groups * 16, LANES).T
     extra = jnp.concatenate(
         [pltpu.roll(flipped[:padded], (LANES - 16 * group) % LANES, 1) for group in range(groups)], axis=0
     )
@@ -392,7 +405,7 @@
             power = power * scale
         return mixed.astype(jnp.bfloat16).astype(F32)
 
-    symmetry, energy = extra[:, 6:7], extra[:, 7:8]
+    symmetry, energy = extra[:, 6:7], extra[:, 7:8] + extra[:, 10:11]
     potential = symmetry * (symmetry + 1.0) / (2.0 * radius * radius) + energy
     mixed = mix(jnp.concatenate([cells, extra], axis=1), jnp.concatenate([ratio, extra_ratio], axis=1))
     main, beside = mixed[:, :LANES], mixed[:, LANES:]
@@ -400,7 +413,8 @@
     start_ref[...] = edge_ref[pl.ds(pl.multiple_of(ch * padded, 8), padded), :]
     inner_end = (reg == 0) & (ch == 0)
     seams = ((0, WINDOW - 1), (WINDOW, 2 * WINDOW - 1))
-    lows = [jnp.where(inner_end, extra[:, 8 + part : 9 + part], extra[:, part : part + 1]) for part in range(2)]
+    ends = [extra[:, 8 + part : 9 + part] + extra[:, 11 + part : 12 + part] for part in range(2)]
+    lows = [jnp.where(inner_end, ends[part], extra[:, part : part + 1]) for part in range(2)]
     highs = [extra[:, 2 + part : 3 + part] for part in range(2)]
     first = FIRST * turn_lanes(stencil(cells, lows, highs, potential, seams) + main)
     later = mix(first, ratio)
@@ -459,7 +473,8 @@
     outer_copy = pltpu.make_async_copy(cross_ref, message_hbm.at[:, total_ref.shape[0] :], out_sems.at[message_hbm.shape[0]])
     outer_copy.start()
     block = lambda i: near_ref[i] if i < near else rest(i)
-    add_blocks(ints_ref, near + held_ref.shape[0], block, mine_ref, left_ref, right_ref, total_ref, states_ref, sums_ref)
+    sum_blocks(ints_ref, near + held_ref.shape[0], block, mine_ref, left_ref, right_ref, states_ref, sums_ref)
+    total_ref[...] = jnp.zeros(total_ref.shape, F32)
     reg = ints_ref[0]
     chan = surf_ref.shape[0]
     tiles = surf_ref.shape[1] // LANES
@@ -470,6 +485,7 @@
     image = [side[:, part : part + 1] + mixed[:, 4 + part : 5 + part] for part in range(2)]
     slope = [FIRST * image[1] - boundary[:, 0:1], -FIRST * image[0] - boundary[:, 1:2]]
     surface_rows(slope, surf_ref, wide(side[:, 2:3]), reg * tiles, tiles, total_ref)
+    fold_sums(sums_ref, total_ref)
     lines = total_ref.shape[0]
     groups = message_hbm.shape[0]
     copies = [pltpu.make_async_copy(total_ref, message_hbm.at[group, :lines], out_sems.at[group]) for group in range(groups)]
@@ -613,12 +629,15 @@
 
     message, side = pl.pallas_call(
         pack_kernel,
-        out_shape=(shape_of(groups, lines + padded + 16, LANES), shape_of(padded, LANES)),
+        out_shape=(
+            jax.ShapeDtypeStruct((groups, 2 * lines + WINDOW + 16, LANES), jnp.bfloat16), shape_of(padded, LANES),
+        ),
         in_specs=[smem] + [vmem] * 8,
         out_specs=(hbm, vmem),
         scratch_shapes=both
         + [
-            pltpu.VMEM((lines, LANES), F32), pltpu.VMEM((groups, padded + 16, LANES), F32),
+            pltpu.VMEM((lines, LANES), F32), pltpu.VMEM((2 * lines, LANES), jnp.bfloat16),
+            pltpu.VMEM((groups, WINDOW + 16, LANES), jnp.bfloat16),
             pltpu.SemaphoreType.DMA((groups + 1,)),
         ],
         compiler_params=params(8),
@@ -650,7 +669,7 @@
     from_pair = lax.ppermute(pair, "reg", on_chip)
     from_other = lax.ppermute(other, "reg", off_chip)
 
-    moves = [[(2, 0), (4, 6), (10, 8), (12, 14)], [(6, 0), (14, 8)], [(8, 0)]]
+    moves = [[(2, 0), (4, 6), (8, 10), (12, 14)], [(6, 0)], [(10, 0)], [(14, 0)]]
     ends = pair[HALO_ROWS:] + from_pair[HALO_ROWS:]
     ends = ends + lax.ppermute(ends, "reg", moves[0])
     cross, start, near_blocks = pl.pallas_call(
@@ -666,7 +685,6 @@
         name="outer",
     )(ints, received, far(mats), far(blocks))
     cross, ends = lax.optimization_barrier((cross, ends))
-    ends = ends + lax.ppermute(ends, "reg", moves[1])
     message = pl.pallas_call(
         second_kernel,
         out_shape=shape_of(groups, lines + padded, LANES),
@@ -681,7 +699,7 @@
     )(ints, near_blocks, far(blocks), first, from_pair, from_other, pair, surface, side, start, cross)
     message, ends = lax.optimization_barrier((message, ends))
     received = lax.all_to_all(message, "ch", 0, 0)
-    ends = ends + lax.ppermute(ends, "reg", moves[2])
+    ends = ends + sum(lax.ppermute(ends, "reg", move) for move in moves[1:])
 
     inner, outer = pl.pallas_call(
         finish_kernel,

time: 78.8 us -> 76.1 us (0.966)
  the two profiles are of different devices: /device:TPU:14 before, /device:TPU:6 now
where the time goes in v4:
time: 76.1 us; the launch traced here: 74.7 us
  starting transfers between devices  27.7 us (36%)
  Pallas kernels  25.6 us (34%)
  waiting for transfers between devices  18.9 us (25%)
  local copies, waits for them, and re-layouts  1.38 us (2%)
  between operations  0.89 us (1%)
    all_to_all x2, waiting for transfers between devices, local(): received = lax.all_to_all(message, 'ch', 0, 0)  17.8 us
    all_to_all x2, starting transfers between devices, local(): received = lax.all_to_all(message, 'ch', 0, 0)  11.2 us
    all_to_all x1, starting transfers between devices, local(): firsts = lax.all_to_all(first_msg, 'reg', 0, 0)  5.82 us
    ppermute x2, starting transfers between devices, local(): from_other = lax.ppermute(other, 'reg', off_chip)  5.71 us
    pallas_call x1, Pallas kernels, local(): pl.pallas_call(second_kernel, out_shape=shape_of(groups, lines + padded,...  5.23 us
    pallas_call x1, Pallas kernels, local(): pl.pallas_call(dipole_kernel, out_shape=shape_of(lines, LANES), in_specs=...  5.03 us
    pallas_call x1, Pallas kernels, local(): pl.pallas_call(functools.partial(outer_kernel, count), out_shape=(shape_o...  3.54 us
    pallas_call x1, Pallas kernels, local(): pl.pallas_call(start_kernel, out_shape=(shape_of(regs, 2, LANES), shape_o...  3.5 us
  transfers between devices with their start and end apart: 11, of which 4 were waited for; matrix products, arithmetic and copies ran while one was open for 0% of the time, Pallas kernels for 16%

profile of v4, /device:TPU:6, one launch (start us, length us, event | category | flops | bytes accessed | tf_op | source)
XLA Modules:
  0.0 74.7 jit_solution(15773490935555594035)
XLA Ops:
  0.6 0.1 pad_add_fusion.idx_ref
  0.7 0.0 copy-start
  0.7 0.0 copy-start.1
  0.7 3.5 %start.1 = (f32[16,2,128]{2,1,0:T(2,128)}, f32[64,128]{1,0:T(8,128)S(1)}, f32[64,128]{1,0:T(8,128)S(1)}, f32[120,128]{1,0:T(8,128)S(1)}, f32[56,128]{1,0:T(8,128...) custom-call(s32[2]{0:T(128)S(1)} %pad_add_fusion.idx_ref, s32[2,8]{1,0:T(2,128)} %bitcast.26, ...), custom_call_target="tpu_custom_call" | custom-call | tf_op jit(solution)/shard_map/start/pallas_call | solution.py:589
  4.2 0.1 collective-permute-start
  4.3 2.8 %collective-permute-start.1 = (f32[64,128]{1,0:T(8,128)S(1)}, f32[64,128]{1,0:T(8,128)S(1)}, u32[]{:S(2)}, u32[]{:S(2)}) collective-permute-start(f32[64,128]{1,0:T(8,128)S(1)} %get-tuple-element.31), channel_id=1, source_target_pairs={{8,16},{16,8},{24,32},{32,24},{40,48},{48,40},{56,64},{64,56},{72,... | collective-permute-start | bytes 98312 | tf_op jit(solution)/shard_map/ppermute | solution.py:614
  7.1 5.8 %all-to-all-start = ((f32[16,2,128]{2,1,0:T(2,128)}), f32[16,2,128]{2,1,0:T(2,128)S(1)}, u32[]{:S(2)}, u32[]{:S(2)}) async-start(f32[16,2,128]{2,1,0:T(2,128)} %get-tuple-element.34), calls=%async_computation | async-start | bytes 32768 | tf_op jit(solution)/shard_map/all_to_all | solution.py:610
  13.0 0.0 collective-permute-done.pair_ref
  13.0 0.0 collective-permute-done.1.next_ref
  13.0 0.0 copy-start.4
  13.0 0.0 copy-start.5
  13.0 0.0 copy-start.3
  13.0 5.0 %dipole.1.dipole_ref = f32[120,128]{1,0:T(8,128)S(1)} custom-call(s32[18]{0:T(128)S(1)} %get-tuple-element.28.ints_ref.idx_ref, f32[8,512,512]{2,1,0:T(8,128)} %blocks_hbm.5, f32[120,128]{1,0:T(8,128)S(1)} %get-tuple-element.29.mine_ref.u_ref, f32[64,128]{1,0:T(8,128)S(1)} %collective-permute-done.pair_ref, f32[64,128]{1,0:T(8,128)S(1)} %collective-permute-done.1.next_ref), custom_call_target="tpu_custom_call" | custom-call | tf_op jit(solution)/shard_map/dipole/pallas_call | solution.py:620
  18.1 0.0 all-to-all-done.first_ref
  18.1 0.0 copy-done
  18.1 0.0 copy-done.1
  18.1 2.2 %pack.1 = (bf16[8,320,128]{2,1,0:T(8,128)(2,1)}, f32[56,128]{1,0:T(8,128)S(1)}) custom-call(s32[18]{0:T(128)S(1)} %get-tuple-element.28.ints_ref.idx_ref, f32[120,128]{1,0:T(8,128)S(1)} %dipole.1.dipole_ref, f32[52,7680]{1,0:T(8,128)S(1)} %copy-done, f32[56,128]{1,0:T(8,128)S(1)} %get-tuple-element.32.cols_ref, f32[40,128]{1,0:T(8,128)S(1)} %get-tuple-element.33.edge_ref, ...), custom_call_target="tpu_custom_call" | custom-call | tf_op jit(solution)/shard_map/pack/pallas_call | solution.py:630
  20.3 7.7 %all-to-all-start.1 = ((bf16[8,320,128]{2,1,0:T(8,128)(2,1)}), bf16[8,320,128]{2,1,0:T(8,128)(2,1)S(1)}, u32[]{:S(2)}, u32[]{:S(2)}) async-start(bf16[8,320,128]{2,1,0:T(8,128)(2,1)} %get-tuple-element.35), calls=%async_computation.1 | async-start | bytes 1310720 | tf_op jit(solution)/shard_map/all_to_all | solution.py:646
  27.9 0.1 pad.13.clone
  28.0 0.0 copy-done.4
  28.0 0.0 copy-done.5
  28.0 0.0 copy-done.3
  28.1 0.1 maximum_maximum_fusion
  28.1 0.1 reshape.36
  28.2 0.1 reshape.37
  28.3 3.4 %aside.1 = (bf16[1344,448]{1,0:T(8,128)(2,1)S(1)}, f32[2,52,512]{2,1,0:T(8,128)S(1)}) custom-call(s32[18]{0:T(128)S(1)} %get-tuple-element.28.ints_ref.idx_ref, f32[16,512]{1,0:T(8,128)S(1)} %pad.9.table_ref, f32[416,128]{1,0:T(8,128)S(1)} %bitcast.23, f32[56,128]{1,0:T(8,128)S(1)} %get-tuple-element.36.side_ref), custom_call_target="tpu_custom_call" | custom-call | tf_op jit(solution)/shard_map/aside/pallas_call | solution.py:650
  31.8 0.0 copy-start.2
  31.8 1.1 %copy-done.2 = bf16[1344,448]{1,0:T(8,128)(2,1)} copy-done((bf16[1344,448]{1,0:T(8,128)(2,1)}, bf16[1344,448]{1,0:T(8,128)(2,1)S(1)}, u32[]{:S(2)}) %copy-start.2) | copy-done | bytes 1204248
  32.9 8.4 %all-to-all-done.1.received_ref = bf16[8,320,128]{2,1,0:T(8,128)(2,1)S(1)} async-done(((bf16[8,320,128]{2,1,0:T(8,128)(2,1)}), bf16[8,320,128]{2,1,0:T(8,128)(2,1)S(1)}, u32[]{:S(2)}, u32[]{:S(2)}) %all-to-all-start.1) | async-done | bytes 655392 | tf_op jit(solution)/shard_map/all_to_all | solution.py:646
  41.2 1.3 %update.1 = (f32[120,128]{1,0:T(8,128)S(1)}, f32[64,128]{1,0:T(8,128)S(1)}, f32[64,128]{1,0:T(8,128)S(1)}) custom-call(s32[18]{0:T(128)S(1)} %get-tuple-element.28.ints_ref.idx_ref, bf16[8,320,128]{2,1,0:T(8,128)(2,1)S(1)} %all-to-all-done.1.received_ref, f32[120,128]{1,0:T(8,128)S(1)} %get-tuple-element.29.mine_ref.u_ref, ...), custom_call_target="tpu_custom_call" | custom-call | tf_op jit(solution)/shard_map/update/pallas_call | solution.py:660
  42.5 0.0 collective-permute-start.2
  42.5 2.9 %collective-permute-start.3 = (f32[64,128]{1,0:T(8,128)S(1)}, f32[64,128]{1,0:T(8,128)S(1)}, u32[]{:S(2)}, u32[]{:S(2)}) collective-permute-start(f32[64,128]{1,0:T(8,128)S(1)} %get-tuple-element.44), channel_id=1, source_target_pairs={{8,16},{16,8},{24,32},{32,24},{40,48},{48,40},{56,64},{64,56},{72,... | collective-permute-start | bytes 98312 | tf_op jit(solution)/shard_map/ppermute | solution.py:670
  45.4 0.0 collective-permute-done.2.pair_ref
  45.4 1.5 %collective-permute-start.4 = (f32[8,128]{1,0:T(8,128)S(1)}, f32[8,128]{1,0:T(8,128)S(1)}, u32[]{:S(2)}, u32[]{:S(2)}) collective-permute-start(f32[8,128]{1,0:T(8,128)S(1)} %slice_add_fusion), channel_id=1, source_target_pairs={{16,0},{32,48},{64,80},{96,112},{17,1},{33,49},{65,81},{97,113},{1... | collective-permute-start | bytes 12296 | tf_op jit(solution)/shard_map/ppermute | solution.py:674
  46.9 3.5 %outer.1 = (f32[8,56,128]{2,1,0:T(8,128)S(1)}, f32[56,128]{1,0:T(8,128)S(1)}, f32[5,512,512]{2,1,0:T(8,128)S(1)}) custom-call(s32[18]{0:T(128)S(1)} %get-tuple-element.28.ints_ref.idx_ref, bf16[8,320,128]{2,1,0:T(8,128)(2,1)S(1)} %all-to-all-done.1.received_ref, bf16[1344,448]{1,0:T(8,128)(2,1)} %copy-done.2, f32[8,512,512]{2,1,0:T(8,128)} %blocks_hbm.5), custom_call_target="tpu_custom_call" | custom-call | tf_op jit(solution)/shard_map/outer/pallas_call | solution.py:675
  50.5 0.5 collective-permute-done.4
  50.9 0.0 collective-permute-done.3.next_ref
  50.9 5.2 %second.1 = f32[8,176,128]{2,1,0:T(8,128)} custom-call(s32[18]{0:T(128)S(1)} %get-tuple-element.28.ints_ref.idx_ref, f32[5,512,512]{2,1,0:T(8,128)S(1)} %get-tuple-element.40.near_ref, f32[8,512,512]{2,1,0:T(8,128)} %blocks_hbm.5, f32[120,128]{1,0:T(8,128)S(1)} %get-tuple-element.42.mine_ref.first_ref, f32[64,128]{1,0:T(8,128)S(1)} %collective-permute-done.2.pair_ref, ...), custom_call_target="tpu_custom_call" | custom-call | tf_op jit(solution)/shard_map/second/pallas_call | solution.py:688
  56.2 3.6 %all-to-all-start.2 = ((f32[8,176,128]{2,1,0:T(8,128)}), f32[8,176,128]{2,1,0:T(8,128)S(1)}, u32[]{:S(2)}, u32[]{:S(2)}) async-start(f32[8,176,128]{2,1,0:T(8,128)} %second.1), calls=%async_computation.2 | async-start | bytes 1441792 | tf_op jit(solution)/shard_map/all_to_all | solution.py:701
  59.7 0.7 collective-permute-start.7
  60.4 2.1 %collective-permute-start.5 = (f32[8,128]{1,0:T(8,128)S(1)}, f32[8,128]{1,0:T(8,128)S(1)}, u32[]{:S(2)}, u32[]{:S(2)}) collective-permute-start(f32[8,128]{1,0:T(8,128)S(1)} %add.32), channel_id=1, source_target_pairs={{48,0},{49,1},{50,2},{51,3},{52,4},{53,5},{54,6},{55,7}} | collective-permute-start | bytes 12296 | tf_op jit(solution)/shard_map/ppermute | solution.py:702
  62.5 0.7 collective-permute-start.6
  63.2 0.0 collective-permute-done.7
  63.2 0.6 collective-permute-done.5
  63.8 0.0 collective-permute-done.6
  63.8 9.4 %all-to-all-done.2.received_ref = f32[8,176,128]{2,1,0:T(8,128)S(1)} async-done(((f32[8,176,128]{2,1,0:T(8,128)}), f32[8,176,128]{2,1,0:T(8,128)S(1)}, u32[]{:S(2)}, u32[]{:S(2)}) %all-to-all-start.2) | async-done | bytes 720928 | tf_op jit(solution)/shard_map/all_to_all | solution.py:701
  73.2 1.4 %finish.1 = (f32[2,7680]{1,0:T(2,128)}, f32[416,128]{1,0:T(8,128)}) custom-call(s32[18]{0:T(128)S(1)} %get-tuple-element.28.ints_ref.idx_ref, f32[8,176,128]{2,1,0:T(8,128)S(1)} %all-to-all-done.2.received_ref, f32[120,128]{1,0:T(8,128)S(1)} %get-tuple-element.29.mine_ref.u_ref, f32[120,128]{1,0:T(8,128)S(1)} %get-tuple-element.42.mine_ref.first_ref, ...), custom_call_target="tpu_custom_call" | custom-call | tf_op jit(solution)/shard_map/finish/pallas_call | solution.py:704
  (7 shorter events, 0.1 us)
Async XLA Ops:
  0.7 17.4 %copy-start = (f32[52,7680]{1,0:T(8,128)S(1)}, f32[52,7680]{1,0:T(8,128)}, u32[]{:S(2)}) copy-start(f32[52,7680]{1,0:T(8,128)} %surf_ref.5) | copy-start | bytes 4792324
  0.7 17.4 %copy-start.1 = (f32[2,52,512]{2,0,1:T(2,128)S(1)}, f32[2,52,512]{2,0,1:T(2,128)}, u32[]{:S(2)}) copy-start(f32[2,52,512]{2,0,1:T(2,128)} %param.17) | copy-start | bytes 638980
  4.2 8.7 %collective-permute-start = (f32[64,128]{1,0:T(8,128)S(1)}, f32[64,128]{1,0:T(8,128)S(1)}, u32[]{:S(2)}, u32[]{:S(2)}) collective-permute-start(f32[64,128]{1,0:T(8,128)S(1)} %get-tuple-element.30), channel_id=1, source_target_pairs={{0,8},{8,0},{16,24},{24,16},{32,40},{40,32},{48,56},{56,48},{64,72... | collective-permute-start | bytes 98312 | tf_op jit(solution)/shard_map/ppermute | solution.py:613
  4.3 8.7 %collective-permute-start.1 = (f32[64,128]{1,0:T(8,128)S(1)}, f32[64,128]{1,0:T(8,128)S(1)}, u32[]{:S(2)}, u32[]{:S(2)}) collective-permute-start(f32[64,128]{1,0:T(8,128)S(1)} %get-tuple-element.31), channel_id=1, source_target_pairs={{8,16},{16,8},{24,32},{32,24},{40,48},{48,40},{56,64},{64,56},{72,... | collective-permute-start | bytes 98312 | tf_op jit(solution)/shard_map/ppermute | solution.py:614
  7.1 10.9 %all-to-all-start = ((f32[16,2,128]{2,1,0:T(2,128)}), f32[16,2,128]{2,1,0:T(2,128)S(1)}, u32[]{:S(2)}, u32[]{:S(2)}) async-start(f32[16,2,128]{2,1,0:T(2,128)} %get-tuple-element.34), calls=%async_computation | async-start | bytes 32768 | tf_op jit(solution)/shard_map/all_to_all | solution.py:610
  13.0 15.0 %copy-start.4 = (s32[416,4]{0,1:T(4,128)S(1)}, s32[416,4]{0,1:T(4,128)}, u32[]{:S(2)}) copy-start(s32[416,4]{0,1:T(4,128)} %param.19) | copy-start | bytes 19972
  13.0 15.0 %copy-start.5 = (s32[416,4]{0,1:T(4,128)S(1)}, s32[416,4]{0,1:T(4,128)}, u32[]{:S(2)}) copy-start(s32[416,4]{0,1:T(4,128)} %param.20) | copy-start | bytes 19972
  13.0 15.1 %copy-start.3 = (f32[416,4]{0,1:T(4,128)S(1)}, f32[416,4]{0,1:T(4,128)}, u32[]{:S(2)}) copy-start(f32[416,4]{0,1:T(4,128)} %param.21) | copy-start | bytes 19972
  20.3 21.0 %all-to-all-start.1 = ((bf16[8,320,128]{2,1,0:T(8,128)(2,1)}), bf16[8,320,128]{2,1,0:T(8,128)(2,1)S(1)}, u32[]{:S(2)}, u32[]{:S(2)}) async-start(bf16[8,320,128]{2,1,0:T(8,128)(2,1)} %get-tuple-element.35), calls=%async_computation.1 | async-start | bytes 1310720 | tf_op jit(solution)/shard_map/all_to_all | solution.py:646
  31.8 1.1 %copy-start.2 = (bf16[1344,448]{1,0:T(8,128)(2,1)}, bf16[1344,448]{1,0:T(8,128)(2,1)S(1)}, u32[]{:S(2)}) copy-start(bf16[1344,448]{1,0:T(8,128)(2,1)S(1)} %get-tuple-element.39.mats_hbm) | copy-start | bytes 3612676
  42.5 2.9 %collective-permute-start.2 = (f32[64,128]{1,0:T(8,128)S(1)}, f32[64,128]{1,0:T(8,128)S(1)}, u32[]{:S(2)}, u32[]{:S(2)}) collective-permute-start(f32[64,128]{1,0:T(8,128)S(1)} %get-tuple-element.43.own_ref), channel_id=1, source_target_pairs={{0,8},{8,0},{16,24},{24,16},{32,40},{40,32},{48,56},{56,48},{64,72... | collective-permute-start | bytes 98312 | tf_op jit(solution)/shard_map/ppermute | solution.py:669
  42.5 8.4 %collective-permute-start.3 = (f32[64,128]{1,0:T(8,128)S(1)}, f32[64,128]{1,0:T(8,128)S(1)}, u32[]{:S(2)}, u32[]{:S(2)}) collective-permute-start(f32[64,128]{1,0:T(8,128)S(1)} %get-tuple-element.44), channel_id=1, source_target_pairs={{8,16},{16,8},{24,32},{32,24},{40,48},{48,40},{56,64},{64,56},{72,... | collective-permute-start | bytes 98312 | tf_op jit(solution)/shard_map/ppermute | solution.py:670
  45.4 5.5 %collective-permute-start.4 = (f32[8,128]{1,0:T(8,128)S(1)}, f32[8,128]{1,0:T(8,128)S(1)}, u32[]{:S(2)}, u32[]{:S(2)}) collective-permute-start(f32[8,128]{1,0:T(8,128)S(1)} %slice_add_fusion), channel_id=1, source_target_pairs={{16,0},{32,48},{64,80},{96,112},{17,1},{33,49},{65,81},{97,113},{1... | collective-permute-start | bytes 12296 | tf_op jit(solution)/shard_map/ppermute | solution.py:674
  56.2 17.1 %all-to-all-start.2 = ((f32[8,176,128]{2,1,0:T(8,128)}), f32[8,176,128]{2,1,0:T(8,128)S(1)}, u32[]{:S(2)}, u32[]{:S(2)}) async-start(f32[8,176,128]{2,1,0:T(8,128)} %second.1), calls=%async_computation.2 | async-start | bytes 1441792 | tf_op jit(solution)/shard_map/all_to_all | solution.py:701
  59.7 3.4 %collective-permute-start.7 = (f32[8,128]{1,0:T(8,128)S(1)}, f32[8,128]{1,0:T(8,128)S(1)}, u32[]{:S(2)}, u32[]{:S(2)}) collective-permute-start(f32[8,128]{1,0:T(8,128)S(1)} %add.32), channel_id=1, source_target_pairs={{112,0},{113,1},{114,2},{115,3},{116,4},{117,5},{118,6},{119,7}} | collective-permute-start | bytes 12296 | tf_op jit(solution)/shard_map/ppermute | solution.py:702
  60.4 3.4 %collective-permute-start.5 = (f32[8,128]{1,0:T(8,128)S(1)}, f32[8,128]{1,0:T(8,128)S(1)}, u32[]{:S(2)}, u32[]{:S(2)}) collective-permute-start(f32[8,128]{1,0:T(8,128)S(1)} %add.32), channel_id=1, source_target_pairs={{48,0},{49,1},{50,2},{51,3},{52,4},{53,5},{54,6},{55,7}} | collective-permute-start | bytes 12296 | tf_op jit(solution)/shard_map/ppermute | solution.py:702
  62.5 1.3 %collective-permute-start.6 = (f32[8,128]{1,0:T(8,128)S(1)}, f32[8,128]{1,0:T(8,128)S(1)}, u32[]{:S(2)}, u32[]{:S(2)}) collective-permute-start(f32[8,128]{1,0:T(8,128)S(1)} %add.32), channel_id=1, source_target_pairs={{80,0},{81,1},{82,2},{83,3},{84,4},{85,5},{86,6},{87,7}} | collective-permute-start | bytes 12296 | tf_op jit(solution)/shard_map/ppermute | solution.py:702

commit v5 on v4

--- a/solution.py
+++ b/solution.py
@@ -18,6 +18,7 @@
 HALO_BLOCKS = 7
 HALO_ROWS = 8 * HALO_BLOCKS
 WINDOW = 64
+SURFACE_PARTS = 4
 F32 = jnp.float32
 NT = (((1,), (1,)), ((), ()))
 
@@ -50,10 +51,12 @@
     return w_ref[pl.ds(2 * piece + part, chan, stride=2 * pieces), :]
 
 
-def boundary_sum(vec_rows, surf_ref, sym, first_tile, tiles):
+def boundary_sum(vec_rows, surf_ref, sym, first_tile, tiles, waits=()):
     chan = surf_ref.shape[0]
     sums = [jnp.zeros((chan, LANES), F32) for _ in range(2)]
     for tile in range(tiles):
+        if waits and tile % (tiles // len(waits)) == 0:
+            waits[tile // (tiles // len(waits))].wait()
         here = ((first_tile + tile) // 16).astype(F32)
         values = jnp.where(sym == here, surf_ref[:, LANES * tile : LANES * (tile + 1)], 0.0)
         for part in range(2):
@@ -98,12 +101,15 @@
     first_ref, pair_ref, next_ref, rows_ref, cols_ref, edge_ref, doubled_ref, ints_ref,
     left_ref, right_ref, wt_ref, u_ref, surf_ref, w_ref, energy_ref, sym_ref, level_ref, pattern_ref, sems,
 ):
+    width = surf_ref.shape[1] // SURFACE_PARTS
+    spans = [pl.ds(part * width, width) for part in range(SURFACE_PARTS)]
     copies = [
         pltpu.make_async_copy(source, target, sems.at[i])
         for i, (source, target) in enumerate(
             [
                 (sym_hbm, sym_ref), (level_hbm, level_ref), (w_hbm, w_ref), (energy_hbm, energy_ref), (u_hbm, u_ref),
-                (surf_hbm, surf_ref), (pattern_hbm, pattern_ref),
+                (pattern_hbm, pattern_ref),
+                *((surf_hbm.at[:, span], surf_ref.at[:, span]) for span in spans),
             ]
         )
     ]
@@ -131,10 +137,9 @@
     copies[4].wait()
     for tile in range(tiles):
         rows_ref[2 * tile : 2 * tile + 2, :] = u_ref[:, LANES * tile : LANES * (tile + 1)]
-    copies[5].wait()
     partial = boundary_sum(
         lambda tile, part: u_ref[part : part + 1, LANES * tile : LANES * (tile + 1)],
-        surf_ref, sym, reg * tiles, tiles,
+        surf_ref, sym, reg * tiles, tiles, copies[6:],
     )
     lane = lane_index((chan, LANES))
     cols = jnp.where(lane == 0, sym, 0.0)
@@ -175,7 +180,7 @@
             axis=0,
         )
     edge_ref[4 * windows : 4 * windows + 8, :] = jnp.concatenate([cell1, cell0, sym_row, energy_row, zeros], axis=0)
-    copies[6].wait()
+    copies[5].wait()
     ints_ref[0], ints_ref[1] = idx_ref[0], idx_ref[1]
     held = pattern_ref.shape[1]
     for i in range(held):
@@ -600,7 +605,7 @@
             pltpu.VMEM((2, count, LANES), F32), pltpu.VMEM((2, tile_len), F32), pltpu.VMEM((chan, tile_len), F32),
             pltpu.VMEM(cells.shape, F32), pltpu.VMEM((lines // 2, LANES), F32),
             pltpu.VMEM((1, chan), jnp.int32), pltpu.VMEM((1, chan), F32), pltpu.SMEM((2, blocks.shape[0]), jnp.int32),
-            pltpu.SemaphoreType.DMA((7,)),
+            pltpu.SemaphoreType.DMA((6 + SURFACE_PARTS,)),
         ],
         compiler_params=params(8),
         name="start",

time: 76.1 us -> 75.7 us (level)
  no operation moved by 1% of the time
where the time goes in v5:
time: 75.7 us; the launch traced here: 74.4 us
  starting transfers between devices  27.7 us (37%)
  Pallas kernels  25.3 us (33%)
  waiting for transfers between devices  18.9 us (25%)
  local copies, waits for them, and re-layouts  1.38 us (2%)
  between operations  0.89 us (1%)
    all_to_all x2, waiting for transfers between devices, local(): received = lax.all_to_all(message, 'ch', 0, 0)  17.8 us
    all_to_all x2, starting transfers between devices, local(): received = lax.all_to_all(message, 'ch', 0, 0)  11.2 us
    all_to_all x1, starting transfers between devices, local(): firsts = lax.all_to_all(first_msg, 'reg', 0, 0)  5.82 us
    ppermute x2, starting transfers between devices, local(): from_other = lax.ppermute(other, 'reg', off_chip)  5.71 us
    pallas_call x1, Pallas kernels, local(): pl.pallas_call(second_kernel, out_shape=shape_of(groups, lines + padded,...  5.23 us
    pallas_call x1, Pallas kernels, local(): pl.pallas_call(dipole_kernel, out_shape=shape_of(lines, LANES), in_specs=...  5.03 us
    pallas_call x1, Pallas kernels, local(): pl.pallas_call(functools.partial(outer_kernel, count), out_shape=(shape_o...  3.54 us
    pallas_call x1, Pallas kernels, local(): pl.pallas_call(functools.partial(aside_kernel, regs), out_shape=(jax.Shap...  3.42 us
  transfers between devices with their start and end apart: 11, of which 4 were waited for; matrix products, arithmetic and copies ran while one was open for 0% of the time, Pallas kernels for 16%

profile of v5, /device:TPU:6, one launch (start us, length us, event | category | flops | bytes accessed | tf_op | source)
XLA Modules:
  0.0 74.4 jit_solution(13275691953524268301)
XLA Ops:
  0.6 0.1 pad_add_fusion.idx_ref
  0.7 0.0 copy-start
  0.7 0.0 copy-start.1
  0.7 3.1 %start.1 = (f32[16,2,128]{2,1,0:T(2,128)}, f32[64,128]{1,0:T(8,128)S(1)}, f32[64,128]{1,0:T(8,128)S(1)}, f32[120,128]{1,0:T(8,128)S(1)}, f32[56,128]{1,0:T(8,128...) custom-call(s32[2]{0:T(128)S(1)} %pad_add_fusion.idx_ref, s32[2,8]{1,0:T(2,128)} %bitcast.26, ...), custom_call_target="tpu_custom_call" | custom-call | tf_op jit(solution)/shard_map/start/pallas_call | solution.py:594
  3.9 0.1 collective-permute-start
  4.0 2.8 %collective-permute-start.1 = (f32[64,128]{1,0:T(8,128)S(1)}, f32[64,128]{1,0:T(8,128)S(1)}, u32[]{:S(2)}, u32[]{:S(2)}) collective-permute-start(f32[64,128]{1,0:T(8,128)S(1)} %get-tuple-element.31), channel_id=1, source_target_pairs={{8,16},{16,8},{24,32},{32,24},{40,48},{48,40},{56,64},{64,56},{72,... | collective-permute-start | bytes 98312 | tf_op jit(solution)/shard_map/ppermute | solution.py:619
  6.8 5.8 %all-to-all-start = ((f32[16,2,128]{2,1,0:T(2,128)}), f32[16,2,128]{2,1,0:T(2,128)S(1)}, u32[]{:S(2)}, u32[]{:S(2)}) async-start(f32[16,2,128]{2,1,0:T(2,128)} %get-tuple-element.34), calls=%async_computation | async-start | bytes 32768 | tf_op jit(solution)/shard_map/all_to_all | solution.py:615
  12.6 0.0 collective-permute-done.pair_ref
  12.6 0.0 collective-permute-done.1.next_ref
  12.6 0.0 copy-start.4
  12.6 0.0 copy-start.5
  12.7 0.0 copy-start.3
  12.7 5.0 %dipole.1.dipole_ref = f32[120,128]{1,0:T(8,128)S(1)} custom-call(s32[18]{0:T(128)S(1)} %get-tuple-element.28.ints_ref.idx_ref, f32[8,512,512]{2,1,0:T(8,128)} %blocks_hbm.5, f32[120,128]{1,0:T(8,128)S(1)} %get-tuple-element.29.mine_ref.u_ref, f32[64,128]{1,0:T(8,128)S(1)} %collective-permute-done.pair_ref, f32[64,128]{1,0:T(8,128)S(1)} %collective-permute-done.1.next_ref), custom_call_target="tpu_custom_call" | custom-call | tf_op jit(solution)/shard_map/dipole/pallas_call | solution.py:625
  17.7 0.0 all-to-all-done.first_ref
  17.7 0.0 copy-done
  17.7 0.0 copy-done.1
  17.7 2.2 %pack.1 = (bf16[8,320,128]{2,1,0:T(8,128)(2,1)}, f32[56,128]{1,0:T(8,128)S(1)}) custom-call(s32[18]{0:T(128)S(1)} %get-tuple-element.28.ints_ref.idx_ref, f32[120,128]{1,0:T(8,128)S(1)} %dipole.1.dipole_ref, f32[52,7680]{1,0:T(8,128)S(1)} %copy-done, f32[56,128]{1,0:T(8,128)S(1)} %get-tuple-element.32.cols_ref, f32[40,128]{1,0:T(8,128)S(1)} %get-tuple-element.33.edge_ref, ...), custom_call_target="tpu_custom_call" | custom-call | tf_op jit(solution)/shard_map/pack/pallas_call | solution.py:635
  19.9 7.7 %all-to-all-start.1 = ((bf16[8,320,128]{2,1,0:T(8,128)(2,1)}), bf16[8,320,128]{2,1,0:T(8,128)(2,1)S(1)}, u32[]{:S(2)}, u32[]{:S(2)}) async-start(bf16[8,320,128]{2,1,0:T(8,128)(2,1)} %get-tuple-element.35), calls=%async_computation.1 | async-start | bytes 1310720 | tf_op jit(solution)/shard_map/all_to_all | solution.py:651
  27.6 0.1 pad.13.clone
  27.7 0.0 copy-done.4
  27.7 0.0 copy-done.5
  27.7 0.0 copy-done.3
  27.7 0.1 maximum_maximum_fusion
  27.8 0.1 reshape.36
  27.9 0.1 reshape.37
  28.0 3.4 %aside.1 = (bf16[1344,448]{1,0:T(8,128)(2,1)S(1)}, f32[2,52,512]{2,1,0:T(8,128)S(1)}) custom-call(s32[18]{0:T(128)S(1)} %get-tuple-element.28.ints_ref.idx_ref, f32[16,512]{1,0:T(8,128)S(1)} %pad.9.table_ref, f32[416,128]{1,0:T(8,128)S(1)} %bitcast.23, f32[56,128]{1,0:T(8,128)S(1)} %get-tuple-element.36.side_ref), custom_call_target="tpu_custom_call" | custom-call | tf_op jit(solution)/shard_map/aside/pallas_call | solution.py:655
  31.4 0.0 copy-start.2
  31.4 1.1 %copy-done.2 = bf16[1344,448]{1,0:T(8,128)(2,1)} copy-done((bf16[1344,448]{1,0:T(8,128)(2,1)}, bf16[1344,448]{1,0:T(8,128)(2,1)S(1)}, u32[]{:S(2)}) %copy-start.2) | copy-done | bytes 1204248
  32.5 8.4 %all-to-all-done.1.received_ref = bf16[8,320,128]{2,1,0:T(8,128)(2,1)S(1)} async-done(((bf16[8,320,128]{2,1,0:T(8,128)(2,1)}), bf16[8,320,128]{2,1,0:T(8,128)(2,1)S(1)}, u32[]{:S(2)}, u32[]{:S(2)}) %all-to-all-start.1) | async-done | bytes 655392 | tf_op jit(solution)/shard_map/all_to_all | solution.py:651
  40.9 1.3 %update.1 = (f32[120,128]{1,0:T(8,128)S(1)}, f32[64,128]{1,0:T(8,128)S(1)}, f32[64,128]{1,0:T(8,128)S(1)}) custom-call(s32[18]{0:T(128)S(1)} %get-tuple-element.28.ints_ref.idx_ref, bf16[8,320,128]{2,1,0:T(8,128)(2,1)S(1)} %all-to-all-done.1.received_ref, f32[120,128]{1,0:T(8,128)S(1)} %get-tuple-element.29.mine_ref.u_ref, ...), custom_call_target="tpu_custom_call" | custom-call | tf_op jit(solution)/shard_map/update/pallas_call | solution.py:665
  42.2 0.0 collective-permute-start.2
  42.2 2.9 %collective-permute-start.3 = (f32[64,128]{1,0:T(8,128)S(1)}, f32[64,128]{1,0:T(8,128)S(1)}, u32[]{:S(2)}, u32[]{:S(2)}) collective-permute-start(f32[64,128]{1,0:T(8,128)S(1)} %get-tuple-element.44), channel_id=1, source_target_pairs={{8,16},{16,8},{24,32},{32,24},{40,48},{48,40},{56,64},{64,56},{72,... | collective-permute-start | bytes 98312 | tf_op jit(solution)/shard_map/ppermute | solution.py:675
  45.1 0.0 collective-permute-done.2.pair_ref
  45.1 1.5 %collective-permute-start.4 = (f32[8,128]{1,0:T(8,128)S(1)}, f32[8,128]{1,0:T(8,128)S(1)}, u32[]{:S(2)}, u32[]{:S(2)}) collective-permute-start(f32[8,128]{1,0:T(8,128)S(1)} %slice_add_fusion), channel_id=1, source_target_pairs={{16,0},{32,48},{64,80},{96,112},{17,1},{33,49},{65,81},{97,113},{1... | collective-permute-start | bytes 12296 | tf_op jit(solution)/shard_map/ppermute | solution.py:679
  46.6 3.5 %outer.1 = (f32[8,56,128]{2,1,0:T(8,128)S(1)}, f32[56,128]{1,0:T(8,128)S(1)}, f32[5,512,512]{2,1,0:T(8,128)S(1)}) custom-call(s32[18]{0:T(128)S(1)} %get-tuple-element.28.ints_ref.idx_ref, bf16[8,320,128]{2,1,0:T(8,128)(2,1)S(1)} %all-to-all-done.1.received_ref, bf16[1344,448]{1,0:T(8,128)(2,1)} %copy-done.2, f32[8,512,512]{2,1,0:T(8,128)} %blocks_hbm.5), custom_call_target="tpu_custom_call" | custom-call | tf_op jit(solution)/shard_map/outer/pallas_call | solution.py:680
  50.1 0.5 collective-permute-done.4
  50.6 0.0 collective-permute-done.3.next_ref
  50.6 5.2 %second.1 = f32[8,176,128]{2,1,0:T(8,128)} custom-call(s32[18]{0:T(128)S(1)} %get-tuple-element.28.ints_ref.idx_ref, f32[5,512,512]{2,1,0:T(8,128)S(1)} %get-tuple-element.40.near_ref, f32[8,512,512]{2,1,0:T(8,128)} %blocks_hbm.5, f32[120,128]{1,0:T(8,128)S(1)} %get-tuple-element.42.mine_ref.first_ref, f32[64,128]{1,0:T(8,128)S(1)} %collective-permute-done.2.pair_ref, ...), custom_call_target="tpu_custom_call" | custom-call | tf_op jit(solution)/shard_map/second/pallas_call | solution.py:693
  55.8 3.6 %all-to-all-start.2 = ((f32[8,176,128]{2,1,0:T(8,128)}), f32[8,176,128]{2,1,0:T(8,128)S(1)}, u32[]{:S(2)}, u32[]{:S(2)}) async-start(f32[8,176,128]{2,1,0:T(8,128)} %second.1), calls=%async_computation.2 | async-start | bytes 1441792 | tf_op jit(solution)/shard_map/all_to_all | solution.py:706
  59.4 0.7 collective-permute-start.7
  60.1 2.1 %collective-permute-start.5 = (f32[8,128]{1,0:T(8,128)S(1)}, f32[8,128]{1,0:T(8,128)S(1)}, u32[]{:S(2)}, u32[]{:S(2)}) collective-permute-start(f32[8,128]{1,0:T(8,128)S(1)} %add.32), channel_id=1, source_target_pairs={{48,0},{49,1},{50,2},{51,3},{52,4},{53,5},{54,6},{55,7}} | collective-permute-start | bytes 12296 | tf_op jit(solution)/shard_map/ppermute | solution.py:707
  62.2 0.7 collective-permute-start.6
  62.8 0.0 collective-permute-done.7
  62.8 0.6 collective-permute-done.5
  63.5 0.0 collective-permute-done.6
  63.5 9.4 %all-to-all-done.2.received_ref = f32[8,176,128]{2,1,0:T(8,128)S(1)} async-done(((f32[8,176,128]{2,1,0:T(8,128)}), f32[8,176,128]{2,1,0:T(8,128)S(1)}, u32[]{:S(2)}, u32[]{:S(2)}) %all-to-all-start.2) | async-done | bytes 720928 | tf_op jit(solution)/shard_map/all_to_all | solution.py:706
  72.9 1.4 %finish.1 = (f32[2,7680]{1,0:T(2,128)}, f32[416,128]{1,0:T(8,128)}) custom-call(s32[18]{0:T(128)S(1)} %get-tuple-element.28.ints_ref.idx_ref, f32[8,176,128]{2,1,0:T(8,128)S(1)} %all-to-all-done.2.received_ref, f32[120,128]{1,0:T(8,128)S(1)} %get-tuple-element.29.mine_ref.u_ref, f32[120,128]{1,0:T(8,128)S(1)} %get-tuple-element.42.mine_ref.first_ref, ...), custom_call_target="tpu_custom_call" | custom-call | tf_op jit(solution)/shard_map/finish/pallas_call | solution.py:709
  (7 shorter events, 0.1 us)
Async XLA Ops:
  0.7 17.0 %copy-start = (f32[52,7680]{1,0:T(8,128)S(1)}, f32[52,7680]{1,0:T(8,128)}, u32[]{:S(2)}) copy-start(f32[52,7680]{1,0:T(8,128)} %surf_ref.5) | copy-start | bytes 4792324
  0.7 17.0 %copy-start.1 = (f32[2,52,512]{2,0,1:T(2,128)S(1)}, f32[2,52,512]{2,0,1:T(2,128)}, u32[]{:S(2)}) copy-start(f32[2,52,512]{2,0,1:T(2,128)} %param.17) | copy-start | bytes 638980
  3.9 8.7 %collective-permute-start = (f32[64,128]{1,0:T(8,128)S(1)}, f32[64,128]{1,0:T(8,128)S(1)}, u32[]{:S(2)}, u32[]{:S(2)}) collective-permute-start(f32[64,128]{1,0:T(8,128)S(1)} %get-tuple-element.30), channel_id=1, source_target_pairs={{0,8},{8,0},{16,24},{24,16},{32,40},{40,32},{48,56},{56,48},{64,72... | collective-permute-start | bytes 98312 | tf_op jit(solution)/shard_map/ppermute | solution.py:618
  4.0 8.7 %collective-permute-start.1 = (f32[64,128]{1,0:T(8,128)S(1)}, f32[64,128]{1,0:T(8,128)S(1)}, u32[]{:S(2)}, u32[]{:S(2)}) collective-permute-start(f32[64,128]{1,0:T(8,128)S(1)} %get-tuple-element.31), channel_id=1, source_target_pairs={{8,16},{16,8},{24,32},{32,24},{40,48},{48,40},{56,64},{64,56},{72,... | collective-permute-start | bytes 98312 | tf_op jit(solution)/shard_map/ppermute | solution.py:619
  6.8 10.9 %all-to-all-start = ((f32[16,2,128]{2,1,0:T(2,128)}), f32[16,2,128]{2,1,0:T(2,128)S(1)}, u32[]{:S(2)}, u32[]{:S(2)}) async-start(f32[16,2,128]{2,1,0:T(2,128)} %get-tuple-element.34), calls=%async_computation | async-start | bytes 32768 | tf_op jit(solution)/shard_map/all_to_all | solution.py:615
  12.6 15.0 %copy-start.4 = (s32[416,4]{0,1:T(4,128)S(1)}, s32[416,4]{0,1:T(4,128)}, u32[]{:S(2)}) copy-start(s32[416,4]{0,1:T(4,128)} %param.19) | copy-start | bytes 19972
  12.6 15.0 %copy-start.5 = (s32[416,4]{0,1:T(4,128)S(1)}, s32[416,4]{0,1:T(4,128)}, u32[]{:S(2)}) copy-start(s32[416,4]{0,1:T(4,128)} %param.20) | copy-start | bytes 19972
  12.7 15.1 %copy-start.3 = (f32[416,4]{0,1:T(4,128)S(1)}, f32[416,4]{0,1:T(4,128)}, u32[]{:S(2)}) copy-start(f32[416,4]{0,1:T(4,128)} %param.21) | copy-start | bytes 19972
  19.9 21.0 %all-to-all-start.1 = ((bf16[8,320,128]{2,1,0:T(8,128)(2,1)}), bf16[8,320,128]{2,1,0:T(8,128)(2,1)S(1)}, u32[]{:S(2)}, u32[]{:S(2)}) async-start(bf16[8,320,128]{2,1,0:T(8,128)(2,1)} %get-tuple-element.35), calls=%async_computation.1 | async-start | bytes 1310720 | tf_op jit(solution)/shard_map/all_to_all | solution.py:651
  31.4 1.1 %copy-start.2 = (bf16[1344,448]{1,0:T(8,128)(2,1)}, bf16[1344,448]{1,0:T(8,128)(2,1)S(1)}, u32[]{:S(2)}) copy-start(bf16[1344,448]{1,0:T(8,128)(2,1)S(1)} %get-tuple-element.39.mats_hbm) | copy-start | bytes 3612676
  42.2 2.9 %collective-permute-start.2 = (f32[64,128]{1,0:T(8,128)S(1)}, f32[64,128]{1,0:T(8,128)S(1)}, u32[]{:S(2)}, u32[]{:S(2)}) collective-permute-start(f32[64,128]{1,0:T(8,128)S(1)} %get-tuple-element.43.own_ref), channel_id=1, source_target_pairs={{0,8},{8,0},{16,24},{24,16},{32,40},{40,32},{48,56},{56,48},{64,72... | collective-permute-start | bytes 98312 | tf_op jit(solution)/shard_map/ppermute | solution.py:674
  42.2 8.4 %collective-permute-start.3 = (f32[64,128]{1,0:T(8,128)S(1)}, f32[64,128]{1,0:T(8,128)S(1)}, u32[]{:S(2)}, u32[]{:S(2)}) collective-permute-start(f32[64,128]{1,0:T(8,128)S(1)} %get-tuple-element.44), channel_id=1, source_target_pairs={{8,16},{16,8},{24,32},{32,24},{40,48},{48,40},{56,64},{64,56},{72,... | collective-permute-start | bytes 98312 | tf_op jit(solution)/shard_map/ppermute | solution.py:675
  45.1 5.5 %collective-permute-start.4 = (f32[8,128]{1,0:T(8,128)S(1)}, f32[8,128]{1,0:T(8,128)S(1)}, u32[]{:S(2)}, u32[]{:S(2)}) collective-permute-start(f32[8,128]{1,0:T(8,128)S(1)} %slice_add_fusion), channel_id=1, source_target_pairs={{16,0},{32,48},{64,80},{96,112},{17,1},{33,49},{65,81},{97,113},{1... | collective-permute-start | bytes 12296 | tf_op jit(solution)/shard_map/ppermute | solution.py:679
  55.8 17.1 %all-to-all-start.2 = ((f32[8,176,128]{2,1,0:T(8,128)}), f32[8,176,128]{2,1,0:T(8,128)S(1)}, u32[]{:S(2)}, u32[]{:S(2)}) async-start(f32[8,176,128]{2,1,0:T(8,128)} %second.1), calls=%async_computation.2 | async-start | bytes 1441792 | tf_op jit(solution)/shard_map/all_to_all | solution.py:706
  59.4 3.4 %collective-permute-start.7 = (f32[8,128]{1,0:T(8,128)S(1)}, f32[8,128]{1,0:T(8,128)S(1)}, u32[]{:S(2)}, u32[]{:S(2)}) collective-permute-start(f32[8,128]{1,0:T(8,128)S(1)} %add.32), channel_id=1, source_target_pairs={{112,0},{113,1},{114,2},{115,3},{116,4},{117,5},{118,6},{119,7}} | collective-permute-start | bytes 12296 | tf_op jit(solution)/shard_map/ppermute | solution.py:707
  60.1 3.4 %collective-permute-start.5 = (f32[8,128]{1,0:T(8,128)S(1)}, f32[8,128]{1,0:T(8,128)S(1)}, u32[]{:S(2)}, u32[]{:S(2)}) collective-permute-start(f32[8,128]{1,0:T(8,128)S(1)} %add.32), channel_id=1, source_target_pairs={{48,0},{49,1},{50,2},{51,3},{52,4},{53,5},{54,6},{55,7}} | collective-permute-start | bytes 12296 | tf_op jit(solution)/shard_map/ppermute | solution.py:707
  62.2 1.3 %collective-permute-start.6 = (f32[8,128]{1,0:T(8,128)S(1)}, f32[8,128]{1,0:T(8,128)S(1)}, u32[]{:S(2)}, u32[]{:S(2)}) collective-permute-start(f32[8,128]{1,0:T(8,128)S(1)} %add.32), channel_id=1, source_target_pairs={{80,0},{81,1},{82,2},{83,3},{84,4},{85,5},{86,6},{87,7}} | collective-permute-start | bytes 12296 | tf_op jit(solution)/shard_map/ppermute | solution.py:707

commit v6 on v5

--- a/solution.py
+++ b/solution.py
@@ -433,7 +433,8 @@
     copy.wait()
 
 
-def plain_part(regs, reg, w_ref, side_ref, plain_ref):
+def plain_kernel(regs, idx_ref, w_ref, side_ref, plain_ref):
+    reg = idx_ref[0]
     chan, count = plain_ref.shape[1], plain_ref.shape[2]
     side = side_ref[...][:chan]
     symmetry, energy = side[:, 2:3], side[:, 3:4]
@@ -531,9 +532,17 @@
             outer_ref[pl.ds(2 * piece + part, chan, stride=sources), :] = cells
 
 
-def aside_kernel(regs, idx_ref, table_ref, w_ref, side_ref, mats_ref, plain_ref):
-    plain_part(regs, idx_ref[0], w_ref, side_ref, plain_ref)
-    build_mats(table_ref, mats_ref)
+def mats_kernel(table_ref, after_ref, mats_hbm, mats_ref, sems):
+    del after_ref
+    rows = mats_ref.shape[0] // NLAM
+    copies = []
+    for first, last in build_mats(table_ref, mats_ref):
+        for level in range(NLAM):
+            span = pl.ds(level * rows + first, last - first)
+            copies.append(pltpu.make_async_copy(mats_ref.at[span], mats_hbm.at[span], sems.at[len(copies)]))
+            copies[-1].start()
+    for copy in copies:
+        copy.wait()
 
 
 def build_mats(table_ref, mats_ref):
@@ -555,6 +564,7 @@
         for level in range(NLAM):
             at = level * rows + first
             mats_ref[at : at + count, :] = sums[level][:, :rows].astype(jnp.bfloat16)
+        yield first, first + count
 
 
 def coupling_table(source, order_list, weight, groups, chan, padded):
@@ -652,14 +662,16 @@
 
     table = coupling_table(couple_source, couple_order, couple_weight, groups, chan, padded)
     mats_shape = (NLAM * groups * padded, groups * padded)
-    mats, plain = pl.pallas_call(
-        functools.partial(aside_kernel, regs),
-        out_shape=(jax.ShapeDtypeStruct(mats_shape, jnp.bfloat16), shape_of(2, chan, count)),
-        in_specs=[smem] + [vmem] * 3,
-        out_specs=(vmem,) * 2,
+    copies = NLAM * -(-mats_shape[1] // LANES)
+    mats = pl.pallas_call(
+        mats_kernel,
+        out_shape=pltpu.HBM(mats_shape, jnp.bfloat16),
+        in_specs=[vmem, hbm],
+        out_specs=hbm,
+        scratch_shapes=[pltpu.VMEM(mats_shape, jnp.bfloat16), pltpu.SemaphoreType.DMA((copies,))],
         compiler_params=params(8),
-        name="aside",
-    )(ints, table, cells, side)
+        name="mats",
+    )(table, side)
     received, mats = lax.optimization_barrier((received, mats))
 
     first, pair, other = pl.pallas_call(
@@ -702,8 +714,16 @@
         compiler_params=params(16),
         name="second",
     )(ints, near_blocks, far(blocks), first, from_pair, from_other, pair, surface, side, start, cross)
-    message, ends = lax.optimization_barrier((message, ends))
+    message, ends, side = lax.optimization_barrier((message, ends, side))
     received = lax.all_to_all(message, "ch", 0, 0)
+    plain = pl.pallas_call(
+        functools.partial(plain_kernel, regs),
+        out_shape=shape_of(2, chan, count),
+        in_specs=[smem] + [vmem] * 2,
+        out_specs=vmem,
+        compiler_params=params(8),
+        name="plain",
+    )(ints, cells, side)
     ends = ends + sum(lax.ppermute(ends, "reg", move) for move in moves[1:])
 
     inner, outer = pl.pallas_call(

time: 75.7 us -> 75.4 us (level)
  local copies, waits for them, and re-layouts: 1.38 us -> 0.28 us
  Pallas kernels: 25.3 us -> 26.3 us
    unnamed x12 -> x10, local copies, waits for them, and re-layouts: 1.13 us -> 0.03 us
    pallas_call x1 -> x2, Pallas kernels: 3.42 us -> 4.44 us  [the longest x1 3.22 us: local(): pl.pallas_call(mats_kernel, out_shape=pltpu.HBM(mats_shape, jnp.bfloat16)...]
  transfers between devices with their start and end apart: 11 -> 11, of which waited for: 4 -> 3; matrix products, arithmetic and copies ran while one was open for 0% -> 0% of each run, Pallas kernels for 16% -> 17%
where the time goes in v6:
time: 75.4 us; the launch traced here: 74.4 us
  starting transfers between devices  27.5 us (36%)
  Pallas kernels  26.3 us (35%)
  waiting for transfers between devices  19.2 us (25%)
  between operations  0.9 us (1%)
    all_to_all x2, waiting for transfers between devices, local(): received = lax.all_to_all(message, 'ch', 0, 0)  18.5 us
    all_to_all x2, starting transfers between devices, local(): received = lax.all_to_all(message, 'ch', 0, 0)  11.2 us
    all_to_all x1, starting transfers between devices, local(): firsts = lax.all_to_all(first_msg, 'reg', 0, 0)  5.82 us
    ppermute x2, starting transfers between devices, local(): from_other = lax.ppermute(other, 'reg', off_chip)  5.71 us
    pallas_call x1, Pallas kernels, local(): pl.pallas_call(second_kernel, out_shape=shape_of(groups, lines + padded,...  5.23 us
    pallas_call x1, Pallas kernels, local(): pl.pallas_call(dipole_kernel, out_shape=shape_of(lines, LANES), in_specs=...  5.03 us
    pallas_call x1, Pallas kernels, local(): pl.pallas_call(functools.partial(outer_kernel, count), out_shape=(shape_o...  3.54 us
    ppermute x3, starting transfers between devices, local(): ends = ends + sum((lax.ppermute(ends, 'reg', move) for move in moves[1:]))  3.41 us
  transfers between devices with their start and end apart: 11, of which 3 were waited for; matrix products, arithmetic and copies ran while one was open for 0% of the time, Pallas kernels for 17%

profile of v6, /device:TPU:6, one launch (start us, length us, event | category | flops | bytes accessed | tf_op | source)
XLA Modules:
  0.0 74.4 jit_solution(2056548964890644458)
XLA Ops:
  0.6 0.1 pad_add_fusion.idx_ref
  0.7 0.0 copy-start
  0.7 0.0 copy-start.1
  0.7 3.1 %start.1 = (f32[16,2,128]{2,1,0:T(2,128)}, f32[64,128]{1,0:T(8,128)S(1)}, f32[64,128]{1,0:T(8,128)S(1)}, f32[120,128]{1,0:T(8,128)S(1)}, f32[56,128]{1,0:T(8,128...) custom-call(s32[2]{0:T(128)S(1)} %pad_add_fusion.idx_ref, s32[2,8]{1,0:T(2,128)} %bitcast.26, ...), custom_call_target="tpu_custom_call" | custom-call | tf_op jit(solution)/shard_map/start/pallas_call | solution.py:604
  3.9 0.1 collective-permute-start
  4.0 2.8 %collective-permute-start.1 = (f32[64,128]{1,0:T(8,128)S(1)}, f32[64,128]{1,0:T(8,128)S(1)}, u32[]{:S(2)}, u32[]{:S(2)}) collective-permute-start(f32[64,128]{1,0:T(8,128)S(1)} %get-tuple-element.30), channel_id=1, source_target_pairs={{8,16},{16,8},{24,32},{32,24},{40,48},{48,40},{56,64},{64,56},{72,... | collective-permute-start | bytes 98312 | tf_op jit(solution)/shard_map/ppermute | solution.py:629
  6.8 5.8 %all-to-all-start = ((f32[16,2,128]{2,1,0:T(2,128)}), f32[16,2,128]{2,1,0:T(2,128)S(1)}, u32[]{:S(2)}, u32[]{:S(2)}) async-start(f32[16,2,128]{2,1,0:T(2,128)} %get-tuple-element.33), calls=%async_computation | async-start | bytes 32768 | tf_op jit(solution)/shard_map/all_to_all | solution.py:625
  12.6 0.0 collective-permute-done.pair_ref
  12.6 0.0 collective-permute-done.1.next_ref
  12.6 0.0 copy-start.3
  12.6 0.0 copy-start.4
  12.7 0.0 copy-start.2
  12.7 5.0 %dipole.1.dipole_ref = f32[120,128]{1,0:T(8,128)S(1)} custom-call(s32[18]{0:T(128)S(1)} %get-tuple-element.27.ints_ref.idx_ref, f32[8,512,512]{2,1,0:T(8,128)} %blocks_hbm.5, f32[120,128]{1,0:T(8,128)S(1)} %get-tuple-element.28.mine_ref.u_ref, f32[64,128]{1,0:T(8,128)S(1)} %collective-permute-done.pair_ref, f32[64,128]{1,0:T(8,128)S(1)} %collective-permute-done.1.next_ref), custom_call_target="tpu_custom_call" | custom-call | tf_op jit(solution)/shard_map/dipole/pallas_call | solution.py:635
  17.7 0.0 all-to-all-done.first_ref
  17.7 0.0 copy-done
  17.7 0.0 copy-done.1
  17.7 2.2 %pack.1 = (bf16[8,320,128]{2,1,0:T(8,128)(2,1)}, f32[56,128]{1,0:T(8,128)S(1)}) custom-call(s32[18]{0:T(128)S(1)} %get-tuple-element.27.ints_ref.idx_ref, f32[120,128]{1,0:T(8,128)S(1)} %dipole.1.dipole_ref, f32[52,7680]{1,0:T(8,128)S(1)} %copy-done, f32[56,128]{1,0:T(8,128)S(1)} %get-tuple-element.31.cols_ref, f32[40,128]{1,0:T(8,128)S(1)} %get-tuple-element.32.edge_ref, ...), custom_call_target="tpu_custom_call" | custom-call | tf_op jit(solution)/shard_map/pack/pallas_call | solution.py:645
  19.9 7.7 %all-to-all-start.1 = ((bf16[8,320,128]{2,1,0:T(8,128)(2,1)}), bf16[8,320,128]{2,1,0:T(8,128)(2,1)S(1)}, u32[]{:S(2)}, u32[]{:S(2)}) async-start(bf16[8,320,128]{2,1,0:T(8,128)(2,1)} %get-tuple-element.34), calls=%async_computation.1 | async-start | bytes 1310720 | tf_op jit(solution)/shard_map/all_to_all | solution.py:661
  27.6 0.1 pad.13.clone
  27.7 0.0 copy-done.3
  27.7 0.0 copy-done.4
  27.7 0.0 copy-done.2
  27.7 0.1 maximum_maximum_fusion
  27.8 0.1 reshape.36
  27.9 0.1 reshape.37
  28.0 3.2 %mats.1.mats_hbm = bf16[1344,448]{1,0:T(8,128)(2,1)} custom-call(f32[16,512]{1,0:T(8,128)S(1)} %pad.9.table_ref, f32[56,128]{1,0:T(8,128)S(1)} %get-tuple-element.48.after_ref.side_ref), custom_call_target="tpu_custom_call" | custom-call | tf_op jit(solution)/shard_map/mats/pallas_call | solution.py:666
  31.2 9.7 %all-to-all-done.1.received_ref = bf16[8,320,128]{2,1,0:T(8,128)(2,1)S(1)} async-done(((bf16[8,320,128]{2,1,0:T(8,128)(2,1)}), bf16[8,320,128]{2,1,0:T(8,128)(2,1)S(1)}, u32[]{:S(2)}, u32[]{:S(2)}) %all-to-all-start.1) | async-done | bytes 655392 | tf_op jit(solution)/shard_map/all_to_all | solution.py:661
  40.9 1.3 %update.1 = (f32[120,128]{1,0:T(8,128)S(1)}, f32[64,128]{1,0:T(8,128)S(1)}, f32[64,128]{1,0:T(8,128)S(1)}) custom-call(s32[18]{0:T(128)S(1)} %get-tuple-element.27.ints_ref.idx_ref, bf16[8,320,128]{2,1,0:T(8,128)(2,1)S(1)} %all-to-all-done.1.received_ref, f32[120,128]{1,0:T(8,128)S(1)} %get-tuple-element.28.mine_ref.u_ref, ...), custom_call_target="tpu_custom_call" | custom-call | tf_op jit(solution)/shard_map/update/pallas_call | solution.py:677
  42.2 0.0 collective-permute-start.2
  42.2 2.9 %collective-permute-start.3 = (f32[64,128]{1,0:T(8,128)S(1)}, f32[64,128]{1,0:T(8,128)S(1)}, u32[]{:S(2)}, u32[]{:S(2)}) collective-permute-start(f32[64,128]{1,0:T(8,128)S(1)} %get-tuple-element.42), channel_id=1, source_target_pairs={{8,16},{16,8},{24,32},{32,24},{40,48},{48,40},{56,64},{64,56},{72,... | collective-permute-start | bytes 98312 | tf_op jit(solution)/shard_map/ppermute | solution.py:687
  45.1 0.0 collective-permute-done.2.pair_ref
  45.1 1.3 %collective-permute-start.4 = (f32[8,128]{1,0:T(8,128)S(1)}, f32[8,128]{1,0:T(8,128)S(1)}, u32[]{:S(2)}, u32[]{:S(2)}) collective-permute-start(f32[8,128]{1,0:T(8,128)S(1)} %slice_add_fusion), channel_id=1, source_target_pairs={{16,0},{32,48},{64,80},{96,112},{17,1},{33,49},{65,81},{97,113},{1... | collective-permute-start | bytes 12296 | tf_op jit(solution)/shard_map/ppermute | solution.py:691
  46.4 3.5 %outer.1 = (f32[8,56,128]{2,1,0:T(8,128)S(1)}, f32[56,128]{1,0:T(8,128)S(1)}, f32[5,512,512]{2,1,0:T(8,128)S(1)}) custom-call(s32[18]{0:T(128)S(1)} %get-tuple-element.27.ints_ref.idx_ref, bf16[8,320,128]{2,1,0:T(8,128)(2,1)S(1)} %all-to-all-done.1.received_ref, bf16[1344,448]{1,0:T(8,128)(2,1)} %mats.1.mats_hbm, f32[8,512,512]{2,1,0:T(8,128)} %blocks_hbm.5), custom_call_target="tpu_custom_call" | custom-call | tf_op jit(solution)/shard_map/outer/pallas_call | solution.py:692
  50.0 0.7 collective-permute-done.4
  50.6 0.0 collective-permute-done.3.next_ref
  50.6 5.2 %second.1 = f32[8,176,128]{2,1,0:T(8,128)} custom-call(s32[18]{0:T(128)S(1)} %get-tuple-element.27.ints_ref.idx_ref, f32[5,512,512]{2,1,0:T(8,128)S(1)} %get-tuple-element.38.near_ref, f32[8,512,512]{2,1,0:T(8,128)} %blocks_hbm.5, f32[120,128]{1,0:T(8,128)S(1)} %get-tuple-element.40.mine_ref.first_ref, f32[64,128]{1,0:T(8,128)S(1)} %collective-permute-done.2.pair_ref, ...), custom_call_target="tpu_custom_call" | custom-call | tf_op jit(solution)/shard_map/second/pallas_call | solution.py:705
  55.9 3.6 %all-to-all-start.2 = ((f32[8,176,128]{2,1,0:T(8,128)}), f32[8,176,128]{2,1,0:T(8,128)S(1)}, u32[]{:S(2)}, u32[]{:S(2)}) async-start(f32[8,176,128]{2,1,0:T(8,128)} %second.1), calls=%async_computation.2 | async-start | bytes 1441792 | tf_op jit(solution)/shard_map/all_to_all | solution.py:718
  59.5 0.7 collective-permute-start.7
  60.1 2.1 %collective-permute-start.5 = (f32[8,128]{1,0:T(8,128)S(1)}, f32[8,128]{1,0:T(8,128)S(1)}, u32[]{:S(2)}, u32[]{:S(2)}) collective-permute-start(f32[8,128]{1,0:T(8,128)S(1)} %add.32), channel_id=1, source_target_pairs={{48,0},{49,1},{50,2},{51,3},{52,4},{53,5},{54,6},{55,7}} | collective-permute-start | bytes 12296 | tf_op jit(solution)/shard_map/ppermute | solution.py:727
  62.2 0.7 collective-permute-start.6
  62.9 1.2 %plain.1.plain_ref = f32[2,52,512]{2,1,0:T(8,128)S(1)} custom-call(s32[18]{0:T(128)S(1)} %get-tuple-element.27.ints_ref.idx_ref, f32[416,128]{1,0:T(8,128)S(1)} %bitcast.23, f32[56,128]{1,0:T(8,128)S(1)} %get-tuple-element.48.after_ref.side_ref), custom_call_target="tpu_custom_call" | custom-call | tf_op jit(solution)/shard_map/plain/pallas_call | solution.py:719
  64.1 0.0 collective-permute-done.7
  64.1 0.0 collective-permute-done.5
  64.1 0.0 collective-permute-done.6
  64.2 8.8 %all-to-all-done.2.received_ref = f32[8,176,128]{2,1,0:T(8,128)S(1)} async-done(((f32[8,176,128]{2,1,0:T(8,128)}), f32[8,176,128]{2,1,0:T(8,128)S(1)}, u32[]{:S(2)}, u32[]{:S(2)}) %all-to-all-start.2) | async-done | bytes 720928 | tf_op jit(solution)/shard_map/all_to_all | solution.py:718
  73.0 1.4 %finish.1 = (f32[2,7680]{1,0:T(2,128)}, f32[416,128]{1,0:T(8,128)}) custom-call(s32[18]{0:T(128)S(1)} %get-tuple-element.27.ints_ref.idx_ref, f32[8,176,128]{2,1,0:T(8,128)S(1)} %all-to-all-done.2.received_ref, f32[120,128]{1,0:T(8,128)S(1)} %get-tuple-element.28.mine_ref.u_ref, f32[120,128]{1,0:T(8,128)S(1)} %get-tuple-element.40.mine_ref.first_ref, ...), custom_call_target="tpu_custom_call" | custom-call | tf_op jit(solution)/shard_map/finish/pallas_call | solution.py:729
  (7 shorter events, 0.1 us)
Async XLA Ops:
  0.7 17.0 %copy-start = (f32[52,7680]{1,0:T(8,128)S(1)}, f32[52,7680]{1,0:T(8,128)}, u32[]{:S(2)}) copy-start(f32[52,7680]{1,0:T(8,128)} %surf_ref.5) | copy-start | bytes 4792324
  0.7 17.0 %copy-start.1 = (f32[2,52,512]{2,0,1:T(2,128)S(1)}, f32[2,52,512]{2,0,1:T(2,128)}, u32[]{:S(2)}) copy-start(f32[2,52,512]{2,0,1:T(2,128)} %param.17) | copy-start | bytes 638980
  3.9 8.7 %collective-permute-start = (f32[64,128]{1,0:T(8,128)S(1)}, f32[64,128]{1,0:T(8,128)S(1)}, u32[]{:S(2)}, u32[]{:S(2)}) collective-permute-start(f32[64,128]{1,0:T(8,128)S(1)} %get-tuple-element.29), channel_id=1, source_target_pairs={{0,8},{8,0},{16,24},{24,16},{32,40},{40,32},{48,56},{56,48},{64,72... | collective-permute-start | bytes 98312 | tf_op jit(solution)/shard_map/ppermute | solution.py:628
  4.0 8.7 %collective-permute-start.1 = (f32[64,128]{1,0:T(8,128)S(1)}, f32[64,128]{1,0:T(8,128)S(1)}, u32[]{:S(2)}, u32[]{:S(2)}) collective-permute-start(f32[64,128]{1,0:T(8,128)S(1)} %get-tuple-element.30), channel_id=1, source_target_pairs={{8,16},{16,8},{24,32},{32,24},{40,48},{48,40},{56,64},{64,56},{72,... | collective-permute-start | bytes 98312 | tf_op jit(solution)/shard_map/ppermute | solution.py:629
  6.8 10.9 %all-to-all-start = ((f32[16,2,128]{2,1,0:T(2,128)}), f32[16,2,128]{2,1,0:T(2,128)S(1)}, u32[]{:S(2)}, u32[]{:S(2)}) async-start(f32[16,2,128]{2,1,0:T(2,128)} %get-tuple-element.33), calls=%async_computation | async-start | bytes 32768 | tf_op jit(solution)/shard_map/all_to_all | solution.py:625
  12.6 15.0 %copy-start.3 = (s32[416,4]{0,1:T(4,128)S(1)}, s32[416,4]{0,1:T(4,128)}, u32[]{:S(2)}) copy-start(s32[416,4]{0,1:T(4,128)} %param.19) | copy-start | bytes 19972
  12.6 15.0 %copy-start.4 = (s32[416,4]{0,1:T(4,128)S(1)}, s32[416,4]{0,1:T(4,128)}, u32[]{:S(2)}) copy-start(s32[416,4]{0,1:T(4,128)} %param.20) | copy-start | bytes 19972
  12.7 15.1 %copy-start.2 = (f32[416,4]{0,1:T(4,128)S(1)}, f32[416,4]{0,1:T(4,128)}, u32[]{:S(2)}) copy-start(f32[416,4]{0,1:T(4,128)} %param.21) | copy-start | bytes 19972
  19.9 21.0 %all-to-all-start.1 = ((bf16[8,320,128]{2,1,0:T(8,128)(2,1)}), bf16[8,320,128]{2,1,0:T(8,128)(2,1)S(1)}, u32[]{:S(2)}, u32[]{:S(2)}) async-start(bf16[8,320,128]{2,1,0:T(8,128)(2,1)} %get-tuple-element.34), calls=%async_computation.1 | async-start | bytes 1310720 | tf_op jit(solution)/shard_map/all_to_all | solution.py:661
  42.2 2.9 %collective-permute-start.2 = (f32[64,128]{1,0:T(8,128)S(1)}, f32[64,128]{1,0:T(8,128)S(1)}, u32[]{:S(2)}, u32[]{:S(2)}) collective-permute-start(f32[64,128]{1,0:T(8,128)S(1)} %get-tuple-element.41.own_ref), channel_id=1, source_target_pairs={{0,8},{8,0},{16,24},{24,16},{32,40},{40,32},{48,56},{56,48},{64,72... | collective-permute-start | bytes 98312 | tf_op jit(solution)/shard_map/ppermute | solution.py:686
  42.2 8.4 %collective-permute-start.3 = (f32[64,128]{1,0:T(8,128)S(1)}, f32[64,128]{1,0:T(8,128)S(1)}, u32[]{:S(2)}, u32[]{:S(2)}) collective-permute-start(f32[64,128]{1,0:T(8,128)S(1)} %get-tuple-element.42), channel_id=1, source_target_pairs={{8,16},{16,8},{24,32},{32,24},{40,48},{48,40},{56,64},{64,56},{72,... | collective-permute-start | bytes 98312 | tf_op jit(solution)/shard_map/ppermute | solution.py:687
  45.1 5.5 %collective-permute-start.4 = (f32[8,128]{1,0:T(8,128)S(1)}, f32[8,128]{1,0:T(8,128)S(1)}, u32[]{:S(2)}, u32[]{:S(2)}) collective-permute-start(f32[8,128]{1,0:T(8,128)S(1)} %slice_add_fusion), channel_id=1, source_target_pairs={{16,0},{32,48},{64,80},{96,112},{17,1},{33,49},{65,81},{97,113},{1... | collective-permute-start | bytes 12296 | tf_op jit(solution)/shard_map/ppermute | solution.py:691
  55.9 17.1 %all-to-all-start.2 = ((f32[8,176,128]{2,1,0:T(8,128)}), f32[8,176,128]{2,1,0:T(8,128)S(1)}, u32[]{:S(2)}, u32[]{:S(2)}) async-start(f32[8,176,128]{2,1,0:T(8,128)} %second.1), calls=%async_computation.2 | async-start | bytes 1441792 | tf_op jit(solution)/shard_map/all_to_all | solution.py:718
  59.5 4.7 %collective-permute-start.7 = (f32[8,128]{1,0:T(8,128)S(1)}, f32[8,128]{1,0:T(8,128)S(1)}, u32[]{:S(2)}, u32[]{:S(2)}) collective-permute-start(f32[8,128]{1,0:T(8,128)S(1)} %add.32), channel_id=1, source_target_pairs={{112,0},{113,1},{114,2},{115,3},{116,4},{117,5},{118,6},{119,7}} | collective-permute-start | bytes 12296 | tf_op jit(solution)/shard_map/ppermute | solution.py:727
  60.1 4.0 %collective-permute-start.5 = (f32[8,128]{1,0:T(8,128)S(1)}, f32[8,128]{1,0:T(8,128)S(1)}, u32[]{:S(2)}, u32[]{:S(2)}) collective-permute-start(f32[8,128]{1,0:T(8,128)S(1)} %add.32), channel_id=1, source_target_pairs={{48,0},{49,1},{50,2},{51,3},{52,4},{53,5},{54,6},{55,7}} | collective-permute-start | bytes 12296 | tf_op jit(solution)/shard_map/ppermute | solution.py:727
  62.2 1.9 %collective-permute-start.6 = (f32[8,128]{1,0:T(8,128)S(1)}, f32[8,128]{1,0:T(8,128)S(1)}, u32[]{:S(2)}, u32[]{:S(2)}) collective-permute-start(f32[8,128]{1,0:T(8,128)S(1)} %add.32), channel_id=1, source_target_pairs={{80,0},{81,1},{82,2},{83,3},{84,4},{85,5},{86,6},{87,7}} | collective-permute-start | bytes 12296 | tf_op jit(solution)/shard_map/ppermute | solution.py:727
